TPU v7x, 32 devices: a whole 2x2x4 slice. The times are simulated.
32 devices in a mesh: row: 8 (over z, y), col: 4 (over x, core).
Axes of the slice: x: 2, y: 2, z: 4, core: 2. Of those that a mesh axis runs over, the one named last changes fastest.
Arguments:
- feats: bfloat16 [16384, 256], P(('row', 'col')), may hold values from -6 to 6
- w_msg: bfloat16 [256, 256], replicated, may hold values from -0.375 to 0.375
- w_self: bfloat16 [256, 256], replicated, may hold values from -0.375 to 0.375
- bias: float32 [256], replicated, may hold values from -3 to 3
- hit_mask: int32 [16384], P(('row', 'col')), may hold values 0 or 1
- block_cols: int32 [8, 4, 48], P('row', 'col'), may hold values from 0 to 31, as said below
- block_count: int32 [8, 4], P('row', 'col'), may hold values from 16 to 48, as said below
- edge_vals: bfloat16 [8, 4, 48, 128, 128], P('row', 'col'), may hold values from -0.1875 to 0.1875
- grad_out: bfloat16 [16384, 256], P(('row', 'col')), may hold values from -3 to 3
Outputs:
- hidden: bfloat16 [16384, 256], P(('row', 'col'))
- grad_feats: bfloat16 [16384, 256], P(('row', 'col'))
- edge_grad: bfloat16 [8, 4, 48, 128, 128], P('row', 'col')
- w_msg_grad: float32 [256, 256], replicated
- w_self_grad: float32 [256, 256], replicated
- bias_grad: float32 [256], replicated
Inputs may be any that keep to these rules, and one draw needn't show every extreme that they name: `block_cols`: slot s of a tile serves the tile's local block row s % 16; the block columns of the slots that serve one block row of one tile are different. Slots from block_count on are unused.
All inputs are finite; a program needn't handle non-finite values. No bound on the sum of `hit_mask` on one device may be relied on, other than what follows from the above.
Results may differ from a plain program's by a relative error of at most 0.015.
Values may be sent and summed in bfloat16 or wider, within the bound.
No kernel may reach another device: no remote copies, remote signals or barrier semaphores. Data moves between devices by JAX's collectives and lax.ppermute only.
A program may use at most 128 MiB of HBM per device.

v0:
```python
import math

import jax
import jax.numpy as jnp
from jax import lax
from jax.sharding import PartitionSpec as P


def activate(pre, row_mask, grad_in):
    sig = jax.nn.sigmoid(pre)
    hidden = (pre * sig * row_mask).astype(jnp.bfloat16)
    deriv = sig * (1.0 + pre * (1.0 - sig))
    grad_pre = (grad_in.astype(jnp.float32) * row_mask * deriv).astype(jnp.bfloat16)
    return (hidden, grad_pre)


def per_device(feats, w_msg, w_self, bias, hit_mask, block_cols, block_count, edge_vals, grad_out):
    row_count = lax.axis_size("row")
    col_count = lax.axis_size("col")
    own_rows = feats.shape[0]
    width = feats.shape[1]
    row_mask = hit_mask.astype(jnp.float32)[:, None]
    messages = (jnp.dot(feats, w_msg, preferred_element_type=jnp.float32) * row_mask).astype(
        jnp.bfloat16
    )
    column_msgs = lax.all_gather(messages, "row", axis=0, tiled=True)
    slot_cols = block_cols[0, 0]
    edge_block = edge_vals[0, 0]
    slot_total = edge_block.shape[0]
    edge_size = edge_block.shape[1]
    tile_rows = col_count * own_rows // edge_size
    tile_cols = row_count * own_rows // edge_size
    slot_depth = slot_total // tile_rows
    slot_flags = jnp.arange(slot_total, dtype=jnp.int32) < block_count[0, 0]
    edge_live = (edge_block * slot_flags.astype(jnp.bfloat16)[:, None, None]).reshape(
        slot_depth, tile_rows, edge_size, edge_size
    )
    col_blocks = column_msgs.reshape(tile_cols, edge_size, width)[slot_cols].reshape(
        slot_depth, tile_rows, edge_size, width
    )
    partial_value = jnp.einsum(
        "krij,krjf->rif", edge_live, col_blocks, preferred_element_type=jnp.float32
    ).reshape(tile_rows * edge_size, width)
    summed = lax.psum_scatter(
        partial_value.astype(jnp.bfloat16), "col", scatter_dimension=0, tiled=True
    ).astype(jnp.float32)
    pre = summed + jnp.dot(feats, w_self, preferred_element_type=jnp.float32) + bias
    hidden, grad_pre = activate(pre, row_mask, grad_out)
    grad_rows_all = lax.all_gather(grad_pre, "col", axis=0, tiled=True)
    grad_tile = grad_rows_all.reshape(tile_rows, edge_size, width)
    backward = jnp.einsum(
        "krij,rif->krjf", edge_live, grad_tile, preferred_element_type=jnp.float32
    ).reshape(slot_total, edge_size, width)
    back_part = jax.ops.segment_sum(backward, slot_cols, num_segments=tile_cols).reshape(
        tile_cols * edge_size, width
    )
    edge_grad = (
        jnp.einsum(
            "rif,krjf->krij", grad_tile, col_blocks, preferred_element_type=jnp.float32
        ).reshape(slot_total, edge_size, edge_size)
        * slot_flags.astype(jnp.float32)[:, None, None]
    ).astype(jnp.bfloat16)
    grad_sum = lax.psum_scatter(
        back_part.astype(jnp.bfloat16), "row", scatter_dimension=0, tiled=True
    ).astype(jnp.float32)
    grad_msg = (grad_sum * row_mask).astype(jnp.bfloat16)
    grad_feats = (
        jnp.einsum("hg,fg->hf", grad_msg, w_msg, preferred_element_type=jnp.float32)
        + jnp.einsum("hg,fg->hf", grad_pre, w_self, preferred_element_type=jnp.float32)
    ).astype(jnp.bfloat16)
    local_msg = jnp.einsum("hf,hg->fg", feats, grad_msg, preferred_element_type=jnp.float32)
    local_self = jnp.einsum("hf,hg->fg", feats, grad_pre, preferred_element_type=jnp.float32)
    local_bias = jnp.sum(grad_pre.astype(jnp.float32), axis=0)
    total_msg, total_self, total_bias = lax.psum(
        (local_msg, local_self, local_bias), ("row", "col")
    )
    factor = 1.0 / math.sqrt(own_rows * row_count * col_count)
    return (
        hidden,
        grad_feats,
        edge_grad[None, None],
        total_msg * factor,
        total_self * factor,
        total_bias * factor,
    )


def solution(mesh):
    placed = (
        P(("row", "col"), None),
        P(),
        P(),
        P(),
        P(("row", "col")),
        P("row", "col", None),
        P("row", "col"),
        P("row", "col", None, None, None),
        P(("row", "col"), None),
    )
    return jax.shard_map(
        per_device,
        mesh=mesh,
        in_specs=placed,
        out_specs=(
            P(("row", "col"), None),
            P(("row", "col"), None),
            P("row", "col", None, None, None),
            P(),
            P(),
            P(),
        ),
        check_vma=False,
    )
```

profile of v0, /device:TPU:0, one launch (start us, length us, event | category | flops | bytes accessed | tf_op | source)
XLA Modules:
  0.0 355.3 jit_solution(8910724853989069301)
XLA Ops:
  7.2 0.0 copy-start
  7.2 0.0 all-gather.3.cloned.1.call-start
  7.2 0.7 convert_element_type.67
  7.9 0.2 copy-done
  8.1 1.8 fusion.10
  10.0 0.0 all-gather.3.cloned.1.call-update
  10.0 0.0 reduce-scatter.3.cloned.1.call-start
  10.7 0.7 fusion.16
  11.4 51.4 %all-gather.3.cloned.1.call-done = bf16[4096,256]{1,0:T(8,128)(2,1)} async-done(((bf16[512,256]{1,0:T(8,128)(2,1)}), bf16[4096,256]{1,0:T(8,128)(2,1)}) %all-gather.3.cloned.1.call-update) | async-done | bytes 2097168 | tf_op jit(solution)/shard_map/all_gather | solution.py:26
  62.7 2.3 gather_fusion
  65.1 0.0 copy-start.2
  65.1 0.0 copy-start.4
  65.1 3.2 bitcast_convert_fusion
  68.3 0.0 reduce-scatter.3.cloned.1.call-update
  68.3 0.0 all-gather.5.cloned.1.call-start
  68.4 23.5 %reduce-scatter.3.cloned.1.call-done = bf16[512,256]{1,0:T(8,128)(2,1)} async-done(((bf16[2048,256]{1,0:T(8,128)(2,1)}), bf16[512,256]{1,0:T(8,128)(2,1)}) %reduce-scatter.3.cloned.1.call-update) | async-done | bytes 262160 | tf_op jit(solution)/shard_map/reduce_scatter | solution.py:44
  91.8 0.0 copy-done.2
  91.8 0.0 copy-done.4
  91.8 2.3 convert_reduce_fusion
  94.1 0.0 all-gather.5.cloned.1.call-update
  94.1 0.0 reduce-scatter.5.cloned.1.call-start
  94.2 16.8 %all-gather.5.cloned.1.call-done = bf16[2048,256]{1,0:T(8,128)(2,1)} async-done(((bf16[512,256]{1,0:T(8,128)(2,1)}), bf16[2048,256]{1,0:T(8,128)(2,1)}) %all-gather.5.cloned.1.call-update) | async-done | bytes 1048592 | tf_op jit(solution)/shard_map/all_gather | solution.py:49
  111.0 5.4 %convolution_bitcast_fusion = f32[3,16,128,256]{2,3,0,1:T(8,128)} fusion(bf16[16,128,256,1]{2,1,3,0:T(8,128)(2,1)} %bitcast.52, bf16[3,16,128,128]{3,2,1,0:T(8,128)(2,1)} %bitcast.55, bf16[3,16]{0,1:T(8,128)(2,1)S(1)} %fusion.15), kind=kOutput, calls=%fused_computation.7 | convolution fusion | flops 405798912 | bytes 8912992 | tf_op jit(solution)/shard_map/krij,rif->krjf/dot_general | solution.py:51
  116.4 6.5 %copy.22 = f32[3,16,128,256]{3,2,1,0:T(8,128)} copy(f32[3,16,128,256]{2,3,0,1:T(8,128)} %convolution_bitcast_fusion) | data formatting | bytes 12582912 | tf_op jit(solution)/shard_map/krij,rif->krjf/transpose | solution.py:51
  123.0 0.0 copy-start.3
  123.0 2.5 broadcast_in_dim.2
  125.5 0.0 copy-done.3
  125.5 14.7 %scatter_fusion = f32[32,128,256]{2,1,0:T(8,128)} fusion(f32[32,128,256]{2,1,0:T(8,128)} %broadcast_in_dim.2, s32[48]{0:T(128)S(1)} %bitcast.57, f32[48,128,256]{2,1,0:T(8,128)} %bitcast.46), kind=kCustom, calls=%fused_computation.1 | custom fusion | flops 1572864 | bytes 18874560 | tf_op jit(solution)/shard_map/scatter-add | solution.py:54
  140.2 3.8 %convert_element_type.75 = bf16[32,128,256]{2,1,0:T(8,128)(2,1)} convert(f32[32,128,256]{2,1,0:T(8,128)} %scatter_fusion) | non-fusion elementwise | flops 1048576 | bytes 6291456 | tf_op jit(solution)/shard_map/convert_element_type | solution.py:64
  144.0 0.0 reduce-scatter.5.cloned.1.call-update
  144.1 0.0 all-reduce.3.cloned.1.call-start
  144.1 40.0 %psum.23 = f32[256]{0:T(256)S(1)} all-reduce(f32[256]{0:T(256)S(1)} %get-tuple-element.20), channel_id=1, replica_groups=mesh['row'=8,'col'=4] {'row','col'}, use_global_device_ids=true, to_apply=%region_6.0 | all-reduce | flops 256 | bytes 2048 | tf_op jit(solution)/shard_map/psum | solution.py:74
  184.1 0.6 broadcast_multiply_fusion.2
  184.7 1.9 convolution_bitcast_fusion.1
  186.6 3.9 %fusion.4 = f32[3,16,128,128]{2,3,0,1:T(8,128)} fusion(bf16[16,128,256,1]{2,1,3,0:T(8,128)(2,1)} %bitcast.53, bf16[3,16,128,256]{3,2,1,0:T(8,128)(2,1)S(1)} %bitcast.48), kind=kOutput, calls=%fused_computation.9 | convolution fusion | flops 402653184 | bytes 7340032 | tf_op jit(solution)/shard_map/rif,krjf->krij/dot_general | solution.py:58
  190.5 2.4 copy.24
  192.9 0.0 copy-start.1
  192.9 1.5 multiply_convert_fusion
  194.3 17.7 %reduce-scatter.5.cloned.1.call-done = bf16[512,256]{1,0:T(8,128)(2,1)} async-done(((bf16[4096,256]{1,0:T(8,128)(2,1)}), bf16[512,256]{1,0:T(8,128)(2,1)}) %reduce-scatter.5.cloned.1.call-update) | async-done | bytes 262160 | tf_op jit(solution)/shard_map/reduce_scatter | solution.py:63
  212.1 2.0 convolution_bitcast_fusion.2
  214.1 0.0 all-reduce.3.cloned.1.call-update
  214.1 0.0 copy-done.1
  214.1 1.2 fusion.14
  215.4 2.0 fusion.11
  217.3 128.8 %all-reduce.3.cloned.1.call-done = (f32[256,256]{0,1:T(8,128)}, f32[256,256]{0,1:T(8,128)}) async-done(((f32[256,256]{0,1:T(8,128)}, f32[256,256]{0,1:T(8,128)}), (f32[256,256]{0,1:T(8,128)}, f32[256,256]{0,1:T(8,128)})) %all-reduce.3.cloned.1.call-update) | async-done | bytes 524304 | tf_op jit(solution)/shard_map/psum | solution.py:74
  346.1 1.1 broadcast_multiply_fusion
  347.1 0.8 copy.26
  348.0 0.8 copy.25
  (3 shorter events, 0.0 us)
Async XLA Ops:
  7.2 1.0 copy-start
  7.2 55.6 %all-gather.3.cloned.1.call-start = ((), (), s32[]{:S(2)}) async-start(), calls=%async_computation.2 | async-start | bytes 2359296 | tf_op jit(solution)/shard_map/all_gather | solution.py:26
  10.0 81.8 %reduce-scatter.3.cloned.1.call-start = ((), (), s32[]{:S(2)}) async-start(), calls=%async_computation.3 | async-start | bytes 1310720 | tf_op jit(solution)/shard_map/reduce_scatter | solution.py:44
  65.1 26.7 %copy-start.2 = (bf16[256,256]{1,0:T(8,128)(2,1)S(1)}, bf16[256,256]{1,0:T(8,128)(2,1)}, u32[]{:S(2)}) copy-start(bf16[256,256]{1,0:T(8,128)(2,1)} %param.11) | copy-start | bytes 393220
  65.1 26.7 %copy-start.4 = (f32[256]{0:T(256)S(1)}, f32[256]{0:T(256)}, u32[]{:S(2)}) copy-start(f32[256]{0:T(256)} %param.12) | copy-start | bytes 3076
  68.3 42.7 %all-gather.5.cloned.1.call-start = ((), (), s32[]{:S(2)}) async-start(), calls=%async_computation.4 | async-start | bytes 1310720 | tf_op jit(solution)/shard_map/all_gather | solution.py:49
  94.1 118.0 %reduce-scatter.5.cloned.1.call-start = ((), (), s32[]{:S(2)}) async-start(), calls=%async_computation.5 | async-start | bytes 2359296 | tf_op jit(solution)/shard_map/reduce_scatter | solution.py:63
  123.0 2.5 copy-start.3
  144.1 202.0 %all-reduce.3.cloned.1.call-start = ((), (), s32[]{:S(2)}) async-start(), calls=%async_computation.6 | async-start | bytes 1048576 | tf_op jit(solution)/shard_map/psum | solution.py:74
  192.9 21.3 %copy-start.1 = (bf16[256,256]{1,0:T(8,128)(2,1)S(1)}, bf16[256,256]{1,0:T(8,128)(2,1)}, u32[]{:S(2)}) copy-start(bf16[256,256]{1,0:T(8,128)(2,1)} %param.10) | copy-start | bytes 393220
Sparse Core Ops, SparseCore 0:
  10.7 51.9 all-gather.2
  68.4 23.3 reduce-scatter.2
  94.3 16.7 all-gather.4
  144.2 67.8 reduce-scatter.4
  218.9 127.1 all-reduce.2
where the time goes:
time: 356 us; the launch traced here: 355 us
  waiting for transfers between devices  238 us (67%)
  blocking collectives  40 us (11%)
  matrix products  23.7 us (7%)
  other arithmetic  23 us (6%)
  local copies, waits for them, and re-layouts  15.6 us (4%)
  between operations  14.5 us (4%)
    psum x1, waiting for transfers between devices, per_device(): lax.psum((local_msg, local_self, local_bias), ('row', 'col'))  129 us
    all_gather x1, waiting for transfers between devices, per_device(): column_msgs = lax.all_gather(messages, 'row', axis=0, tiled=True)  51.4 us
    psum x1, blocking collectives, per_device(): lax.psum((local_msg, local_self, local_bias), ('row', 'col'))  40 us
    reduce_scatter x1, waiting for transfers between devices, per_device(): lax.psum_scatter(partial_value.astype(jnp.bfloat16), 'col', scatter_dimen...  23.5 us
    reduce_scatter x1, waiting for transfers between devices, per_device(): lax.psum_scatter(back_part.astype(jnp.bfloat16), 'row', scatter_dimension...  17.7 us
    all_gather x1, waiting for transfers between devices, per_device(): grad_rows_all = lax.all_gather(grad_pre, 'col', axis=0, tiled=True)  16.8 us
    scatter-add x1, other arithmetic, per_device(): jax.ops.segment_sum(backward, slot_cols, num_segments=tile_cols)  14.7 us
  transfers between devices with their start and end apart: 5, of which 5 were waited for; matrix products, arithmetic and copies ran while one was open for 4% of the time, Pallas kernels for 0%

commit v1 on v0

v1 whole, which is shorter than its diff:
```python
import functools
import math

import jax
import jax.numpy as jnp
from jax import lax
from jax.experimental import pallas as pl
from jax.experimental.pallas import tpu as pltpu
from jax.sharding import PartitionSpec as P

BF16 = jnp.bfloat16
F32 = jnp.float32
VMEM = pl.BlockSpec(memory_space=pltpu.VMEM)
SMEM = pl.BlockSpec(memory_space=pltpu.SMEM)
ANY = pl.BlockSpec(memory_space=pl.ANY)


def exchange(value, axis, bit):
    size = lax.axis_size(axis)
    return lax.ppermute(value, axis, [(i, i ^ bit) for i in range(size)])


def bits_of(size):
    assert size & (size - 1) == 0
    return [1 << n for n in range(size.bit_length() - 1)]


def gather_by_offset(own, axis):
    held = {0: own}
    for bit in reversed(bits_of(lax.axis_size(axis))):
        for offset in list(held):
            held[offset | bit] = exchange(held[offset], axis, bit)
    return [held[k] for k in range(lax.axis_size(axis))]


def scatter_by_offset(parts, axis):
    parts = dict(enumerate(parts))
    last = []
    for bit in bits_of(lax.axis_size(axis)):
        for offset in sorted(parts, reverse=True):
            if offset & bit:
                got = exchange(parts.pop(offset), axis, bit)
                if offset ^ bit:
                    base = parts[offset ^ bit].astype(F32)
                    parts[offset ^ bit] = (base + got.astype(F32)).astype(BF16)
                else:
                    last.append(got)
    return [parts[0]] + last


def nbytes(shape, dtype):
    return math.prod(shape) * jnp.dtype(dtype).itemsize


def kernel_call(body, outs, in_specs, out_specs, scratch, flops, args):
    listed = jax.tree.leaves(outs)
    moved = sum(nbytes(a.shape, a.dtype) for a in (*args, *listed))
    return pl.pallas_call(
        body,
        out_shape=outs,
        in_specs=in_specs,
        out_specs=out_specs,
        scratch_shapes=scratch,
        compiler_params=pltpu.CompilerParams(vmem_limit_bytes=56 * 1024 * 1024),
        cost_estimate=pl.CostEstimate(flops=flops, bytes_accessed=moved, transcendentals=0),
    )(*args)


def tn(a, b):
    return lax.dot_general(a, b, (((0,), (0,)), ((), ())), preferred_element_type=F32)


def nt(a, b):
    return lax.dot_general(a, b, (((1,), (1,)), ((), ())), preferred_element_type=F32)


def load_all(refs, held, sems):
    rows = refs[0].shape[0]
    copies = [
        pltpu.make_async_copy(ref, held.at[pl.ds(k * rows, rows)], sems.at[k])
        for k, ref in enumerate(refs)
    ]
    for copy in copies:
        copy.start()
    return copies


def spmm_body(n_row, n_col, size, depth, cols, count, place, edges, *refs):
    held_refs, outs, (held, sems) = refs[:n_row], refs[n_row : n_row + n_col], refs[n_row + n_col :]
    own = outs[0].shape[0] // size
    tile_rows = n_col * own
    for copy in load_all(held_refs, held, sems):
        copy.wait()
    r, c, used = place[0], place[1], count[0]
    for offset in range(n_col):
        for i in range(own):
            row = (c ^ offset) * own + i
            total = None
            for k in range(depth):
                slot = k * tile_rows + row
                m = cols[slot]
                at = ((m // own) ^ r) * own + m % own
                block = edges[slot]
                block = jnp.where(slot < used, block, jnp.zeros_like(block))
                term = jnp.dot(
                    block,
                    held[pl.ds(pl.multiple_of(at * size, size), size), :],
                    preferred_element_type=F32,
                )
                total = term if total is None else total + term
            outs[offset][pl.ds(i * size, size), :] = total.astype(BF16)


def back_body(n_row, n_col, size, depth, cols, count, place, edges, *refs):
    grads, outs = refs[:n_col], refs[n_col : n_col + n_row]
    held, terms, total, sems = refs[n_col + n_row :]
    own = outs[0].shape[0] // size
    tile_rows = n_col * own
    for copy in load_all(grads, held, sems):
        copy.wait()
    r, c, used = place[0], place[1], count[0]
    total[...] = jnp.zeros_like(total)
    for row in range(tile_rows):
        at = ((row // own) ^ c) * own + row % own
        grad = held[pl.ds(pl.multiple_of(at * size, size), size), :]
        for k in range(depth):
            slot = k * tile_rows + row
            terms[slot] = tn(edges[slot], grad)
    for slot in range(depth * tile_rows):
        m = cols[slot]
        at = ((m // own) ^ r) * own + m % own
        spot = pl.ds(pl.multiple_of(at * size, size), size)

        @pl.when(slot < used)
        def _():
            total[spot, :] = total[spot, :] + terms[slot]

    rows = own * size
    for k in range(n_row):
        outs[k][...] = total[pl.ds(k * rows, rows), :].astype(BF16)


def edge_body(n_row, n_col, size, depth, cols, count, place, *refs):
    grads, feats = refs[:n_col], refs[n_col : n_col + n_row]
    out, held, held_feats, sems, feat_sems = refs[n_col + n_row :]
    own = grads[0].shape[0] // size
    tile_rows = n_col * own
    first, second = load_all(grads, held, sems), load_all(feats, held_feats, feat_sems)
    for copy in first + second:
        copy.wait()
    r, c, used = place[0], place[1], count[0]
    for row in range(tile_rows):
        at = ((row // own) ^ c) * own + row % own
        grad = held[pl.ds(pl.multiple_of(at * size, size), size), :]
        for k in range(depth):
            slot = k * tile_rows + row
            m = cols[slot]
            spot = ((m // own) ^ r) * own + m % own
            value = nt(grad, held_feats[pl.ds(pl.multiple_of(spot * size, size), size), :])
            out[slot] = jnp.where(slot < used, value, jnp.zeros_like(value)).astype(BF16)


def act_body(step, n_terms, *refs):
    terms = refs[:n_terms]
    feats, w_msg, w_self, bias, mask, grad_out, hidden, grad_pre, grad_w, summed = refs[n_terms:]
    for at in range(0, feats.shape[0], step):
        rows = pl.ds(at, step)
        total = terms[0][rows, :].astype(F32)
        for term in terms[1:]:
            total = total + term[rows, :].astype(F32)
        high = total.astype(BF16)
        low = (total - high.astype(F32)).astype(BF16)
        summed[rows, :] = high
        pre = jnp.dot(high, w_msg[...], preferred_element_type=F32)
        pre = pre + jnp.dot(low, w_msg[...], preferred_element_type=F32)
        pre = pre + jnp.dot(feats[rows, :], w_self[...], preferred_element_type=F32) + bias[...]
        live = mask[rows, :].astype(F32)
        sig = jax.nn.sigmoid(pre)
        hidden[rows, :] = (pre * sig * live).astype(BF16)
        deriv = sig * (1.0 + pre * (1.0 - sig))
        grad = (grad_out[rows, :].astype(F32) * live * deriv).astype(BF16)
        grad_pre[rows, :] = grad
        grad_w[rows, :] = nt(grad, w_msg[...]).astype(BF16)


def weight_body(n_col, factor, place, summed, feats, grad_pre, w_self, even, odd, own_part, stack):
    width = feats.shape[1]
    grad = grad_pre[...]
    own_part[...] = nt(grad, w_self[...])
    stack[pl.ds(0, width), :] = tn(summed[...], grad) * factor
    stack[pl.ds(width, width), :] = tn(feats[...], grad) * factor
    rest = stack.shape[0] - 2 * width
    total = jnp.sum(grad.astype(F32), axis=0, keepdims=True) * factor
    stack[pl.ds(2 * width, rest), :] = jnp.broadcast_to(total, (rest, width))
    c = place[1]
    piece = stack.shape[0] // n_col
    for k in range(n_col):
        spot = pl.ds(pl.multiple_of((c ^ k) * piece, 8), piece)
        (odd if k % 2 else even)[k // 2] = stack[spot, :]


def join_body(n_col, place, even, odd, w_msg, w_self, bias, stack):
    c = place[1]
    piece = stack.shape[0] // n_col
    width = w_msg.shape[0]
    for k in range(n_col):
        spot = pl.ds(pl.multiple_of((c ^ k) * piece, 8), piece)
        stack[spot, :] = (odd if k % 2 else even)[k // 2]
    w_msg[...] = stack[pl.ds(0, width), :]
    w_self[...] = stack[pl.ds(width, width), :]
    bias[...] = stack[pl.ds(2 * width, 1), :]


def per_device(feats, w_msg, w_self, bias, hit_mask, block_cols, block_count, edge_vals, grad_out):
    n_row, n_col = lax.axis_size("row"), lax.axis_size("col")
    own_rows, width = feats.shape
    edges = edge_vals[0, 0]
    slots, size = edges.shape[0], edges.shape[1]
    own = own_rows // size
    tile_rows = n_col * own
    depth = slots // tile_rows
    cols, count = block_cols[0, 0], block_count[0]
    place = jnp.stack([lax.axis_index("row"), lax.axis_index("col")]).astype(jnp.int32)
    mask = hit_mask[:, None]
    block = jax.ShapeDtypeStruct((own_rows, width), BF16)
    wide = jax.ShapeDtypeStruct((own_rows, width), F32)
    edge_flops = 2 * slots * size * size * width
    dims = (n_row, n_col, size, depth)
    sems = pltpu.SemaphoreType.DMA

    masked = jnp.where(mask != 0, feats, jnp.zeros_like(feats))
    held = gather_by_offset(masked, "row")

    partial = kernel_call(
        functools.partial(spmm_body, *dims),
        [block] * n_col,
        [SMEM] * 3 + [VMEM] + [ANY] * n_row,
        [VMEM] * n_col,
        [pltpu.VMEM((n_row * own_rows, width), BF16), sems((n_row,))],
        edge_flops,
        (cols, count, place, edges, *held),
    )
    terms = scatter_by_offset(partial, "col")

    hidden, grad_pre, grad_w, summed = kernel_call(
        functools.partial(act_body, size, len(terms)),
        [block] * 4,
        [VMEM] * (len(terms) + 6),
        [VMEM] * 4,
        [],
        10 * own_rows * width * width,
        (*terms, feats, w_msg, w_self, bias[None, :], mask, grad_out),
    )
    grads = gather_by_offset(grad_w, "col")

    pieces = kernel_call(
        functools.partial(back_body, *dims),
        [block] * n_row,
        [SMEM] * 3 + [VMEM] + [ANY] * n_col,
        [VMEM] * n_row,
        [
            pltpu.VMEM((n_col * own_rows, width), BF16),
            pltpu.VMEM((slots, size, width), F32),
            pltpu.VMEM((n_row * own_rows, width), F32),
            sems((n_col,)),
        ],
        edge_flops,
        (cols, count, place, edges, *grads),
    )

    rows = 2 * width + 8
    rows += -rows % (8 * n_col)
    half = jax.ShapeDtypeStruct((n_col // 2, rows // n_col, width), F32)
    factor = 1.0 / math.sqrt(own_rows * n_row * n_col)
    even, odd, own_part = kernel_call(
        functools.partial(weight_body, n_col, factor),
        [half, half, wide],
        [SMEM] + [VMEM] * 4,
        [VMEM] * 3,
        [pltpu.VMEM((rows, width), F32)],
        6 * own_rows * width * width,
        (place, summed, feats, grad_pre, w_self),
    )
    part = even + exchange(odd, "col", 1)
    for bit in bits_of(n_col)[1:]:
        part = jnp.stack([part[k] for k in range(0, part.shape[0], 2)]) + exchange(
            jnp.stack([part[k] for k in range(1, part.shape[0], 2)]), "col", bit
        )
    total = part[0]
    for bit in bits_of(n_row):
        total = total + exchange(total, "row", bit)
    found = total[None]
    for bit in reversed(bits_of(n_col)[1:]):
        other = exchange(found, "col", bit)
        found = jnp.stack([found, other], axis=1).reshape(-1, *total.shape)
    other = exchange(found, "col", 1)
    square = jax.ShapeDtypeStruct((width, width), F32)
    msg_grad, self_grad, bias_grad = kernel_call(
        functools.partial(join_body, n_col),
        [square, square, jax.ShapeDtypeStruct((1, width), F32)],
        [SMEM] + [VMEM] * 2,
        [VMEM] * 3,
        [pltpu.VMEM((rows, width), F32)],
        0,
        (place, found, other),
    )

    edge_grad = kernel_call(
        functools.partial(edge_body, *dims),
        jax.ShapeDtypeStruct((slots, size, size), BF16),
        [SMEM] * 3 + [ANY] * (n_col + n_row),
        VMEM,
        [
            pltpu.VMEM((n_col * own_rows, width), BF16),
            pltpu.VMEM((n_row * own_rows, width), BF16),
            sems((n_col,)),
            sems((n_row,)),
        ],
        edge_flops,
        (cols, count, place, *grads, *held),
    )

    back = scatter_by_offset(pieces, "row")
    summed_back = sum(term.astype(F32) for term in back)
    grad_feats = (jnp.where(mask != 0, summed_back, 0.0) + own_part).astype(BF16)
    return hidden, grad_feats, edge_grad[None, None], msg_grad, self_grad, bias_grad[0]


def solution(mesh):
    placed = (
        P(("row", "col"), None),
        P(),
        P(),
        P(),
        P(("row", "col")),
        P("row", "col", None),
        P("row", "col"),
        P("row", "col", None, None, None),
        P(("row", "col"), None),
    )
    return jax.shard_map(
        per_device,
        mesh=mesh,
        in_specs=placed,
        out_specs=(
            P(("row", "col"), None),
            P(("row", "col"), None),
            P("row", "col", None, None, None),
            P(),
            P(),
            P(),
        ),
        check_vma=False,
    )
```

time: 356 us -> 128 us (0.36)
  waiting for transfers between devices: 238 us -> 60.7 us
  blocking collectives: 40 us -> 0 us
  starting transfers between devices: 0.21 us -> 31.5 us
  matrix products: 23.7 us -> 0 us
  Pallas kernels: 0 us -> 23.5 us
  other arithmetic: 23 us -> 6.56 us
  between operations: 14.5 us -> 1.51 us
  local copies, waits for them, and re-layouts: 15.6 us -> 3.73 us
    psum x1 -> x0, waiting for transfers between devices: 129 us -> none  [per_device(): lax.psum((local_msg, local_self, local_bias), ('row', 'col'))]
    all_gather x2 -> x0, waiting for transfers between devices: 68.2 us -> none  [the longest x1 51.4 us: per_device(): column_msgs = lax.all_gather(messages, 'row', axis=0, tiled=True)]
    ppermute x0 -> x27, waiting for transfers between devices: none -> 60.7 us  [exchange(): return lax.ppermute(value, axis, [(i, i ^ bit) for i in range(size)])]
    reduce_scatter x2 -> x0, waiting for transfers between devices: 41.2 us -> none  [the longest x1 23.5 us: per_device(): lax.psum_scatter(partial_value.astype(jnp.bfloat16), 'col', scatter_dimen...]
    psum x1 -> x0, blocking collectives: 40 us -> none  [per_device(): lax.psum((local_msg, local_self, local_bias), ('row', 'col'))]
    ppermute x0 -> x27, starting transfers between devices: none -> 31.5 us  [exchange(): return lax.ppermute(value, axis, [(i, i ^ bit) for i in range(size)])]
    dot_general x9 -> x0, matrix products: 23.7 us -> none  [the longest x1 5.42 us: per_device(): jnp.einsum('krij,rif->krjf', edge_live, grad_tile, preferred_element_type...]
    pallas_call x0 -> x6, Pallas kernels: none -> 23.5 us  [kernel_call(): pl.pallas_call(body, out_shape=outs, in_specs=in_specs, out_specs=out_spe...]
  transfers between devices with their start and end apart: 5 -> 27, of which waited for: 5 -> 16; matrix products, arithmetic and copies ran while one was open for 4% -> 4% of each run, Pallas kernels for 0% -> 10%
where the time goes in v1:
time: 128 us; the launch traced here: 127 us
  waiting for transfers between devices  60.7 us (47%)
  starting transfers between devices  31.5 us (25%)
  Pallas kernels  23.5 us (18%)
  other arithmetic  6.56 us (5%)
  local copies, waits for them, and re-layouts  3.73 us (3%)
  between operations  1.51 us (1%)
    ppermute x27, waiting for transfers between devices, exchange(): return lax.ppermute(value, axis, [(i, i ^ bit) for i in range(size)])  60.7 us
    ppermute x27, starting transfers between devices, exchange(): return lax.ppermute(value, axis, [(i, i ^ bit) for i in range(size)])  31.5 us
    pallas_call x6, Pallas kernels, kernel_call(): pl.pallas_call(body, out_shape=outs, in_specs=in_specs, out_specs=out_spe...  23.5 us
    unnamed x42, local copies, waits for them, and re-layouts  2.86 us
  transfers between devices with their start and end apart: 27, of which 16 were waited for; matrix products, arithmetic and copies ran while one was open for 4% of the time, Pallas kernels for 10%

profile of v1, /device:TPU:0, one launch (start us, length us, event | category | flops | bytes accessed | tf_op | source)
XLA Modules:
  0.0 127.5 jit_solution(17588443726240218167)
XLA Ops:
  0.6 0.7 broadcast_compare_fusion
  1.3 1.1 broadcast_select_fusion.refs_0_.refs_4_
  2.4 0.0 copy-start
  2.4 4.1 %collective-permute-start.3 = (bf16[512,256]{1,0:T(8,128)(2,1)S(1)}, bf16[512,256]{1,0:T(8,128)(2,1)S(1)}, u32[]{:S(2)}, u32[]{:S(2)}) collective-permute-start(bf16[512,256]{1,0:T(8,128)(2,1)S(1)} %broadcast_select_fusion.refs_0_.refs_4_), channel_id=1, source_target_pairs={{0,16},{4,20},{8,24},{12,28},{16,0},{20,4},{24,8},{28,12},{1,17},{... | collective-permute-start | bytes 786440 | tf_op jit(solution)/shard_map/ppermute | solution.py:20
  6.5 1.6 %collective-permute-start.1 = (bf16[512,256]{1,0:T(8,128)(2,1)S(1)}, bf16[512,256]{1,0:T(8,128)(2,1)S(1)}, u32[]{:S(2)}, u32[]{:S(2)}) collective-permute-start(bf16[512,256]{1,0:T(8,128)(2,1)S(1)} %broadcast_select_fusion.refs_0_.refs_4_), channel_id=1, source_target_pairs={{0,8},{4,12},{8,0},{12,4},{16,24},{20,28},{24,16},{28,20},{1,9},{5... | collective-permute-start | bytes 786440 | tf_op jit(solution)/shard_map/ppermute | solution.py:20
  8.1 10.5 %collective-permute-done.3.refs_4_.refs_8_ = bf16[512,256]{1,0:T(8,128)(2,1)S(1)} collective-permute-done((bf16[512,256]{1,0:T(8,128)(2,1)S(1)}, bf16[512,256]{1,0:T(8,128)(2,1)S(1)}, u32[]{:S(2)}, u32[]{:S(2)}) %collective-permute-start.3) | collective-permute-done | bytes 262176 | tf_op jit(solution)/shard_map/ppermute | solution.py:20
  18.6 0.6 collective-permute-start.5
  19.2 1.5 %collective-permute-start = (bf16[512,256]{1,0:T(8,128)(2,1)S(1)}, bf16[512,256]{1,0:T(8,128)(2,1)S(1)}, u32[]{:S(2)}, u32[]{:S(2)}) collective-permute-start(bf16[512,256]{1,0:T(8,128)(2,1)S(1)} %broadcast_select_fusion.refs_0_.refs_4_), channel_id=1, source_target_pairs={{0,4},{4,0},{8,12},{12,8},{16,20},{20,16},{24,28},{28,24},{1,5},{5... | collective-permute-start | bytes 786440 | tf_op jit(solution)/shard_map/ppermute | solution.py:20
  20.7 0.5 collective-permute-start.4
  21.2 1.5 %collective-permute-start.2 = (bf16[512,256]{1,0:T(8,128)(2,1)S(1)}, bf16[512,256]{1,0:T(8,128)(2,1)S(1)}, u32[]{:S(2)}, u32[]{:S(2)}) collective-permute-start(bf16[512,256]{1,0:T(8,128)(2,1)S(1)} %collective-permute-done.1.refs_2_.refs_6_), channel_id=1, source_target_pairs={{0,4},{4,0},{8,12},{12,8},{16,20},{20,16},{24,28},{28,24},{1,5},{5... | collective-permute-start | bytes 786440 | tf_op jit(solution)/shard_map/ppermute | solution.py:20
  22.7 3.3 %collective-permute-done.5.refs_6_.refs_10_ = bf16[512,256]{1,0:T(8,128)(2,1)S(1)} collective-permute-done((bf16[512,256]{1,0:T(8,128)(2,1)S(1)}, bf16[512,256]{1,0:T(8,128)(2,1)S(1)}, u32[]{:S(2)}, u32[]{:S(2)}) %collective-permute-start.5) | collective-permute-done | bytes 262176 | tf_op jit(solution)/shard_map/ppermute | solution.py:20
  26.0 1.3 collective-permute-start.6
  27.9 0.6 pad_add_fusion.place
  28.5 0.0 collective-permute-done.refs_1_.refs_5_
  28.5 5.5 %collective-permute-done.4.refs_5_.refs_9_ = bf16[512,256]{1,0:T(8,128)(2,1)S(1)} collective-permute-done((bf16[512,256]{1,0:T(8,128)(2,1)S(1)}, bf16[512,256]{1,0:T(8,128)(2,1)S(1)}, u32[]{:S(2)}, u32[]{:S(2)}) %collective-permute-start.4) | collective-permute-done | bytes 262176 | tf_op jit(solution)/shard_map/ppermute | solution.py:20
  34.0 5.6 %collective-permute-done.2.refs_3_.refs_7_ = bf16[512,256]{1,0:T(8,128)(2,1)S(1)} collective-permute-done((bf16[512,256]{1,0:T(8,128)(2,1)S(1)}, bf16[512,256]{1,0:T(8,128)(2,1)S(1)}, u32[]{:S(2)}, u32[]{:S(2)}) %collective-permute-start.2) | collective-permute-done | bytes 262176 | tf_op jit(solution)/shard_map/ppermute | solution.py:20
  39.6 4.4 %collective-permute-done.6.refs_7_.refs_11_ = bf16[512,256]{1,0:T(8,128)(2,1)S(1)} collective-permute-done((bf16[512,256]{1,0:T(8,128)(2,1)S(1)}, bf16[512,256]{1,0:T(8,128)(2,1)S(1)}, u32[]{:S(2)}, u32[]{:S(2)}) %collective-permute-start.6) | collective-permute-done | bytes 262176 | tf_op jit(solution)/shard_map/ppermute | solution.py:20
  44.0 0.6 copy-done.8
  44.7 4.7 %shard_map.136 = (bf16[512,256]{1,0:T(8,128)(2,1)}, bf16[512,256]{1,0:T(8,128)(2,1)}, bf16[512,256]{1,0:T(8,128)(2,1)}, bf16[512,256]{1,0:T(8,128)(2,1)}) custom-call(s32[48]{0:T(128)} %bitcast.26, s32[1]{0:T(128)} %bitcast.18.count, s32[2]{0:T(128)} %pad_add_fusion.place, bf16[48,128,128]{2,1,0:T(8,128)(2,1)} %bitcast.21, bf16[512,256]{1,0:T(8,128)(2,1)} %copy-done, ...), custom_call_target="tpu_custom_call" | custom-call | flops 402653184 | bytes 4718796 | tf_op jit(solution)/shard_map/pallas_call | solution.py:58
  49.4 0.1 collective-permute-start.8
  49.4 0.5 collective-permute-start.7
  49.9 1.2 collective-permute-done.8
  51.2 1.0 add_convert_fusion.5
  52.2 1.6 %collective-permute-start.9 = (bf16[512,256]{1,0:T(8,128)(2,1)S(1)}, bf16[512,256]{1,0:T(8,128)(2,1)S(1)}, u32[]{:S(2)}, u32[]{:S(2)}) collective-permute-start(bf16[512,256]{1,0:T(8,128)(2,1)S(1)} %add_convert_fusion.5), channel_id=1, source_target_pairs={{0,2},{1,3},{2,0},{3,1},{4,6},{5,7},{6,4},{7,5},{8,10},{9,11},{10,... | collective-permute-start | bytes 786440 | tf_op jit(solution)/shard_map/ppermute | solution.py:20
  53.8 0.9 copy.15.refs_7_
  54.6 6.0 %collective-permute-done.9.refs_2_ = bf16[512,256]{1,0:T(8,128)(2,1)S(1)} collective-permute-done((bf16[512,256]{1,0:T(8,128)(2,1)S(1)}, bf16[512,256]{1,0:T(8,128)(2,1)S(1)}, u32[]{:S(2)}, u32[]{:S(2)}) %collective-permute-start.9) | collective-permute-done | bytes 262176 | tf_op jit(solution)/shard_map/ppermute | solution.py:20
  60.6 0.7 copy-done.17
  61.3 3.4 %shard_map.137 = (bf16[512,256]{1,0:T(8,128)(2,1)}, bf16[512,256]{1,0:T(8,128)(2,1)}, bf16[512,256]{1,0:T(8,128)(2,1)}, bf16[512,256]{1,0:T(8,128)(2,1)}) custom-call(bf16[512,256]{1,0:T(8,128)(2,1)} %get-tuple-element.28.refs_0_, bf16[512,256]{1,0:T(8,128)(2,1)} %copy-done.16, bf16[512,256]{1,0:T(8,128)(2,1)} %copy-done.17, bf16[512,256]{1,0:T(8,128)(2,1)} %feats.1, ...), custom_call_target="tpu_custom_call" | custom-call | flops 335544320 | bytes 2624512 | tf_op jit(solution)/shard_map/pallas_call | solution.py:58
  64.7 2.6 %shard_map.139 = (f32[2,136,256]{2,1,0:T(8,128)}, f32[2,136,256]{2,1,0:T(8,128)}, f32[512,256]{1,0:T(8,128)}) custom-call(s32[2]{0:T(128)} %pad_add_fusion.place, bf16[512,256]{1,0:T(8,128)(2,1)} %get-tuple-element.42.summed, bf16[512,256]{1,0:T(8,128)(2,1)} %feats.1, bf16[512,256]{1,0:T(8,128)(2,1)} %get-tuple-element.43.grad_pre, bf16[256,256]{1,0:T(8,128)(2,1)} %w_self.1), custom_call_target="tpu_custom_call" | custom-call | flops 201326592 | bytes 1998856 | tf_op jit(solution)/shard_map/pallas_call | solution.py:58
  67.2 1.5 %collective-permute-start.11 = (bf16[512,256]{1,0:T(8,128)(2,1)}, bf16[512,256]{1,0:T(8,128)(2,1)S(1)}, u32[]{:S(2)}, u32[]{:S(2)}) collective-permute-start(bf16[512,256]{1,0:T(8,128)(2,1)} %get-tuple-element.33.refs_0_), channel_id=1, source_target_pairs={{0,2},{1,3},{2,0},{3,1},{4,6},{5,7},{6,4},{7,5},{8,10},{9,11},{10,... | collective-permute-start | bytes 786440 | tf_op jit(solution)/shard_map/ppermute | solution.py:20
  68.7 0.3 collective-permute-done.20
  69.0 1.0 add.51
  70.0 1.6 %collective-permute-start.21 = (f32[1,136,256]{2,1,0:T(8,128)S(1)}, f32[1,136,256]{2,1,0:T(8,128)S(1)}, u32[]{:S(2)}, u32[]{:S(2)}) collective-permute-start(f32[1,136,256]{2,1,0:T(8,128)S(1)} %slice.9), channel_id=1, source_target_pairs={{0,2},{1,3},{2,0},{3,1},{4,6},{5,7},{6,4},{7,5},{8,10},{9,11},{10,... | collective-permute-start | bytes 417800 | tf_op jit(solution)/shard_map/ppermute | solution.py:20
  71.6 5.0 %collective-permute-done.11.refs_2_ = bf16[512,256]{1,0:T(8,128)(2,1)S(1)} collective-permute-done((bf16[512,256]{1,0:T(8,128)(2,1)}, bf16[512,256]{1,0:T(8,128)(2,1)S(1)}, u32[]{:S(2)}, u32[]{:S(2)}) %collective-permute-start.11) | collective-permute-done | bytes 262176 | tf_op jit(solution)/shard_map/ppermute | solution.py:20
  76.6 2.6 %collective-permute-done.21 = f32[1,136,256]{2,1,0:T(8,128)S(1)} collective-permute-done((f32[1,136,256]{2,1,0:T(8,128)S(1)}, f32[1,136,256]{2,1,0:T(8,128)S(1)}, u32[]{:S(2)}, u32[]{:S(2)}) %collective-permute-start.21) | collective-permute-done | bytes 139296 | tf_op jit(solution)/shard_map/ppermute | solution.py:20
  79.2 1.6 %collective-permute-start.22 = (f32[136,256]{1,0:T(8,128)S(1)}, f32[136,256]{1,0:T(8,128)S(1)}, u32[]{:S(2)}, u32[]{:S(2)}) collective-permute-start(f32[136,256]{1,0:T(8,128)S(1)} %fusion), channel_id=1, source_target_pairs={{0,4},{4,0},{8,12},{12,8},{16,20},{20,16},{24,28},{28,24},{1,5},{5... | collective-permute-start | bytes 417800 | tf_op jit(solution)/shard_map/ppermute | solution.py:20
  80.8 0.7 copy-done.11
  81.5 0.1 copy-done.12
  81.6 6.1 %shard_map.138 = (bf16[512,256]{1,0:T(8,128)(2,1)}, bf16[512,256]{1,0:T(8,128)(2,1)}, bf16[512,256]{1,0:T(8,128)(2,1)}, bf16[512,256]{1,0:T(8,128)(2,1)}, bf16[5...) custom-call(s32[48]{0:T(128)} %bitcast.27, ...), custom_call_target="tpu_custom_call" | custom-call | flops 402653184 | bytes 4718796 | tf_op jit(solution)/shard_map/pallas_call | solution.py:58
  87.7 0.0 copy-start.15
  87.7 0.4 collective-permute-start.17
  88.2 0.9 collective-permute-start.23
  89.0 1.2 collective-permute-start.13
  90.2 0.8 collective-permute-start.14
  91.1 1.2 collective-permute-start.16
  92.3 1.0 collective-permute-done.23
  93.3 3.6 %collective-permute-start.24 = (f32[136,256]{1,0:T(8,128)S(1)}, f32[136,256]{1,0:T(8,128)S(1)}, u32[]{:S(2)}, u32[]{:S(2)}) collective-permute-start(f32[136,256]{1,0:T(8,128)S(1)} %add.54), channel_id=1, source_target_pairs={{0,16},{4,20},{8,24},{12,28},{16,0},{20,4},{24,8},{28,12},{1,17},{... | collective-permute-start | bytes 417800 | tf_op jit(solution)/shard_map/ppermute | solution.py:20
  96.9 0.3 collective-permute-done.17
  97.2 1.0 add_convert_fusion.2
  98.2 0.5 collective-permute-start.18
  98.7 3.6 %collective-permute-done.24 = f32[136,256]{1,0:T(8,128)S(1)} collective-permute-done((f32[136,256]{1,0:T(8,128)S(1)}, f32[136,256]{1,0:T(8,128)S(1)}, u32[]{:S(2)}, u32[]{:S(2)}) %collective-permute-start.24) | collective-permute-done | bytes 139296 | tf_op jit(solution)/shard_map/ppermute | solution.py:20
  102.3 1.0 collective-permute-start.25
  103.3 5.1 %collective-permute-done.14 = bf16[512,256]{1,0:T(8,128)(2,1)S(1)} collective-permute-done((bf16[512,256]{1,0:T(8,128)(2,1)}, bf16[512,256]{1,0:T(8,128)(2,1)S(1)}, u32[]{:S(2)}, u32[]{:S(2)}) %collective-permute-start.14) | collective-permute-done | bytes 262176 | tf_op jit(solution)/shard_map/ppermute | solution.py:20
  108.4 0.1 add_convert_fusion.4
  108.5 0.5 collective-permute-start.15
  109.0 0.1 collective-permute-start.26
  109.1 3.5 %collective-permute-done.16 = bf16[512,256]{1,0:T(8,128)(2,1)S(1)} collective-permute-done((bf16[512,256]{1,0:T(8,128)(2,1)}, bf16[512,256]{1,0:T(8,128)(2,1)S(1)}, u32[]{:S(2)}, u32[]{:S(2)}) %collective-permute-start.16) | collective-permute-done | bytes 262176 | tf_op jit(solution)/shard_map/ppermute | solution.py:20
  112.6 0.1 add_convert_fusion.1
  112.7 3.4 %collective-permute-start.19 = (bf16[512,256]{1,0:T(8,128)(2,1)S(1)}, bf16[512,256]{1,0:T(8,128)(2,1)S(1)}, u32[]{:S(2)}, u32[]{:S(2)}) collective-permute-start(bf16[512,256]{1,0:T(8,128)(2,1)S(1)} %add_convert_fusion.1), channel_id=1, source_target_pairs={{0,16},{4,20},{8,24},{12,28},{16,0},{20,4},{24,8},{28,12},{1,17},{... | collective-permute-start | bytes 786440 | tf_op jit(solution)/shard_map/ppermute | solution.py:20
  116.1 4.9 %shard_map.140 = bf16[48,128,128]{2,1,0:T(8,128)(2,1)} custom-call(s32[48]{0:T(128)} %bitcast.28, s32[1]{0:T(128)} %bitcast.20.count, s32[2]{0:T(128)} %pad_add_fusion.place, bf16[512,256]{1,0:T(8,128)(2,1)} %get-tuple-element.33.refs_0_, bf16[512,256]{1,0:T(8,128)(2,1)} %copy-done.11, bf16[512,256]{1,0:T(8,128)(2,1)} %copy-done.10, ...), custom_call_target="tpu_custom_call" | custom-call | flops 402653184 | bytes 4718796 | tf_op jit(solution)/shard_map/pallas_call | solution.py:58
  121.0 0.7 copy-done.14
  121.6 1.9 %shard_map.141 = (f32[256,256]{1,0:T(8,128)}, f32[256,256]{1,0:T(8,128)}, f32[1,256]{1,0:T(1,128)}) custom-call(s32[2]{0:T(128)} %pad_add_fusion.place, f32[2,136,256]{2,1,0:T(8,128)} %copy-done.1, f32[2,136,256]{2,1,0:T(8,128)} %copy-done.14), custom_call_target="tpu_custom_call" | custom-call | bytes 1082376 | tf_op jit(solution)/shard_map/pallas_call | solution.py:58
  123.5 3.1 %collective-permute-done.19 = bf16[512,256]{1,0:T(8,128)(2,1)S(1)} collective-permute-done((bf16[512,256]{1,0:T(8,128)(2,1)S(1)}, bf16[512,256]{1,0:T(8,128)(2,1)S(1)}, u32[]{:S(2)}, u32[]{:S(2)}) %collective-permute-start.19) | collective-permute-done | bytes 262176 | tf_op jit(solution)/shard_map/ppermute | solution.py:20
  126.6 0.9 add_convert_fusion
  (54 shorter events, 0.2 us)
Async XLA Ops:
  2.4 41.6 %copy-start = (bf16[512,256]{1,0:T(8,128)(2,1)}, bf16[512,256]{1,0:T(8,128)(2,1)S(1)}, u32[]{:S(2)}) copy-start(bf16[512,256]{1,0:T(8,128)(2,1)S(1)} %broadcast_select_fusion.refs_0_.refs_4_) | copy-start | bytes 786436
  2.4 16.1 %collective-permute-start.3 = (bf16[512,256]{1,0:T(8,128)(2,1)S(1)}, bf16[512,256]{1,0:T(8,128)(2,1)S(1)}, u32[]{:S(2)}, u32[]{:S(2)}) collective-permute-start(bf16[512,256]{1,0:T(8,128)(2,1)S(1)} %broadcast_select_fusion.refs_0_.refs_4_), channel_id=1, source_target_pairs={{0,16},{4,20},{8,24},{12,28},{16,0},{20,4},{24,8},{28,12},{1,17},{... | collective-permute-start | bytes 786440 | tf_op jit(solution)/shard_map/ppermute | solution.py:20
  6.5 14.7 %collective-permute-start.1 = (bf16[512,256]{1,0:T(8,128)(2,1)S(1)}, bf16[512,256]{1,0:T(8,128)(2,1)S(1)}, u32[]{:S(2)}, u32[]{:S(2)}) collective-permute-start(bf16[512,256]{1,0:T(8,128)(2,1)S(1)} %broadcast_select_fusion.refs_0_.refs_4_), channel_id=1, source_target_pairs={{0,8},{4,12},{8,0},{12,4},{16,24},{20,28},{24,16},{28,20},{1,9},{5... | collective-permute-start | bytes 786440 | tf_op jit(solution)/shard_map/ppermute | solution.py:20
  18.6 25.4 %copy-start.2 = (bf16[512,256]{1,0:T(8,128)(2,1)}, bf16[512,256]{1,0:T(8,128)(2,1)S(1)}, u32[]{:S(2)}) copy-start(bf16[512,256]{1,0:T(8,128)(2,1)S(1)} %collective-permute-done.3.refs_4_.refs_8_) | copy-start | bytes 786436
  18.6 7.4 %collective-permute-start.5 = (bf16[512,256]{1,0:T(8,128)(2,1)S(1)}, bf16[512,256]{1,0:T(8,128)(2,1)S(1)}, u32[]{:S(2)}, u32[]{:S(2)}) collective-permute-start(bf16[512,256]{1,0:T(8,128)(2,1)S(1)} %collective-permute-done.3.refs_4_.refs_8_), channel_id=1, source_target_pairs={{0,8},{4,12},{8,0},{12,4},{16,24},{20,28},{24,16},{28,20},{1,9},{5... | collective-permute-start | bytes 786440 | tf_op jit(solution)/shard_map/ppermute | solution.py:20
  19.2 9.3 %collective-permute-start = (bf16[512,256]{1,0:T(8,128)(2,1)S(1)}, bf16[512,256]{1,0:T(8,128)(2,1)S(1)}, u32[]{:S(2)}, u32[]{:S(2)}) collective-permute-start(bf16[512,256]{1,0:T(8,128)(2,1)S(1)} %broadcast_select_fusion.refs_0_.refs_4_), channel_id=1, source_target_pairs={{0,4},{4,0},{8,12},{12,8},{16,20},{20,16},{24,28},{28,24},{1,5},{5... | collective-permute-start | bytes 786440 | tf_op jit(solution)/shard_map/ppermute | solution.py:20
  20.7 13.3 %collective-permute-start.4 = (bf16[512,256]{1,0:T(8,128)(2,1)S(1)}, bf16[512,256]{1,0:T(8,128)(2,1)S(1)}, u32[]{:S(2)}, u32[]{:S(2)}) collective-permute-start(bf16[512,256]{1,0:T(8,128)(2,1)S(1)} %collective-permute-done.3.refs_4_.refs_8_), channel_id=1, source_target_pairs={{0,4},{4,0},{8,12},{12,8},{16,20},{20,16},{24,28},{28,24},{1,5},{5... | collective-permute-start | bytes 786440 | tf_op jit(solution)/shard_map/ppermute | solution.py:20
  21.2 22.8 %copy-start.3 = (bf16[512,256]{1,0:T(8,128)(2,1)}, bf16[512,256]{1,0:T(8,128)(2,1)S(1)}, u32[]{:S(2)}) copy-start(bf16[512,256]{1,0:T(8,128)(2,1)S(1)} %collective-permute-done.1.refs_2_.refs_6_) | copy-start | bytes 786436
  21.2 18.4 %collective-permute-start.2 = (bf16[512,256]{1,0:T(8,128)(2,1)S(1)}, bf16[512,256]{1,0:T(8,128)(2,1)S(1)}, u32[]{:S(2)}, u32[]{:S(2)}) collective-permute-start(bf16[512,256]{1,0:T(8,128)(2,1)S(1)} %collective-permute-done.1.refs_2_.refs_6_), channel_id=1, source_target_pairs={{0,4},{4,0},{8,12},{12,8},{16,20},{20,16},{24,28},{28,24},{1,5},{5... | collective-permute-start | bytes 786440 | tf_op jit(solution)/shard_map/ppermute | solution.py:20
  26.0 18.0 %copy-start.4 = (bf16[512,256]{1,0:T(8,128)(2,1)}, bf16[512,256]{1,0:T(8,128)(2,1)S(1)}, u32[]{:S(2)}) copy-start(bf16[512,256]{1,0:T(8,128)(2,1)S(1)} %collective-permute-done.5.refs_6_.refs_10_) | copy-start | bytes 786436
  26.0 18.0 %collective-permute-start.6 = (bf16[512,256]{1,0:T(8,128)(2,1)S(1)}, bf16[512,256]{1,0:T(8,128)(2,1)S(1)}, u32[]{:S(2)}, u32[]{:S(2)}) collective-permute-start(bf16[512,256]{1,0:T(8,128)(2,1)S(1)} %collective-permute-done.5.refs_6_.refs_10_), channel_id=1, source_target_pairs={{0,4},{4,0},{8,12},{12,8},{16,20},{20,16},{24,28},{28,24},{1,5},{5... | collective-permute-start | bytes 786440 | tf_op jit(solution)/shard_map/ppermute | solution.py:20
  28.5 15.5 %copy-start.5 = (bf16[512,256]{1,0:T(8,128)(2,1)}, bf16[512,256]{1,0:T(8,128)(2,1)S(1)}, u32[]{:S(2)}) copy-start(bf16[512,256]{1,0:T(8,128)(2,1)S(1)} %collective-permute-done.refs_1_.refs_5_) | copy-start | bytes 786436
  34.0 10.0 %copy-start.6 = (bf16[512,256]{1,0:T(8,128)(2,1)}, bf16[512,256]{1,0:T(8,128)(2,1)S(1)}, u32[]{:S(2)}) copy-start(bf16[512,256]{1,0:T(8,128)(2,1)S(1)} %collective-permute-done.4.refs_5_.refs_9_) | copy-start | bytes 786436
  39.6 4.4 %copy-start.7 = (bf16[512,256]{1,0:T(8,128)(2,1)}, bf16[512,256]{1,0:T(8,128)(2,1)S(1)}, u32[]{:S(2)}) copy-start(bf16[512,256]{1,0:T(8,128)(2,1)S(1)} %collective-permute-done.2.refs_3_.refs_7_) | copy-start | bytes 786436
  44.0 0.7 copy-start.8
  44.7 9.1 %copy-start.20 = (s32[512]{0:T(512)S(1)}, s32[512]{0:T(512)}, u32[]{:S(2)}) copy-start(s32[512]{0:T(512)} %param.13) | copy-start | bytes 6148
  49.4 1.8 %collective-permute-start.8 = (bf16[512,256]{1,0:T(8,128)(2,1)}, bf16[512,256]{1,0:T(8,128)(2,1)S(1)}, u32[]{:S(2)}, u32[]{:S(2)}) collective-permute-start(bf16[512,256]{1,0:T(8,128)(2,1)} %get-tuple-element.31), channel_id=1, source_target_pairs={{0,1},{1,0},{2,3},{3,2},{4,5},{5,4},{6,7},{7,6},{8,9},{9,8},{10,11... | collective-permute-start | bytes 786440 | tf_op jit(solution)/shard_map/ppermute | solution.py:20
  49.4 5.2 %collective-permute-start.7 = (bf16[512,256]{1,0:T(8,128)(2,1)}, bf16[512,256]{1,0:T(8,128)(2,1)S(1)}, u32[]{:S(2)}, u32[]{:S(2)}) collective-permute-start(bf16[512,256]{1,0:T(8,128)(2,1)} %get-tuple-element.29), channel_id=1, source_target_pairs={{0,1},{1,0},{2,3},{3,2},{4,5},{5,4},{6,7},{7,6},{8,9},{9,8},{10,11... | collective-permute-start | bytes 786440 | tf_op jit(solution)/shard_map/ppermute | solution.py:20
  52.2 8.4 %collective-permute-start.9 = (bf16[512,256]{1,0:T(8,128)(2,1)S(1)}, bf16[512,256]{1,0:T(8,128)(2,1)S(1)}, u32[]{:S(2)}, u32[]{:S(2)}) collective-permute-start(bf16[512,256]{1,0:T(8,128)(2,1)S(1)} %add_convert_fusion.5), channel_id=1, source_target_pairs={{0,2},{1,3},{2,0},{3,1},{4,6},{5,7},{6,4},{7,5},{8,10},{9,11},{10,... | collective-permute-start | bytes 786440 | tf_op jit(solution)/shard_map/ppermute | solution.py:20
  54.6 6.0 %copy-start.16 = (bf16[512,256]{1,0:T(8,128)(2,1)}, bf16[512,256]{1,0:T(8,128)(2,1)S(1)}, u32[]{:S(2)}) copy-start(bf16[512,256]{1,0:T(8,128)(2,1)S(1)} %collective-permute-done.7.refs_1_) | copy-start | bytes 786436
  60.6 0.7 copy-start.17
  64.6 6.9 %copy-start.9 = (bf16[512,256]{1,0:T(8,128)(2,1)S(1)}, bf16[512,256]{1,0:T(8,128)(2,1)}, u32[]{:S(2)}) copy-start(bf16[512,256]{1,0:T(8,128)(2,1)} %get-tuple-element.33.refs_0_) | copy-start | bytes 786436
  67.2 1.8 %collective-permute-start.20 = (f32[2,136,256]{2,1,0:T(8,128)}, f32[2,136,256]{2,1,0:T(8,128)S(1)}, u32[]{:S(2)}, u32[]{:S(2)}) collective-permute-start(f32[2,136,256]{2,1,0:T(8,128)} %get-tuple-element.46), channel_id=1, source_target_pairs={{0,1},{1,0},{2,3},{3,2},{4,5},{5,4},{6,7},{7,6},{8,9},{9,8},{10,11... | collective-permute-start | bytes 835592 | tf_op jit(solution)/shard_map/ppermute | solution.py:20
  67.2 9.3 %collective-permute-start.11 = (bf16[512,256]{1,0:T(8,128)(2,1)}, bf16[512,256]{1,0:T(8,128)(2,1)S(1)}, u32[]{:S(2)}, u32[]{:S(2)}) collective-permute-start(bf16[512,256]{1,0:T(8,128)(2,1)} %get-tuple-element.33.refs_0_), channel_id=1, source_target_pairs={{0,2},{1,3},{2,0},{3,1},{4,6},{5,7},{6,4},{7,5},{8,10},{9,11},{10,... | collective-permute-start | bytes 786440 | tf_op jit(solution)/shard_map/ppermute | solution.py:20
  70.0 9.1 %collective-permute-start.21 = (f32[1,136,256]{2,1,0:T(8,128)S(1)}, f32[1,136,256]{2,1,0:T(8,128)S(1)}, u32[]{:S(2)}, u32[]{:S(2)}) collective-permute-start(f32[1,136,256]{2,1,0:T(8,128)S(1)} %slice.9), channel_id=1, source_target_pairs={{0,2},{1,3},{2,0},{3,1},{4,6},{5,7},{6,4},{7,5},{8,10},{9,11},{10,... | collective-permute-start | bytes 417800 | tf_op jit(solution)/shard_map/ppermute | solution.py:20
  71.6 9.2 %collective-permute-start.10 = (bf16[512,256]{1,0:T(8,128)(2,1)S(1)}, bf16[512,256]{1,0:T(8,128)(2,1)S(1)}, u32[]{:S(2)}, u32[]{:S(2)}) collective-permute-start(bf16[512,256]{1,0:T(8,128)(2,1)S(1)} %copy-done.9), channel_id=1, source_target_pairs={{0,1},{1,0},{2,3},{3,2},{4,5},{5,4},{6,7},{7,6},{8,9},{9,8},{10,11... | collective-permute-start | bytes 786440 | tf_op jit(solution)/shard_map/ppermute | solution.py:20
  76.6 4.2 %copy-start.10 = (bf16[512,256]{1,0:T(8,128)(2,1)}, bf16[512,256]{1,0:T(8,128)(2,1)S(1)}, u32[]{:S(2)}) copy-start(bf16[512,256]{1,0:T(8,128)(2,1)S(1)} %collective-permute-done.11.refs_2_) | copy-start | bytes 786436
  76.6 4.2 %collective-permute-start.12 = (bf16[512,256]{1,0:T(8,128)(2,1)S(1)}, bf16[512,256]{1,0:T(8,128)(2,1)S(1)}, u32[]{:S(2)}, u32[]{:S(2)}) collective-permute-start(bf16[512,256]{1,0:T(8,128)(2,1)S(1)} %collective-permute-done.11.refs_2_), channel_id=1, source_target_pairs={{0,1},{1,0},{2,3},{3,2},{4,5},{5,4},{6,7},{7,6},{8,9},{9,8},{10,11... | collective-permute-start | bytes 786440 | tf_op jit(solution)/shard_map/ppermute | solution.py:20
  79.2 8.9 %collective-permute-start.22 = (f32[136,256]{1,0:T(8,128)S(1)}, f32[136,256]{1,0:T(8,128)S(1)}, u32[]{:S(2)}, u32[]{:S(2)}) collective-permute-start(f32[136,256]{1,0:T(8,128)S(1)} %fusion), channel_id=1, source_target_pairs={{0,4},{4,0},{8,12},{12,8},{16,20},{20,16},{24,28},{28,24},{1,5},{5... | collective-permute-start | bytes 417800 | tf_op jit(solution)/shard_map/ppermute | solution.py:20
  80.8 0.7 copy-start.11
  80.8 0.8 copy-start.12
  87.7 20.8 %copy-start.15 = (bf16[512,256]{1,0:T(8,128)(2,1)S(1)}, bf16[512,256]{1,0:T(8,128)(2,1)}, u32[]{:S(2)}) copy-start(bf16[512,256]{1,0:T(8,128)(2,1)} %get-tuple-element.36) | copy-start | bytes 786436
  87.7 9.5 %collective-permute-start.17 = (bf16[512,256]{1,0:T(8,128)(2,1)}, bf16[512,256]{1,0:T(8,128)(2,1)S(1)}, u32[]{:S(2)}, u32[]{:S(2)}) collective-permute-start(bf16[512,256]{1,0:T(8,128)(2,1)} %get-tuple-element.41), channel_id=1, source_target_pairs={{0,4},{4,0},{8,12},{12,8},{16,20},{20,16},{24,28},{28,24},{1,5},{5... | collective-permute-start | bytes 786440 | tf_op jit(solution)/shard_map/ppermute | solution.py:20
  88.1 24.4 %copy-start.19 = (bf16[512,256]{1,0:T(8,128)(2,1)S(1)}, bf16[512,256]{1,0:T(8,128)(2,1)}, u32[]{:S(2)}) copy-start(bf16[512,256]{1,0:T(8,128)(2,1)} %get-tuple-element.38) | copy-start | bytes 786436
  88.2 5.1 %collective-permute-start.23 = (f32[136,256]{1,0:T(8,128)S(1)}, f32[136,256]{1,0:T(8,128)S(1)}, u32[]{:S(2)}, u32[]{:S(2)}) collective-permute-start(f32[136,256]{1,0:T(8,128)S(1)} %add.53), channel_id=1, source_target_pairs={{0,8},{4,12},{8,0},{12,4},{16,24},{20,28},{24,16},{28,20},{1,9},{5... | collective-permute-start | bytes 417800 | tf_op jit(solution)/shard_map/ppermute | solution.py:20
  89.0 34.5 %collective-permute-start.13 = (bf16[512,256]{1,0:T(8,128)(2,1)}, bf16[512,256]{1,0:T(8,128)(2,1)S(1)}, u32[]{:S(2)}, u32[]{:S(2)}) collective-permute-start(bf16[512,256]{1,0:T(8,128)(2,1)} %get-tuple-element.35), channel_id=1, source_target_pairs={{0,4},{4,0},{8,12},{12,8},{16,20},{20,16},{24,28},{28,24},{1,5},{5... | collective-permute-start | bytes 786440 | tf_op jit(solution)/shard_map/ppermute | solution.py:20
  90.2 18.2 %collective-permute-start.14 = (bf16[512,256]{1,0:T(8,128)(2,1)}, bf16[512,256]{1,0:T(8,128)(2,1)S(1)}, u32[]{:S(2)}, u32[]{:S(2)}) collective-permute-start(bf16[512,256]{1,0:T(8,128)(2,1)} %get-tuple-element.37), channel_id=1, source_target_pairs={{0,4},{4,0},{8,12},{12,8},{16,20},{20,16},{24,28},{28,24},{1,5},{5... | collective-permute-start | bytes 786440 | tf_op jit(solution)/shard_map/ppermute | solution.py:20
  91.1 21.5 %collective-permute-start.16 = (bf16[512,256]{1,0:T(8,128)(2,1)}, bf16[512,256]{1,0:T(8,128)(2,1)S(1)}, u32[]{:S(2)}, u32[]{:S(2)}) collective-permute-start(bf16[512,256]{1,0:T(8,128)(2,1)} %get-tuple-element.39), channel_id=1, source_target_pairs={{0,4},{4,0},{8,12},{12,8},{16,20},{20,16},{24,28},{28,24},{1,5},{5... | collective-permute-start | bytes 786440 | tf_op jit(solution)/shard_map/ppermute | solution.py:20
  93.3 8.9 %collective-permute-start.24 = (f32[136,256]{1,0:T(8,128)S(1)}, f32[136,256]{1,0:T(8,128)S(1)}, u32[]{:S(2)}, u32[]{:S(2)}) collective-permute-start(f32[136,256]{1,0:T(8,128)S(1)} %add.54), channel_id=1, source_target_pairs={{0,16},{4,20},{8,24},{12,28},{16,0},{20,4},{24,8},{28,12},{1,17},{... | collective-permute-start | bytes 417800 | tf_op jit(solution)/shard_map/ppermute | solution.py:20
  98.2 14.4 %collective-permute-start.18 = (bf16[512,256]{1,0:T(8,128)(2,1)S(1)}, bf16[512,256]{1,0:T(8,128)(2,1)S(1)}, u32[]{:S(2)}, u32[]{:S(2)}) collective-permute-start(bf16[512,256]{1,0:T(8,128)(2,1)S(1)} %add_convert_fusion.2), channel_id=1, source_target_pairs={{0,8},{4,12},{8,0},{12,4},{16,24},{20,28},{24,16},{28,20},{1,9},{5... | collective-permute-start | bytes 786440 | tf_op jit(solution)/shard_map/ppermute | solution.py:20
  102.3 6.7 %collective-permute-start.25 = (f32[1,136,256]{2,1,0:T(8,128)S(1)}, f32[1,136,256]{2,1,0:T(8,128)S(1)}, u32[]{:S(2)}, u32[]{:S(2)}) collective-permute-start(f32[1,136,256]{2,1,0:T(8,128)S(1)} %get-tuple-element.51), channel_id=1, source_target_pairs={{0,2},{1,3},{2,0},{3,1},{4,6},{5,7},{6,4},{7,5},{8,10},{9,11},{10,... | collective-permute-start | bytes 417800 | tf_op jit(solution)/shard_map/ppermute | solution.py:20
  108.5 15.0 %collective-permute-start.15 = (bf16[512,256]{1,0:T(8,128)(2,1)S(1)}, bf16[512,256]{1,0:T(8,128)(2,1)S(1)}, u32[]{:S(2)}, u32[]{:S(2)}) collective-permute-start(bf16[512,256]{1,0:T(8,128)(2,1)S(1)} %add_convert_fusion.4), channel_id=1, source_target_pairs={{0,8},{4,12},{8,0},{12,4},{16,24},{20,28},{24,16},{28,20},{1,9},{5... | collective-permute-start | bytes 786440 | tf_op jit(solution)/shard_map/ppermute | solution.py:20
  109.0 11.9 %copy-start.1 = (f32[2,136,256]{2,1,0:T(8,128)}, f32[2,136,256]{2,1,0:T(8,128)S(1)}, u32[]{:S(2)}) copy-start(f32[2,136,256]{2,1,0:T(8,128)S(1)} %maximum_bitcast_fusion.even) | copy-start | bytes 835588
  109.0 11.9 %collective-permute-start.26 = (f32[2,136,256]{2,1,0:T(8,128)S(1)}, f32[2,136,256]{2,1,0:T(8,128)S(1)}, u32[]{:S(2)}, u32[]{:S(2)}) collective-permute-start(f32[2,136,256]{2,1,0:T(8,128)S(1)} %maximum_bitcast_fusion.even), channel_id=1, source_target_pairs={{0,1},{1,0},{2,3},{3,2},{4,5},{5,4},{6,7},{7,6},{8,9},{9,8},{10,11... | collective-permute-start | bytes 835592 | tf_op jit(solution)/shard_map/ppermute | solution.py:20
  112.7 13.9 %collective-permute-start.19 = (bf16[512,256]{1,0:T(8,128)(2,1)S(1)}, bf16[512,256]{1,0:T(8,128)(2,1)S(1)}, u32[]{:S(2)}, u32[]{:S(2)}) collective-permute-start(bf16[512,256]{1,0:T(8,128)(2,1)S(1)} %add_convert_fusion.1), channel_id=1, source_target_pairs={{0,16},{4,20},{8,24},{12,28},{16,0},{20,4},{24,8},{28,12},{1,17},{... | collective-permute-start | bytes 786440 | tf_op jit(solution)/shard_map/ppermute | solution.py:20
  116.1 10.6 %copy-start.13 = (f32[512,256]{1,0:T(8,128)S(1)}, f32[512,256]{1,0:T(8,128)}, u32[]{:S(2)}) copy-start(f32[512,256]{1,0:T(8,128)} %get-tuple-element.44) | copy-start | bytes 1572868
  116.1 10.6 %copy-start.18 = (bf16[512,256]{1,0:T(8,128)(2,1)S(1)}, bf16[512,256]{1,0:T(8,128)(2,1)}, u32[]{:S(2)}) copy-start(bf16[512,256]{1,0:T(8,128)(2,1)} %get-tuple-element.34) | copy-start | bytes 786436
  120.9 0.7 copy-start.14

commit v2 on v1

v2 whole, which is shorter than its diff:
```python
import functools
import math

import jax
import jax.numpy as jnp
from jax import lax
from jax.experimental import pallas as pl
from jax.experimental.pallas import tpu as pltpu
from jax.sharding import PartitionSpec as P

BF16 = jnp.bfloat16
F32 = jnp.float32
VMEM = pl.BlockSpec(memory_space=pltpu.VMEM)
HBM = pl.BlockSpec(memory_space=pltpu.HBM)
SMEM = pl.BlockSpec(memory_space=pltpu.SMEM)


def exchange(value, axis, bit):
    size = lax.axis_size(axis)
    return lax.ppermute(value, axis, [(i, i ^ bit) for i in range(size)])


def bits_of(size):
    assert size & (size - 1) == 0
    return [1 << n for n in range(size.bit_length() - 1)]


def tie(*values):
    return lax.optimization_barrier(values)


def gather_by_offset(own, axis):
    held = {0: own}
    for bit in reversed(bits_of(lax.axis_size(axis))):
        for offset in list(held):
            held[offset | bit] = exchange(held[offset], axis, bit)
    return [held[k] for k in range(lax.axis_size(axis))]


def gather_rows(own, axis):
    size = lax.axis_size(axis)
    if size != 8:
        held = gather_by_offset(own, axis)
        return held, held[1]
    near = exchange(own, axis, 1)
    far = exchange(own, axis, 4)
    diagonal = exchange(own, axis, 3)
    far, near = tie(far, near)
    middle = exchange(own, axis, 2)
    far_near = exchange(far, axis, 1)
    far_middle = exchange(far, axis, 2)
    far_middle, diagonal = tie(far_middle, diagonal)
    last = exchange(far_middle, axis, 1)
    return [own, near, middle, diagonal, far, far_near, far_middle, last], near


def add_rounded(*terms):
    return sum(term.astype(F32) for term in terms).astype(BF16)


def scatter_by_offset(parts, axis):
    parts = dict(enumerate(parts))
    last = []
    for bit in bits_of(lax.axis_size(axis)):
        for offset in sorted(parts, reverse=True):
            if offset & bit:
                got = exchange(parts.pop(offset), axis, bit)
                if offset ^ bit:
                    parts[offset ^ bit] = add_rounded(parts[offset ^ bit], got)
                else:
                    last.append(got)
    return [parts[0]] + last


def scatter_rows(parts, axis):
    if lax.axis_size(axis) != 8:
        return scatter_by_offset(parts, axis)
    got7 = exchange(parts[7], axis, 1)
    got5 = exchange(parts[5], axis, 1)
    got2 = exchange(parts[2], axis, 2)
    got7, part1, part3 = tie(got7, parts[1], parts[3])
    got6 = exchange(add_rounded(parts[6], got7), axis, 2)
    got1 = exchange(part1, axis, 1)
    got3 = exchange(part3, axis, 3)
    got4 = exchange(add_rounded(parts[4], got5, got6), axis, 4)
    return [parts[0], got1, got2, got3, got4]


def nbytes(shape, dtype):
    return math.prod(shape) * jnp.dtype(dtype).itemsize


def kernel_call(body, outs, in_specs, out_specs, scratch, flops, args):
    listed = jax.tree.leaves(outs)
    moved = sum(nbytes(a.shape, a.dtype) for a in (*args, *listed))
    held = moved + sum(nbytes(x.shape, x.dtype) for x in scratch if x.shape[-1] > 8)
    return pl.pallas_call(
        body,
        out_shape=outs,
        in_specs=in_specs,
        out_specs=out_specs,
        scratch_shapes=scratch,
        compiler_params=pltpu.CompilerParams(vmem_limit_bytes=held + held // 4 + 4 * 1024 * 1024),
        cost_estimate=pl.CostEstimate(flops=flops, bytes_accessed=moved, transcendentals=0),
    )(*args)


def tn(a, b):
    return lax.dot_general(a, b, (((0,), (0,)), ((), ())), preferred_element_type=F32)


def nt(a, b):
    return lax.dot_general(a, b, (((1,), (1,)), ((), ())), preferred_element_type=F32)


def each(count, step):
    lax.fori_loop(0, count, lambda i, carry: (step(i), carry)[1], 0)


def copy_all(refs, held, size):
    rows = refs[0].shape[0]
    for k, ref in enumerate(refs):

        def move(i):
            held[pl.ds(pl.multiple_of(k * rows + i * size, size), size), :] = ref[
                pl.ds(pl.multiple_of(i * size, size), size), :
            ]

        each(rows // size, move)


def block_of(cols, slot, own, r, size):
    m = cols[slot]
    return pl.ds(pl.multiple_of((((m // own) ^ r) * own + m % own) * size, size), size)


def live_body(count, edges, out):
    used = count[0]

    def move(slot):
        block = edges[slot]
        out[slot] = jnp.where(slot < used, block, jnp.zeros_like(block))

    each(edges.shape[0], move)


def select_rows(mask, k, size):
    shape = (size, size)
    diagonal = lax.broadcasted_iota(jnp.int32, shape, 0) == lax.broadcasted_iota(jnp.int32, shape, 1)
    live = jnp.broadcast_to(mask[pl.ds(k, 1), :], shape) != 0
    return jnp.where(live & diagonal, 1.0, 0.0).astype(BF16)


def mask_body(size, mask, feats, out, mask_here, feats_here, sems):
    first = pltpu.make_async_copy(mask, mask_here, sems.at[0])
    second = pltpu.make_async_copy(feats, feats_here, sems.at[1])
    first.start()
    second.start()
    first.wait()
    second.wait()
    for k in range(mask.shape[0]):
        rows = pl.ds(k * size, size)
        select = select_rows(mask_here, k, size)
        picked = jnp.dot(select, feats_here[rows, :], preferred_element_type=F32)
        out[rows, :] = picked.astype(BF16)


def prepare_body(size, mask, feats, w_msg, w_self, bias, grad_out, base, grad_live, w_out):
    for k in range(mask.shape[0]):
        rows = pl.ds(k * size, size)
        select = select_rows(mask, k, size)
        own = jnp.dot(feats[rows, :], w_self[...], preferred_element_type=F32)
        base[rows, :] = own + bias[...]
        picked = jnp.dot(select, grad_out[rows, :], preferred_element_type=F32)
        grad_live[rows, :] = picked.astype(BF16)
    w_out[...] = w_msg[...]


def spmm_body(n_row, n_col, size, depth, cols, place, edges, *refs):
    feats, outs, held = refs[:n_row], refs[n_row : n_row + n_col], refs[n_row + n_col]
    own = outs[0].shape[0] // size
    copy_all(feats, held, size)
    r, c = place[0], place[1]
    for offset in reversed(range(n_col)):
        for i in range(own):
            row = (c ^ offset) * own + i
            slots = [k * n_col * own + row for k in range(depth)]
            blocks = jnp.concatenate([edges[slot] for slot in slots], axis=1)
            picked = [held[block_of(cols, slot, own, r, size), :] for slot in slots]
            total = jnp.dot(blocks, jnp.concatenate(picked, axis=0), preferred_element_type=F32)
            outs[offset][pl.ds(i * size, size), :] = total.astype(BF16)


def back_body(n_row, n_col, size, depth, cols, place, edges, *refs):
    grads, outs = refs[:n_col], refs[n_col : n_col + n_row]
    terms, total = refs[n_col + n_row :]
    own = outs[0].shape[0] // size
    r, c = place[0], place[1]

    def clear(i):
        rows = pl.ds(pl.multiple_of(i * size, size), size)
        total[rows, :] = jnp.zeros((size, total.shape[1]), F32)

    each(total.shape[0] // size, clear)
    slots = []
    for offset in range(n_col):
        for i in range(own):
            row = (c ^ offset) * own + i
            grad = grads[offset][pl.ds(i * size, size), :]
            for k in range(depth):
                slot = k * n_col * own + row
                terms[len(slots)] = tn(edges[slot], grad)
                slots.append(slot)
    for at, slot in enumerate(slots):
        spot = block_of(cols, slot, own, r, size)
        total[spot, :] = total[spot, :] + terms[at]
    for k in range(n_row):

        def leave(i):
            rows = pl.ds(pl.multiple_of((k * own + i) * size, size), size)
            outs[k][pl.ds(pl.multiple_of(i * size, size), size), :] = total[rows, :].astype(BF16)

        each(own, leave)


def edge_body(n_row, n_col, size, depth, cols, count, place, *refs):
    grads, (held, out) = refs[:n_col], refs[n_col:]
    own = grads[0].shape[0] // size
    r, c, used = place[0], place[1], count[0]
    for offset in range(n_col):
        for i in range(own):
            row = (c ^ offset) * own + i
            grad = grads[offset][pl.ds(i * size, size), :]
            for k in range(depth):
                slot = k * n_col * own + row
                value = nt(grad, held[block_of(cols, slot, own, r, size), :])
                out[slot] = jnp.where(slot < used, value, jnp.zeros_like(value)).astype(BF16)


def activate(size, k, terms, base, grad_live, w_msg):
    rows = pl.ds(k * size, size)
    total = terms[0][rows, :].astype(F32)
    for term in terms[1:]:
        total = total + term[rows, :].astype(F32)
    high = total.astype(BF16)
    low = (total - high.astype(F32)).astype(BF16)
    pre = jnp.dot(high, w_msg[...], preferred_element_type=F32)
    pre = pre + jnp.dot(low, w_msg[...], preferred_element_type=F32) + base[rows, :]
    sig = jax.nn.sigmoid(pre)
    deriv = sig * (1.0 + pre * (1.0 - sig))
    return high, pre, sig, (grad_live[rows, :].astype(F32) * deriv).astype(BF16)


def act_body(size, n_terms, *refs):
    terms = refs[:n_terms]
    base, grad_live, w_msg, grad_w = refs[n_terms:]
    for k in range(base.shape[0] // size):
        grad = activate(size, k, terms, base, grad_live, w_msg)[3]
        grad_w[pl.ds(k * size, size), :] = nt(grad, w_msg[...]).astype(BF16)


def weight_body(size, n_terms, factor, place, mask, *refs):
    terms = refs[:n_terms]
    base, grad_live, w_msg, feats, w_self, hidden, own_part, same, other = refs[n_terms:-3]
    summed, grad_pre, stack = refs[-3:]
    width = feats.shape[1]
    for k in range(feats.shape[0] // size):
        rows = pl.ds(k * size, size)
        high, pre, sig, grad = activate(size, k, terms, base, grad_live, w_msg)
        summed[rows, :] = high
        grad_pre[rows, :] = grad
        value = (pre * sig).astype(BF16)
        picked = jnp.dot(select_rows(mask, k, size), value, preferred_element_type=F32)
        hidden[rows, :] = picked.astype(BF16)
        own_part[rows, :] = nt(grad, w_self[...])
    grad = grad_pre[...]
    stack[pl.ds(0, width), :] = tn(summed[...], grad) * factor
    stack[pl.ds(width, width), :] = tn(feats[...], grad) * factor
    rest = stack.shape[0] - 2 * width
    total = jnp.sum(grad.astype(F32), axis=0, keepdims=True) * factor
    stack[pl.ds(2 * width, rest), :] = jnp.broadcast_to(total, (rest, width))
    half = stack.shape[0] // 2
    core = place[1] % 2
    same[...] = stack[pl.ds(pl.multiple_of(core * half, 8), half), :]
    other[...] = stack[pl.ds(pl.multiple_of((1 - core) * half, 8), half), :]


def join_body(place, same, other, w_msg, w_self, bias, stack):
    width = w_msg.shape[0]
    half = stack.shape[0] // 2
    core = place[1] % 2
    stack[pl.ds(pl.multiple_of(core * half, 8), half), :] = same[...]
    stack[pl.ds(pl.multiple_of((1 - core) * half, 8), half), :] = other[...]
    w_msg[...] = stack[pl.ds(0, width), :]
    w_self[...] = stack[pl.ds(width, width), :]
    bias[...] = stack[pl.ds(2 * width, 1), :]


def per_device(feats, w_msg, w_self, bias, hit_mask, block_cols, block_count, edge_vals, grad_out):
    n_row, n_col = lax.axis_size("row"), lax.axis_size("col")
    own_rows, width = feats.shape
    edges = edge_vals[0, 0]
    slots, size = edges.shape[0], edges.shape[1]
    own = own_rows // size
    tile_rows = n_col * own
    depth = slots // tile_rows
    cols, count = block_cols[0, 0], block_count[0]
    place = jnp.stack([lax.axis_index("row"), lax.axis_index("col")]).astype(jnp.int32)
    mask = hit_mask.reshape(own, size)
    block = jax.ShapeDtypeStruct((own_rows, width), BF16)
    wide = jax.ShapeDtypeStruct((own_rows, width), F32)
    edge_flops = 2 * slots * size * size * width
    dims = (n_row, n_col, size, depth)

    masked = kernel_call(
        functools.partial(mask_body, size),
        block,
        [HBM] * 2,
        VMEM,
        [
            pltpu.VMEM((own, size), jnp.int32),
            pltpu.VMEM((own_rows, width), BF16),
            pltpu.SemaphoreType.DMA((2,)),
        ],
        2 * own_rows * size * width,
        (mask, feats),
    )
    held, early = gather_rows(masked, "row")
    late_count, late_bias, _ = tie(count, bias, early)
    live = kernel_call(
        live_body,
        jax.ShapeDtypeStruct(edges.shape, BF16),
        [SMEM, VMEM],
        VMEM,
        [],
        0,
        (late_count, edges),
    )
    base, grad_live, w_here = kernel_call(
        functools.partial(prepare_body, size),
        [wide, block, jax.ShapeDtypeStruct(w_msg.shape, BF16)],
        [VMEM] * 6,
        [VMEM] * 3,
        [],
        2 * own_rows * width * (width + size),
        (mask, feats, w_msg, w_self, late_bias[None, :], grad_out),
    )

    *partial, together = kernel_call(
        functools.partial(spmm_body, *dims),
        [block] * n_col + [jax.ShapeDtypeStruct((n_row * own_rows, width), BF16)],
        [SMEM] * 2 + [VMEM] * (1 + n_row),
        [VMEM] * (n_col + 1),
        [],
        edge_flops,
        (cols, place, live, *held),
    )
    terms = scatter_by_offset(partial, "col")

    grad_w = kernel_call(
        functools.partial(act_body, size, len(terms)),
        block,
        [VMEM] * (len(terms) + 3),
        VMEM,
        [],
        6 * own_rows * width * width,
        (*terms, base, grad_live, w_here),
    )
    grads = gather_by_offset(grad_w, "col")

    pieces = kernel_call(
        functools.partial(back_body, *dims),
        [block] * n_row,
        [SMEM] * 2 + [VMEM] * (1 + n_col),
        [VMEM] * n_row,
        [
            pltpu.VMEM((slots, size, width), F32),
            pltpu.VMEM((n_row * own_rows, width), F32),
        ],
        edge_flops,
        (cols, place, live, *grads),
    )

    rows = 2 * width + 32
    half = jax.ShapeDtypeStruct((rows // 2, width), F32)
    factor = 1.0 / math.sqrt(own_rows * n_row * n_col)
    late_live, _ = tie(grad_live, grads[1])
    hidden, own_part, same, other = kernel_call(
        functools.partial(weight_body, size, len(terms), factor),
        [block, wide, half, half],
        [SMEM] + [VMEM] * (len(terms) + 6),
        [VMEM] * 4,
        [
            pltpu.VMEM((own_rows, width), BF16),
            pltpu.VMEM((own_rows, width), BF16),
            pltpu.VMEM((rows, width), F32),
        ],
        14 * own_rows * width * width,
        (place, mask, *terms, base, late_live, w_here, feats, w_self),
    )
    total = same + exchange(other, "col", 1)
    steps = [("row", bit) for bit in reversed(bits_of(n_row))]
    steps = steps[:-1] + [("col", bit) for bit in bits_of(n_col)[1:]] + steps[-1:]
    for axis, bit in steps:
        sent = total.astype(BF16)
        total = sent.astype(F32) + exchange(sent, axis, bit).astype(F32)
    square = jax.ShapeDtypeStruct((width, width), F32)
    msg_grad, self_grad, bias_grad = kernel_call(
        join_body,
        [square, square, jax.ShapeDtypeStruct((1, width), F32)],
        [SMEM] + [VMEM] * 2,
        [VMEM] * 3,
        [pltpu.VMEM((rows, width), F32)],
        0,
        (place, total, exchange(total, "col", 1)),
    )

    edge_grad = kernel_call(
        functools.partial(edge_body, *dims),
        jax.ShapeDtypeStruct((slots, size, size), BF16),
        [SMEM] * 3 + [VMEM] * (n_col + 1),
        VMEM,
        [],
        edge_flops,
        (cols, count, place, *grads, together),
    )

    back = scatter_rows(pieces, "row")
    column = (hit_mask != 0)[:, None]
    early = jnp.where(column, sum(term.astype(F32) for term in back[:-1]), 0.0) + own_part
    early, last = tie(early, back[-1])
    grad_feats = (early + jnp.where(column, last.astype(F32), 0.0)).astype(BF16)
    return hidden, grad_feats, edge_grad[None, None], msg_grad, self_grad, bias_grad[0]


def solution(mesh):
    placed = (
        P(("row", "col"), None),
        P(),
        P(),
        P(),
        P(("row", "col")),
        P("row", "col", None),
        P("row", "col"),
        P("row", "col", None, None, None),
        P(("row", "col"), None),
    )
    return jax.shard_map(
        per_device,
        mesh=mesh,
        in_specs=placed,
        out_specs=(
            P(("row", "col"), None),
            P(("row", "col"), None),
            P("row", "col", None, None, None),
            P(),
            P(),
            P(),
        ),
        check_vma=False,
    )
```

time: 128 us -> 103 us (0.80)
  Pallas kernels: 23.5 us -> 11.8 us
  waiting for transfers between devices: 60.7 us -> 53.5 us
  other arithmetic: 6.56 us -> 1.55 us
    pallas_call x6 -> x9, Pallas kernels: 23.5 us -> 11.8 us  [kernel_call(): pl.pallas_call(body, out_shape=outs, in_specs=in_specs, out_specs=out_spe...]
    ppermute x27 -> x26, waiting for transfers between devices: 60.7 us -> 53.5 us  [exchange(): return lax.ppermute(value, axis, [(i, i ^ bit) for i in range(size)])]
    convert_element_type x5 -> x8, other arithmetic: 3.09 us -> 1.24 us  [the longest x1 0.85 us: per_device(): grad_feats = (early + jnp.where(column, last.astype(F32), 0.0)).astype(BF16)]
    unnamed x42 -> x20, local copies, waits for them, and re-layouts: 2.86 us -> 3.06 us
    ppermute x27 -> x26, starting transfers between devices: 31.5 us -> 31.6 us  [exchange(): return lax.ppermute(value, axis, [(i, i ^ bit) for i in range(size)])]
  transfers between devices with their start and end apart: 27 -> 26, of which waited for: 16 -> 13; matrix products, arithmetic and copies ran while one was open for 4% -> 2% of each run, Pallas kernels for 10% -> 6%
where the time goes in v2:
time: 103 us
  waiting for transfers between devices  53.5 us (52%)
  starting transfers between devices  31.6 us (31%)
  Pallas kernels  11.8 us (11%)
  local copies, waits for them, and re-layouts  3.06 us (3%)
  other arithmetic  1.55 us (2%)
  between operations  1.53 us (1%)
    ppermute x26, waiting for transfers between devices, exchange(): return lax.ppermute(value, axis, [(i, i ^ bit) for i in range(size)])  53.5 us
    ppermute x26, starting transfers between devices, exchange(): return lax.ppermute(value, axis, [(i, i ^ bit) for i in range(size)])  31.6 us
    pallas_call x9, Pallas kernels, kernel_call(): pl.pallas_call(body, out_shape=outs, in_specs=in_specs, out_specs=out_spe...  11.8 us
    unnamed x20, local copies, waits for them, and re-layouts  3.06 us
  transfers between devices with their start and end apart: 26, of which 13 were waited for; matrix products, arithmetic and copies ran while one was open for 2% of the time, Pallas kernels for 6%

profile of v2, /device:TPU:0, one launch (start us, length us, event | category | flops | bytes accessed | tf_op | source)
XLA Modules:
  0.0 103.0 jit_solution(3946513547315636242)
XLA Ops:
  0.6 0.0 copy-start
  0.6 0.9 copy-done
  1.6 0.7 copy-done.6
  2.3 0.3 shard_map.136.refs_0_
  2.5 4.1 %collective-permute-start = (bf16[512,256]{1,0:T(8,128)(2,1)S(1)}, bf16[512,256]{1,0:T(8,128)(2,1)S(1)}, u32[]{:S(2)}, u32[]{:S(2)}) collective-permute-start(bf16[512,256]{1,0:T(8,128)(2,1)S(1)} %shard_map.136.refs_0_), channel_id=1, source_target_pairs={{0,16},{4,20},{8,24},{12,28},{16,0},{20,4},{24,8},{28,12},{1,17},{... | collective-permute-start | bytes 786440 | tf_op jit(solution)/shard_map/ppermute | solution.py:20
  6.6 1.5 %collective-permute-start.1 = (bf16[512,256]{1,0:T(8,128)(2,1)S(1)}, bf16[512,256]{1,0:T(8,128)(2,1)S(1)}, u32[]{:S(2)}, u32[]{:S(2)}) collective-permute-start(bf16[512,256]{1,0:T(8,128)(2,1)S(1)} %shard_map.136.refs_0_), channel_id=1, source_target_pairs={{0,4},{4,0},{8,12},{12,8},{16,20},{20,16},{24,28},{28,24},{1,5},{5... | collective-permute-start | bytes 786440 | tf_op jit(solution)/shard_map/ppermute | solution.py:20
  8.2 1.5 %collective-permute-start.4 = (bf16[512,256]{1,0:T(8,128)(2,1)S(1)}, bf16[512,256]{1,0:T(8,128)(2,1)S(1)}, u32[]{:S(2)}, u32[]{:S(2)}) collective-permute-start(bf16[512,256]{1,0:T(8,128)(2,1)S(1)} %shard_map.136.refs_0_), channel_id=1, source_target_pairs={{0,12},{4,8},{8,4},{12,0},{16,28},{20,24},{24,20},{28,16},{1,13},{... | collective-permute-start | bytes 786440 | tf_op jit(solution)/shard_map/ppermute | solution.py:20
  9.7 9.0 %collective-permute-done.refs_4_ = bf16[512,256]{1,0:T(8,128)(2,1)S(1)} collective-permute-done((bf16[512,256]{1,0:T(8,128)(2,1)S(1)}, bf16[512,256]{1,0:T(8,128)(2,1)S(1)}, u32[]{:S(2)}, u32[]{:S(2)}) %collective-permute-start) | collective-permute-done | bytes 262176 | tf_op jit(solution)/shard_map/ppermute | solution.py:20
  18.7 0.0 collective-permute-done.1.refs_1_
  18.7 2.9 %collective-permute-start.3 = (bf16[512,256]{1,0:T(8,128)(2,1)S(1)}, bf16[512,256]{1,0:T(8,128)(2,1)S(1)}, u32[]{:S(2)}, u32[]{:S(2)}) collective-permute-start(bf16[512,256]{1,0:T(8,128)(2,1)S(1)} %collective-permute-done.refs_4_), channel_id=1, source_target_pairs={{0,8},{4,12},{8,0},{12,4},{16,24},{20,28},{24,16},{28,20},{1,9},{5... | collective-permute-start | bytes 786440 | tf_op jit(solution)/shard_map/ppermute | solution.py:20
  21.6 0.0 collective-permute-start.2
  21.6 1.5 %collective-permute-start.5 = (bf16[512,256]{1,0:T(8,128)(2,1)S(1)}, bf16[512,256]{1,0:T(8,128)(2,1)S(1)}, u32[]{:S(2)}, u32[]{:S(2)}) collective-permute-start(bf16[512,256]{1,0:T(8,128)(2,1)S(1)} %collective-permute-done.refs_4_), channel_id=1, source_target_pairs={{0,4},{4,0},{8,12},{12,8},{16,20},{20,16},{24,28},{28,24},{1,5},{5... | collective-permute-start | bytes 786440 | tf_op jit(solution)/shard_map/ppermute | solution.py:20
  23.1 0.0 collective-permute-done.4.refs_3_
  23.2 5.7 %collective-permute-done.3.refs_6_ = bf16[512,256]{1,0:T(8,128)(2,1)S(1)} collective-permute-done((bf16[512,256]{1,0:T(8,128)(2,1)S(1)}, bf16[512,256]{1,0:T(8,128)(2,1)S(1)}, u32[]{:S(2)}, u32[]{:S(2)}) %collective-permute-start.3) | collective-permute-done | bytes 262176 | tf_op jit(solution)/shard_map/ppermute | solution.py:20
  28.8 1.4 %collective-permute-start.6 = (bf16[512,256]{1,0:T(8,128)(2,1)S(1)}, bf16[512,256]{1,0:T(8,128)(2,1)S(1)}, u32[]{:S(2)}, u32[]{:S(2)}) collective-permute-start(bf16[512,256]{1,0:T(8,128)(2,1)S(1)} %collective-permute-done.3.refs_6_), channel_id=1, source_target_pairs={{0,4},{4,0},{8,12},{12,8},{16,20},{20,16},{24,28},{28,24},{1,5},{5... | collective-permute-start | bytes 786440 | tf_op jit(solution)/shard_map/ppermute | solution.py:20
  30.8 0.0 copy-start.2
  30.8 1.4 %copy-done.2 = bf16[1,1,48,128,128]{4,3,2,1,0:T(8,128)(2,1)S(1)} copy-done((bf16[1,1,48,128,128]{4,3,2,1,0:T(8,128)(2,1)S(1)}, bf16[1,1,48,128,128]{4,3,2,1,0:T(8,128)(2,1)}, u32[]{:S(2)}) %copy-start.2) | copy-done | bytes 1572888
  32.2 0.6 shard_map.137.edges
  32.8 0.1 pad_add_fusion.place
  32.9 0.0 collective-permute-done.2.refs_2_
  32.9 2.3 %collective-permute-done.6.refs_7_ = bf16[512,256]{1,0:T(8,128)(2,1)S(1)} collective-permute-done((bf16[512,256]{1,0:T(8,128)(2,1)S(1)}, bf16[512,256]{1,0:T(8,128)(2,1)S(1)}, u32[]{:S(2)}, u32[]{:S(2)}) %collective-permute-start.6) | collective-permute-done | bytes 262176 | tf_op jit(solution)/shard_map/ppermute | solution.py:20
  35.2 0.0 copy-start.5
  35.2 0.0 copy-start.7
  35.2 0.0 copy-start.9
  35.2 1.5 %shard_map.138 = (bf16[512,256]{1,0:T(8,128)(2,1)S(1)}, bf16[512,256]{1,0:T(8,128)(2,1)S(1)}, bf16[512,256]{1,0:T(8,128)(2,1)S(1)}, bf16[512,256]{1,0:T(8,128)(2,1)S(1)}, bf16[4096,256]{1,0:T(8,128)(2,1)S(1)}) custom-call(s32[48]{0:T(128)S(1)} %bitcast.15, s32[2]{0:T(128)S(1)} %pad_add_fusion.place, bf16[48,128,128]{2,1,0:T(8,128)(2,1)S(1)} %shard_map.137.edges, ...), custom_call_target="tpu_custom_call" | custom-call | flops 402653184 | bytes 6815944 | tf_op jit(solution)/shard_map/pallas_call | solution.py:97
  36.8 0.1 collective-permute-start.8
  36.8 0.5 collective-permute-start.7
  37.3 1.0 collective-permute-done.8
  38.4 0.1 add_convert_fusion.3
  38.4 1.4 %collective-permute-start.9 = (bf16[512,256]{1,0:T(8,128)(2,1)S(1)}, bf16[512,256]{1,0:T(8,128)(2,1)S(1)}, u32[]{:S(2)}, u32[]{:S(2)}) collective-permute-start(bf16[512,256]{1,0:T(8,128)(2,1)S(1)} %add_convert_fusion.3), channel_id=1, source_target_pairs={{0,2},{1,3},{2,0},{3,1},{4,6},{5,7},{6,4},{7,5},{8,10},{9,11},{10,... | collective-permute-start | bytes 786440 | tf_op jit(solution)/shard_map/ppermute | solution.py:20
  39.9 0.3 shard_map.139
  40.2 6.7 %collective-permute-done.9.refs_2_ = bf16[512,256]{1,0:T(8,128)(2,1)S(1)} collective-permute-done((bf16[512,256]{1,0:T(8,128)(2,1)S(1)}, bf16[512,256]{1,0:T(8,128)(2,1)S(1)}, u32[]{:S(2)}, u32[]{:S(2)}) %collective-permute-start.9) | collective-permute-done | bytes 262176 | tf_op jit(solution)/shard_map/ppermute | solution.py:20
  46.9 0.6 shard_map.140.refs_0_
  47.5 0.1 collective-permute-start.10
  47.5 1.5 %collective-permute-done.10.refs_1_ = bf16[512,256]{1,0:T(8,128)(2,1)S(1)} collective-permute-done((bf16[512,256]{1,0:T(8,128)(2,1)S(1)}, bf16[512,256]{1,0:T(8,128)(2,1)S(1)}, u32[]{:S(2)}, u32[]{:S(2)}) %collective-permute-start.10) | collective-permute-done | bytes 262176 | tf_op jit(solution)/shard_map/ppermute | solution.py:20
  49.1 2.1 %shard_map.141 = (bf16[512,256]{1,0:T(8,128)(2,1)}, f32[512,256]{1,0:T(8,128)S(1)}, f32[272,256]{1,0:T(8,128)S(1)}, f32[272,256]{1,0:T(8,128)S(1)}) custom-call(s32[2]{0:T(128)S(1)} %pad_add_fusion.place, s32[4,128]{1,0:T(4,128)S(1)} %bitcast.14, bf16[512,256]{1,0:T(8,128)(2,1)S(1)} %get-tuple-element.46.refs_0_, ...), custom_call_target="tpu_custom_call" | custom-call | flops 469762048 | bytes 3442696 | tf_op jit(solution)/shard_map/pallas_call | solution.py:97
  51.2 0.1 collective-permute-start.20
  51.3 1.4 %collective-permute-start.11 = (bf16[512,256]{1,0:T(8,128)(2,1)S(1)}, bf16[512,256]{1,0:T(8,128)(2,1)S(1)}, u32[]{:S(2)}, u32[]{:S(2)}) collective-permute-start(bf16[512,256]{1,0:T(8,128)(2,1)S(1)} %shard_map.140.refs_0_), channel_id=1, source_target_pairs={{0,2},{1,3},{2,0},{3,1},{4,6},{5,7},{6,4},{7,5},{8,10},{9,11},{10,... | collective-permute-start | bytes 786440 | tf_op jit(solution)/shard_map/ppermute | solution.py:20
  52.7 7.2 %collective-permute-done.11.refs_2_ = bf16[512,256]{1,0:T(8,128)(2,1)S(1)} collective-permute-done((bf16[512,256]{1,0:T(8,128)(2,1)S(1)}, bf16[512,256]{1,0:T(8,128)(2,1)S(1)}, u32[]{:S(2)}, u32[]{:S(2)}) %collective-permute-start.11) | collective-permute-done | bytes 262176 | tf_op jit(solution)/shard_map/ppermute | solution.py:20
  60.0 1.7 %collective-permute-start.21 = (bf16[272,256]{1,0:T(8,128)(2,1)S(1)}, bf16[272,256]{1,0:T(8,128)(2,1)S(1)}, u32[]{:S(2)}, u32[]{:S(2)}) collective-permute-start(bf16[272,256]{1,0:T(8,128)(2,1)S(1)} %add_convert_fusion.7), channel_id=1, source_target_pairs={{0,16},{4,20},{8,24},{12,28},{16,0},{20,4},{24,8},{28,12},{1,17},{... | collective-permute-start | bytes 417800 | tf_op jit(solution)/shard_map/ppermute | solution.py:20
  61.7 2.3 %shard_map.142 = (bf16[512,256]{1,0:T(8,128)(2,1)S(1)}, bf16[512,256]{1,0:T(8,128)(2,1)S(1)}, bf16[512,256]{1,0:T(8,128)(2,1)S(1)}, bf16[512,256]{1,0:T(8,128)(2...) custom-call(s32[48]{0:T(128)S(1)} %bitcast.16, ...), custom_call_target="tpu_custom_call" | custom-call | flops 402653184 | bytes 4718792 | tf_op jit(solution)/shard_map/pallas_call | solution.py:97
  64.0 1.6 %collective-permute-start.13 = (bf16[512,256]{1,0:T(8,128)(2,1)S(1)}, bf16[512,256]{1,0:T(8,128)(2,1)S(1)}, u32[]{:S(2)}, u32[]{:S(2)}) collective-permute-start(bf16[512,256]{1,0:T(8,128)(2,1)S(1)} %get-tuple-element.57), channel_id=1, source_target_pairs={{0,4},{4,0},{8,12},{12,8},{16,20},{20,16},{24,28},{28,24},{1,5},{5... | collective-permute-start | bytes 786440 | tf_op jit(solution)/shard_map/ppermute | solution.py:20
  65.6 4.4 %collective-permute-done.21 = bf16[272,256]{1,0:T(8,128)(2,1)S(1)} collective-permute-done((bf16[272,256]{1,0:T(8,128)(2,1)S(1)}, bf16[272,256]{1,0:T(8,128)(2,1)S(1)}, u32[]{:S(2)}, u32[]{:S(2)}) %collective-permute-start.21) | collective-permute-done | bytes 139296 | tf_op jit(solution)/shard_map/ppermute | solution.py:20
  70.0 0.1 collective-permute-start.22
  70.1 1.4 %collective-permute-start.17 = (bf16[512,256]{1,0:T(8,128)(2,1)S(1)}, bf16[512,256]{1,0:T(8,128)(2,1)S(1)}, u32[]{:S(2)}, u32[]{:S(2)}) collective-permute-start(bf16[512,256]{1,0:T(8,128)(2,1)S(1)} %get-tuple-element.65), channel_id=1, source_target_pairs={{0,4},{4,0},{8,12},{12,8},{16,20},{20,16},{24,28},{28,24},{1,5},{5... | collective-permute-start | bytes 786440 | tf_op jit(solution)/shard_map/ppermute | solution.py:20
  71.5 1.9 %collective-permute-start.15 = (bf16[512,256]{1,0:T(8,128)(2,1)S(1)}, bf16[512,256]{1,0:T(8,128)(2,1)S(1)}, u32[]{:S(2)}, u32[]{:S(2)}) collective-permute-start(bf16[512,256]{1,0:T(8,128)(2,1)S(1)} %get-tuple-element.61), channel_id=1, source_target_pairs={{0,8},{4,12},{8,0},{12,4},{16,24},{20,28},{24,16},{28,20},{1,9},{5... | collective-permute-start | bytes 786440 | tf_op jit(solution)/shard_map/ppermute | solution.py:20
  73.5 3.2 %collective-permute-done.22 = bf16[272,256]{1,0:T(8,128)(2,1)S(1)} collective-permute-done((bf16[272,256]{1,0:T(8,128)(2,1)S(1)}, bf16[272,256]{1,0:T(8,128)(2,1)S(1)}, u32[]{:S(2)}, u32[]{:S(2)}) %collective-permute-start.22) | collective-permute-done | bytes 139296 | tf_op jit(solution)/shard_map/ppermute | solution.py:20
  76.7 1.4 %collective-permute-start.23 = (bf16[272,256]{1,0:T(8,128)(2,1)S(1)}, bf16[272,256]{1,0:T(8,128)(2,1)S(1)}, u32[]{:S(2)}, u32[]{:S(2)}) collective-permute-start(bf16[272,256]{1,0:T(8,128)(2,1)S(1)} %add_convert_fusion.5), channel_id=1, source_target_pairs={{0,2},{1,3},{2,0},{3,1},{4,6},{5,7},{6,4},{7,5},{8,10},{9,11},{10,... | collective-permute-start | bytes 417800 | tf_op jit(solution)/shard_map/ppermute | solution.py:20
  78.1 0.1 add_convert_fusion.2
  78.2 0.1 collective-permute-start.18
  78.3 2.7 %shard_map.143 = bf16[48,128,128]{2,1,0:T(8,128)(2,1)} custom-call(s32[48]{0:T(128)S(1)} %bitcast.17, s32[1]{0:T(128)} %bitcast.10.count, s32[2]{0:T(128)S(1)} %pad_add_fusion.place, bf16[512,256]{1,0:T(8,128)(2,1)S(1)} %shard_map.140.refs_0_, bf16[512,256]{1,0:T(8,128)(2,1)S(1)} %collective-permute-done.10.refs_1_, ...), custom_call_target="tpu_custom_call" | custom-call | flops 402653184 | bytes 4718796 | tf_op jit(solution)/shard_map/pallas_call | solution.py:97
  81.0 1.5 %collective-permute-start.14 = (bf16[512,256]{1,0:T(8,128)(2,1)S(1)}, bf16[512,256]{1,0:T(8,128)(2,1)S(1)}, u32[]{:S(2)}, u32[]{:S(2)}) collective-permute-start(bf16[512,256]{1,0:T(8,128)(2,1)S(1)} %get-tuple-element.60), channel_id=1, source_target_pairs={{0,4},{4,0},{8,12},{12,8},{16,20},{20,16},{24,28},{28,24},{1,5},{5... | collective-permute-start | bytes 786440 | tf_op jit(solution)/shard_map/ppermute | solution.py:20
  82.5 2.0 %collective-permute-start.16 = (bf16[512,256]{1,0:T(8,128)(2,1)S(1)}, bf16[512,256]{1,0:T(8,128)(2,1)S(1)}, u32[]{:S(2)}, u32[]{:S(2)}) collective-permute-start(bf16[512,256]{1,0:T(8,128)(2,1)S(1)} %get-tuple-element.62), channel_id=1, source_target_pairs={{0,12},{4,8},{8,4},{12,0},{16,28},{20,24},{24,20},{28,16},{1,13},{... | collective-permute-start | bytes 786440 | tf_op jit(solution)/shard_map/ppermute | solution.py:20
  84.5 1.6 %collective-permute-start.24 = (bf16[272,256]{1,0:T(8,128)(2,1)S(1)}, bf16[272,256]{1,0:T(8,128)(2,1)S(1)}, u32[]{:S(2)}, u32[]{:S(2)}) collective-permute-start(bf16[272,256]{1,0:T(8,128)(2,1)S(1)} %add_convert_fusion.4), channel_id=1, source_target_pairs={{0,4},{4,0},{8,12},{12,8},{16,20},{20,16},{24,28},{28,24},{1,5},{5... | collective-permute-start | bytes 417800 | tf_op jit(solution)/shard_map/ppermute | solution.py:20
  86.1 1.9 %collective-permute-done.18 = bf16[512,256]{1,0:T(8,128)(2,1)S(1)} collective-permute-done((bf16[512,256]{1,0:T(8,128)(2,1)S(1)}, bf16[512,256]{1,0:T(8,128)(2,1)S(1)}, u32[]{:S(2)}, u32[]{:S(2)}) %collective-permute-start.18) | collective-permute-done | bytes 262176 | tf_op jit(solution)/shard_map/ppermute | solution.py:20
  87.9 0.1 add_convert_fusion.1
  88.0 1.8 %collective-permute-start.19 = (bf16[512,256]{1,0:T(8,128)(2,1)S(1)}, bf16[512,256]{1,0:T(8,128)(2,1)S(1)}, u32[]{:S(2)}, u32[]{:S(2)}) collective-permute-start(bf16[512,256]{1,0:T(8,128)(2,1)S(1)} %add_convert_fusion.1), channel_id=1, source_target_pairs={{0,16},{4,20},{8,24},{12,28},{16,0},{20,4},{24,8},{28,12},{1,17},{... | collective-permute-start | bytes 786440 | tf_op jit(solution)/shard_map/ppermute | solution.py:20
  89.8 2.5 %collective-permute-done.24 = bf16[272,256]{1,0:T(8,128)(2,1)S(1)} collective-permute-done((bf16[272,256]{1,0:T(8,128)(2,1)S(1)}, bf16[272,256]{1,0:T(8,128)(2,1)S(1)}, u32[]{:S(2)}, u32[]{:S(2)}) %collective-permute-start.24) | collective-permute-done | bytes 139296 | tf_op jit(solution)/shard_map/ppermute | solution.py:20
  92.4 0.1 collective-permute-start.25
  92.5 4.6 %collective-permute-done.16 = bf16[512,256]{1,0:T(8,128)(2,1)S(1)} collective-permute-done((bf16[512,256]{1,0:T(8,128)(2,1)S(1)}, bf16[512,256]{1,0:T(8,128)(2,1)S(1)}, u32[]{:S(2)}, u32[]{:S(2)}) %collective-permute-start.16) | collective-permute-done | bytes 262176 | tf_op jit(solution)/shard_map/ppermute | solution.py:20
  97.1 0.2 select_add_fusion
  97.3 3.5 %collective-permute-done.19 = bf16[512,256]{1,0:T(8,128)(2,1)S(1)} collective-permute-done((bf16[512,256]{1,0:T(8,128)(2,1)S(1)}, bf16[512,256]{1,0:T(8,128)(2,1)S(1)}, u32[]{:S(2)}, u32[]{:S(2)}) %collective-permute-start.19) | collective-permute-done | bytes 262176 | tf_op jit(solution)/shard_map/ppermute | solution.py:20
  100.8 0.8 add_convert_fusion
  101.6 1.4 %shard_map.144 = (f32[256,256]{1,0:T(8,128)}, f32[256,256]{1,0:T(8,128)}, f32[1,256]{1,0:T(1,128)}) custom-call(s32[2]{0:T(128)S(1)} %pad_add_fusion.place, f32[272,256]{1,0:T(8,128)S(1)} %convert_add_fusion.same, f32[272,256]{1,0:T(8,128)S(1)} %collective-permute-done.25.other), custom_call_target="tpu_custom_call" | custom-call | bytes 1082376 | tf_op jit(solution)/shard_map/pallas_call | solution.py:97
  (29 shorter events, 0.2 us)
Async XLA Ops:
  0.6 1.0 copy-start
  1.6 0.7 copy-start.6
  2.5 16.1 %collective-permute-start = (bf16[512,256]{1,0:T(8,128)(2,1)S(1)}, bf16[512,256]{1,0:T(8,128)(2,1)S(1)}, u32[]{:S(2)}, u32[]{:S(2)}) collective-permute-start(bf16[512,256]{1,0:T(8,128)(2,1)S(1)} %shard_map.136.refs_0_), channel_id=1, source_target_pairs={{0,16},{4,20},{8,24},{12,28},{16,0},{20,4},{24,8},{28,12},{1,17},{... | collective-permute-start | bytes 786440 | tf_op jit(solution)/shard_map/ppermute | solution.py:20
  6.6 12.0 %collective-permute-start.1 = (bf16[512,256]{1,0:T(8,128)(2,1)S(1)}, bf16[512,256]{1,0:T(8,128)(2,1)S(1)}, u32[]{:S(2)}, u32[]{:S(2)}) collective-permute-start(bf16[512,256]{1,0:T(8,128)(2,1)S(1)} %shard_map.136.refs_0_), channel_id=1, source_target_pairs={{0,4},{4,0},{8,12},{12,8},{16,20},{20,16},{24,28},{28,24},{1,5},{5... | collective-permute-start | bytes 786440 | tf_op jit(solution)/shard_map/ppermute | solution.py:20
  8.2 15.0 %collective-permute-start.4 = (bf16[512,256]{1,0:T(8,128)(2,1)S(1)}, bf16[512,256]{1,0:T(8,128)(2,1)S(1)}, u32[]{:S(2)}, u32[]{:S(2)}) collective-permute-start(bf16[512,256]{1,0:T(8,128)(2,1)S(1)} %shard_map.136.refs_0_), channel_id=1, source_target_pairs={{0,12},{4,8},{8,4},{12,0},{16,28},{20,24},{24,20},{28,16},{1,13},{... | collective-permute-start | bytes 786440 | tf_op jit(solution)/shard_map/ppermute | solution.py:20
  18.7 10.2 %collective-permute-start.3 = (bf16[512,256]{1,0:T(8,128)(2,1)S(1)}, bf16[512,256]{1,0:T(8,128)(2,1)S(1)}, u32[]{:S(2)}, u32[]{:S(2)}) collective-permute-start(bf16[512,256]{1,0:T(8,128)(2,1)S(1)} %collective-permute-done.refs_4_), channel_id=1, source_target_pairs={{0,8},{4,12},{8,0},{12,4},{16,24},{20,28},{24,16},{28,20},{1,9},{5... | collective-permute-start | bytes 786440 | tf_op jit(solution)/shard_map/ppermute | solution.py:20
  21.6 11.3 %collective-permute-start.2 = (bf16[512,256]{1,0:T(8,128)(2,1)S(1)}, bf16[512,256]{1,0:T(8,128)(2,1)S(1)}, u32[]{:S(2)}, u32[]{:S(2)}) collective-permute-start(bf16[512,256]{1,0:T(8,128)(2,1)S(1)} %shard_map.136.refs_0_), channel_id=1, source_target_pairs={{0,8},{4,12},{8,0},{12,4},{16,24},{20,28},{24,16},{28,20},{1,9},{5... | collective-permute-start | bytes 786440 | tf_op jit(solution)/shard_map/ppermute | solution.py:20
  21.6 11.3 %collective-permute-start.5 = (bf16[512,256]{1,0:T(8,128)(2,1)S(1)}, bf16[512,256]{1,0:T(8,128)(2,1)S(1)}, u32[]{:S(2)}, u32[]{:S(2)}) collective-permute-start(bf16[512,256]{1,0:T(8,128)(2,1)S(1)} %collective-permute-done.refs_4_), channel_id=1, source_target_pairs={{0,4},{4,0},{8,12},{12,8},{16,20},{20,16},{24,28},{28,24},{1,5},{5... | collective-permute-start | bytes 786440 | tf_op jit(solution)/shard_map/ppermute | solution.py:20
  28.8 6.4 %collective-permute-start.6 = (bf16[512,256]{1,0:T(8,128)(2,1)S(1)}, bf16[512,256]{1,0:T(8,128)(2,1)S(1)}, u32[]{:S(2)}, u32[]{:S(2)}) collective-permute-start(bf16[512,256]{1,0:T(8,128)(2,1)S(1)} %collective-permute-done.3.refs_6_), channel_id=1, source_target_pairs={{0,4},{4,0},{8,12},{12,8},{16,20},{20,16},{24,28},{28,24},{1,5},{5... | collective-permute-start | bytes 786440 | tf_op jit(solution)/shard_map/ppermute | solution.py:20
  30.8 1.4 %copy-start.2 = (bf16[1,1,48,128,128]{4,3,2,1,0:T(8,128)(2,1)S(1)}, bf16[1,1,48,128,128]{4,3,2,1,0:T(8,128)(2,1)}, u32[]{:S(2)}) copy-start(bf16[1,1,48,128,128]{4,3,2,1,0:T(8,128)(2,1)} %param.16) | copy-start | bytes 4718596
  32.2 2.9 %copy-start.8 = (s32[1,1,48]{2,1,0:T(1,128)S(1)}, s32[1,1,48]{2,1,0:T(1,128)}, u32[]{:S(2)}) copy-start(s32[1,1,48]{2,1,0:T(1,128)} %param.14) | copy-start | bytes 580
  35.2 4.7 %copy-start.1 = (bf16[512,256]{1,0:T(8,128)(2,1)S(1)}, bf16[512,256]{1,0:T(8,128)(2,1)}, u32[]{:S(2)}) copy-start(bf16[512,256]{1,0:T(8,128)(2,1)} %refs_6_.1) | copy-start | bytes 786436
  35.2 4.7 %copy-start.3 = (bf16[256,256]{1,0:T(8,128)(2,1)S(1)}, bf16[256,256]{1,0:T(8,128)(2,1)}, u32[]{:S(2)}) copy-start(bf16[256,256]{1,0:T(8,128)(2,1)} %refs_7_.1) | copy-start | bytes 393220
  35.2 4.7 %copy-start.4 = (bf16[512,256]{1,0:T(8,128)(2,1)S(1)}, bf16[512,256]{1,0:T(8,128)(2,1)}, u32[]{:S(2)}) copy-start(bf16[512,256]{1,0:T(8,128)(2,1)} %grad_out.1) | copy-start | bytes 786436
  35.2 4.6 %copy-start.5 = (bf16[256,256]{1,0:T(8,128)(2,1)S(1)}, bf16[256,256]{1,0:T(8,128)(2,1)}, u32[]{:S(2)}) copy-start(bf16[256,256]{1,0:T(8,128)(2,1)} %w_msg.1) | copy-start | bytes 393220
  35.2 4.6 %copy-start.7 = (s32[512]{0:T(512)S(1)}, s32[512]{0:T(512)}, u32[]{:S(2)}) copy-start(s32[512]{0:T(512)} %param.13) | copy-start | bytes 6148
  35.2 4.6 %copy-start.9 = (f32[256]{0:T(256)S(1)}, f32[256]{0:T(256)}, u32[]{:S(2)}) copy-start(f32[256]{0:T(256)} %param.12) | copy-start | bytes 3076
  36.8 1.6 %collective-permute-start.8 = (bf16[512,256]{1,0:T(8,128)(2,1)S(1)}, bf16[512,256]{1,0:T(8,128)(2,1)S(1)}, u32[]{:S(2)}, u32[]{:S(2)}) collective-permute-start(bf16[512,256]{1,0:T(8,128)(2,1)S(1)} %get-tuple-element.49), channel_id=1, source_target_pairs={{0,1},{1,0},{2,3},{3,2},{4,5},{5,4},{6,7},{7,6},{8,9},{9,8},{10,11... | collective-permute-start | bytes 786440 | tf_op jit(solution)/shard_map/ppermute | solution.py:20
  36.8 3.3 %collective-permute-start.7 = (bf16[512,256]{1,0:T(8,128)(2,1)S(1)}, bf16[512,256]{1,0:T(8,128)(2,1)S(1)}, u32[]{:S(2)}, u32[]{:S(2)}) collective-permute-start(bf16[512,256]{1,0:T(8,128)(2,1)S(1)} %get-tuple-element.47), channel_id=1, source_target_pairs={{0,1},{1,0},{2,3},{3,2},{4,5},{5,4},{6,7},{7,6},{8,9},{9,8},{10,11... | collective-permute-start | bytes 786440 | tf_op jit(solution)/shard_map/ppermute | solution.py:20
  38.4 8.4 %collective-permute-start.9 = (bf16[512,256]{1,0:T(8,128)(2,1)S(1)}, bf16[512,256]{1,0:T(8,128)(2,1)S(1)}, u32[]{:S(2)}, u32[]{:S(2)}) collective-permute-start(bf16[512,256]{1,0:T(8,128)(2,1)S(1)} %add_convert_fusion.3), channel_id=1, source_target_pairs={{0,2},{1,3},{2,0},{3,1},{4,6},{5,7},{6,4},{7,5},{8,10},{9,11},{10,... | collective-permute-start | bytes 786440 | tf_op jit(solution)/shard_map/ppermute | solution.py:20
  47.5 1.6 %collective-permute-start.10 = (bf16[512,256]{1,0:T(8,128)(2,1)S(1)}, bf16[512,256]{1,0:T(8,128)(2,1)S(1)}, u32[]{:S(2)}, u32[]{:S(2)}) collective-permute-start(bf16[512,256]{1,0:T(8,128)(2,1)S(1)} %shard_map.140.refs_0_), channel_id=1, source_target_pairs={{0,1},{1,0},{2,3},{3,2},{4,5},{5,4},{6,7},{7,6},{8,9},{9,8},{10,11... | collective-permute-start | bytes 786440 | tf_op jit(solution)/shard_map/ppermute | solution.py:20
  51.2 8.7 %collective-permute-start.20 = (f32[272,256]{1,0:T(8,128)S(1)}, f32[272,256]{1,0:T(8,128)S(1)}, u32[]{:S(2)}, u32[]{:S(2)}) collective-permute-start(f32[272,256]{1,0:T(8,128)S(1)} %get-tuple-element.72), channel_id=1, source_target_pairs={{0,1},{1,0},{2,3},{3,2},{4,5},{5,4},{6,7},{7,6},{8,9},{9,8},{10,11... | collective-permute-start | bytes 835592 | tf_op jit(solution)/shard_map/ppermute | solution.py:20
  51.3 8.6 %collective-permute-start.11 = (bf16[512,256]{1,0:T(8,128)(2,1)S(1)}, bf16[512,256]{1,0:T(8,128)(2,1)S(1)}, u32[]{:S(2)}, u32[]{:S(2)}) collective-permute-start(bf16[512,256]{1,0:T(8,128)(2,1)S(1)} %shard_map.140.refs_0_), channel_id=1, source_target_pairs={{0,2},{1,3},{2,0},{3,1},{4,6},{5,7},{6,4},{7,5},{8,10},{9,11},{10,... | collective-permute-start | bytes 786440 | tf_op jit(solution)/shard_map/ppermute | solution.py:20
  59.9 1.7 %collective-permute-start.12 = (bf16[512,256]{1,0:T(8,128)(2,1)S(1)}, bf16[512,256]{1,0:T(8,128)(2,1)S(1)}, u32[]{:S(2)}, u32[]{:S(2)}) collective-permute-start(bf16[512,256]{1,0:T(8,128)(2,1)S(1)} %collective-permute-done.11.refs_2_), channel_id=1, source_target_pairs={{0,1},{1,0},{2,3},{3,2},{4,5},{5,4},{6,7},{7,6},{8,9},{9,8},{10,11... | collective-permute-start | bytes 786440 | tf_op jit(solution)/shard_map/ppermute | solution.py:20
  60.0 10.0 %collective-permute-start.21 = (bf16[272,256]{1,0:T(8,128)(2,1)S(1)}, bf16[272,256]{1,0:T(8,128)(2,1)S(1)}, u32[]{:S(2)}, u32[]{:S(2)}) collective-permute-start(bf16[272,256]{1,0:T(8,128)(2,1)S(1)} %add_convert_fusion.7), channel_id=1, source_target_pairs={{0,16},{4,20},{8,24},{12,28},{16,0},{20,4},{24,8},{28,12},{1,17},{... | collective-permute-start | bytes 417800 | tf_op jit(solution)/shard_map/ppermute | solution.py:20
  64.0 9.5 %collective-permute-start.13 = (bf16[512,256]{1,0:T(8,128)(2,1)S(1)}, bf16[512,256]{1,0:T(8,128)(2,1)S(1)}, u32[]{:S(2)}, u32[]{:S(2)}) collective-permute-start(bf16[512,256]{1,0:T(8,128)(2,1)S(1)} %get-tuple-element.57), channel_id=1, source_target_pairs={{0,4},{4,0},{8,12},{12,8},{16,20},{20,16},{24,28},{28,24},{1,5},{5... | collective-permute-start | bytes 786440 | tf_op jit(solution)/shard_map/ppermute | solution.py:20
  70.0 6.6 %collective-permute-start.22 = (bf16[272,256]{1,0:T(8,128)(2,1)S(1)}, bf16[272,256]{1,0:T(8,128)(2,1)S(1)}, u32[]{:S(2)}, u32[]{:S(2)}) collective-permute-start(bf16[272,256]{1,0:T(8,128)(2,1)S(1)} %add_convert_fusion.6), channel_id=1, source_target_pairs={{0,8},{4,12},{8,0},{12,4},{16,24},{20,28},{24,16},{28,20},{1,9},{5... | collective-permute-start | bytes 417800 | tf_op jit(solution)/shard_map/ppermute | solution.py:20
  70.1 14.4 %collective-permute-start.17 = (bf16[512,256]{1,0:T(8,128)(2,1)S(1)}, bf16[512,256]{1,0:T(8,128)(2,1)S(1)}, u32[]{:S(2)}, u32[]{:S(2)}) collective-permute-start(bf16[512,256]{1,0:T(8,128)(2,1)S(1)} %get-tuple-element.65), channel_id=1, source_target_pairs={{0,4},{4,0},{8,12},{12,8},{16,20},{20,16},{24,28},{28,24},{1,5},{5... | collective-permute-start | bytes 786440 | tf_op jit(solution)/shard_map/ppermute | solution.py:20
  71.5 20.9 %collective-permute-start.15 = (bf16[512,256]{1,0:T(8,128)(2,1)S(1)}, bf16[512,256]{1,0:T(8,128)(2,1)S(1)}, u32[]{:S(2)}, u32[]{:S(2)}) collective-permute-start(bf16[512,256]{1,0:T(8,128)(2,1)S(1)} %get-tuple-element.61), channel_id=1, source_target_pairs={{0,8},{4,12},{8,0},{12,4},{16,24},{20,28},{24,16},{28,20},{1,9},{5... | collective-permute-start | bytes 786440 | tf_op jit(solution)/shard_map/ppermute | solution.py:20
  76.7 5.8 %collective-permute-start.23 = (bf16[272,256]{1,0:T(8,128)(2,1)S(1)}, bf16[272,256]{1,0:T(8,128)(2,1)S(1)}, u32[]{:S(2)}, u32[]{:S(2)}) collective-permute-start(bf16[272,256]{1,0:T(8,128)(2,1)S(1)} %add_convert_fusion.5), channel_id=1, source_target_pairs={{0,2},{1,3},{2,0},{3,1},{4,6},{5,7},{6,4},{7,5},{8,10},{9,11},{10,... | collective-permute-start | bytes 417800 | tf_op jit(solution)/shard_map/ppermute | solution.py:20
  78.2 9.7 %collective-permute-start.18 = (bf16[512,256]{1,0:T(8,128)(2,1)S(1)}, bf16[512,256]{1,0:T(8,128)(2,1)S(1)}, u32[]{:S(2)}, u32[]{:S(2)}) collective-permute-start(bf16[512,256]{1,0:T(8,128)(2,1)S(1)} %add_convert_fusion.2), channel_id=1, source_target_pairs={{0,8},{4,12},{8,0},{12,4},{16,24},{20,28},{24,16},{28,20},{1,9},{5... | collective-permute-start | bytes 786440 | tf_op jit(solution)/shard_map/ppermute | solution.py:20
  81.0 11.5 %collective-permute-start.14 = (bf16[512,256]{1,0:T(8,128)(2,1)S(1)}, bf16[512,256]{1,0:T(8,128)(2,1)S(1)}, u32[]{:S(2)}, u32[]{:S(2)}) collective-permute-start(bf16[512,256]{1,0:T(8,128)(2,1)S(1)} %get-tuple-element.60), channel_id=1, source_target_pairs={{0,4},{4,0},{8,12},{12,8},{16,20},{20,16},{24,28},{28,24},{1,5},{5... | collective-permute-start | bytes 786440 | tf_op jit(solution)/shard_map/ppermute | solution.py:20
  82.5 14.6 %collective-permute-start.16 = (bf16[512,256]{1,0:T(8,128)(2,1)S(1)}, bf16[512,256]{1,0:T(8,128)(2,1)S(1)}, u32[]{:S(2)}, u32[]{:S(2)}) collective-permute-start(bf16[512,256]{1,0:T(8,128)(2,1)S(1)} %get-tuple-element.62), channel_id=1, source_target_pairs={{0,12},{4,8},{8,4},{12,0},{16,28},{20,24},{24,20},{28,16},{1,13},{... | collective-permute-start | bytes 786440 | tf_op jit(solution)/shard_map/ppermute | solution.py:20
  84.5 7.8 %collective-permute-start.24 = (bf16[272,256]{1,0:T(8,128)(2,1)S(1)}, bf16[272,256]{1,0:T(8,128)(2,1)S(1)}, u32[]{:S(2)}, u32[]{:S(2)}) collective-permute-start(bf16[272,256]{1,0:T(8,128)(2,1)S(1)} %add_convert_fusion.4), channel_id=1, source_target_pairs={{0,4},{4,0},{8,12},{12,8},{16,20},{20,16},{24,28},{28,24},{1,5},{5... | collective-permute-start | bytes 417800 | tf_op jit(solution)/shard_map/ppermute | solution.py:20
  88.0 12.8 %collective-permute-start.19 = (bf16[512,256]{1,0:T(8,128)(2,1)S(1)}, bf16[512,256]{1,0:T(8,128)(2,1)S(1)}, u32[]{:S(2)}, u32[]{:S(2)}) collective-permute-start(bf16[512,256]{1,0:T(8,128)(2,1)S(1)} %add_convert_fusion.1), channel_id=1, source_target_pairs={{0,16},{4,20},{8,24},{12,28},{16,0},{20,4},{24,8},{28,12},{1,17},{... | collective-permute-start | bytes 786440 | tf_op jit(solution)/shard_map/ppermute | solution.py:20
  92.4 9.3 %collective-permute-start.25 = (f32[272,256]{1,0:T(8,128)S(1)}, f32[272,256]{1,0:T(8,128)S(1)}, u32[]{:S(2)}, u32[]{:S(2)}) collective-permute-start(f32[272,256]{1,0:T(8,128)S(1)} %convert_add_fusion.same), channel_id=1, source_target_pairs={{0,1},{1,0},{2,3},{3,2},{4,5},{5,4},{6,7},{7,6},{8,9},{9,8},{10,11... | collective-permute-start | bytes 835592 | tf_op jit(solution)/shard_map/ppermute | solution.py:20

commit v3 on v2

--- a/solution.py
+++ b/solution.py
@@ -27,6 +27,18 @@
 
 def tie(*values):
     return lax.optimization_barrier(values)
+
+
+def add_over(value, *bits):
+    n_row, n_col = lax.axis_size("row"), lax.axis_size("col")
+    sent = value.astype(BF16)
+    moves = list(bits) if len(bits) == 1 else [*bits, (bits[0][0] ^ bits[1][0], bits[0][1] ^ bits[1][1])]
+    got = []
+    for row, col in moves:
+        pairs = [(i, i ^ (row * n_col + col)) for i in range(n_row * n_col)]
+        got.append(lax.ppermute(sent, ("row", "col"), pairs).astype(F32))
+    sent = sent.astype(F32)
+    return sent + got[0] if len(got) == 1 else (sent + got[0]) + (got[1] + got[2])
 
 
 def gather_by_offset(own, axis):
@@ -75,15 +87,14 @@
 def scatter_rows(parts, axis):
     if lax.axis_size(axis) != 8:
         return scatter_by_offset(parts, axis)
-    got7 = exchange(parts[7], axis, 1)
-    got5 = exchange(parts[5], axis, 1)
-    got2 = exchange(parts[2], axis, 2)
-    got7, part1, part3 = tie(got7, parts[1], parts[3])
-    got6 = exchange(add_rounded(parts[6], got7), axis, 2)
+    got7, got6, got5 = (exchange(parts[4 + bit], axis, bit) for bit in (3, 2, 1))
+    got3 = exchange(parts[3], axis, 1)
+    far = add_rounded(parts[4], got5, got6, got7)
+    got4 = exchange(far, axis, 4)
+    _, part1 = tie(far, parts[1])
     got1 = exchange(part1, axis, 1)
-    got3 = exchange(part3, axis, 3)
-    got4 = exchange(add_rounded(parts[4], got5, got6), axis, 4)
-    return [parts[0], got1, got2, got3, got4]
+    got2 = exchange(add_rounded(parts[2], got3), axis, 2)
+    return [parts[0], got1, got2, got4]
 
 
 def nbytes(shape, dtype):
@@ -165,7 +176,7 @@
         out[rows, :] = picked.astype(BF16)
 
 
-def prepare_body(size, mask, feats, w_msg, w_self, bias, grad_out, base, grad_live, w_out):
+def prepare_body(size, mask, feats, w_msg, w_self, bias, grad_out, base, grad_live, w_out, feats_out):
     for k in range(mask.shape[0]):
         rows = pl.ds(k * size, size)
         select = select_rows(mask, k, size)
@@ -174,6 +185,7 @@
         picked = jnp.dot(select, grad_out[rows, :], preferred_element_type=F32)
         grad_live[rows, :] = picked.astype(BF16)
     w_out[...] = w_msg[...]
+    feats_out[...] = feats[...]
 
 
 def spmm_body(n_row, n_col, size, depth, cols, place, edges, *refs):
@@ -253,26 +265,29 @@
 
 def act_body(size, n_terms, *refs):
     terms = refs[:n_terms]
-    base, grad_live, w_msg, grad_w = refs[n_terms:]
+    base, grad_live, w_msg, grad_w, grad_pre, summed = refs[n_terms:]
     for k in range(base.shape[0] // size):
-        grad = activate(size, k, terms, base, grad_live, w_msg)[3]
-        grad_w[pl.ds(k * size, size), :] = nt(grad, w_msg[...]).astype(BF16)
-
-
-def weight_body(size, n_terms, factor, place, mask, *refs):
-    terms = refs[:n_terms]
-    base, grad_live, w_msg, feats, w_self, hidden, own_part, same, other = refs[n_terms:-3]
-    summed, grad_pre, stack = refs[-3:]
-    width = feats.shape[1]
-    for k in range(feats.shape[0] // size):
         rows = pl.ds(k * size, size)
-        high, pre, sig, grad = activate(size, k, terms, base, grad_live, w_msg)
+        high, _, _, grad = activate(size, k, terms, base, grad_live, w_msg)
         summed[rows, :] = high
         grad_pre[rows, :] = grad
+        grad_w[rows, :] = nt(grad, w_msg[...]).astype(BF16)
+
+
+def rest_body(size, n_terms, mask, *refs):
+    terms = refs[:n_terms]
+    base, grad_live, w_msg, w_self, hidden, own_part = refs[n_terms:]
+    for k in range(base.shape[0] // size):
+        rows = pl.ds(k * size, size)
+        _, pre, sig, grad = activate(size, k, terms, base, grad_live, w_msg)
         value = (pre * sig).astype(BF16)
         picked = jnp.dot(select_rows(mask, k, size), value, preferred_element_type=F32)
         hidden[rows, :] = picked.astype(BF16)
         own_part[rows, :] = nt(grad, w_self[...])
+
+
+def weight_body(factor, place, feats, grad_pre, summed, same, other, stack):
+    width = feats.shape[1]
     grad = grad_pre[...]
     stack[pl.ds(0, width), :] = tn(summed[...], grad) * factor
     stack[pl.ds(width, width), :] = tn(feats[...], grad) * factor
@@ -294,6 +309,13 @@
     w_msg[...] = stack[pl.ds(0, width), :]
     w_self[...] = stack[pl.ds(width, width), :]
     bias[...] = stack[pl.ds(2 * width, 1), :]
+
+
+def finish_body(size, mask, early, last, out):
+    for k in range(mask.shape[0]):
+        rows = pl.ds(k * size, size)
+        picked = jnp.dot(select_rows(mask, k, size), last[rows, :], preferred_element_type=F32)
+        out[rows, :] = (early[rows, :] + picked).astype(BF16)
 
 
 def per_device(feats, w_msg, w_self, bias, hit_mask, block_cols, block_count, edge_vals, grad_out):
@@ -336,11 +358,11 @@
         0,
         (late_count, edges),
     )
-    base, grad_live, w_here = kernel_call(
+    base, grad_live, w_here, feats_here = kernel_call(
         functools.partial(prepare_body, size),
-        [wide, block, jax.ShapeDtypeStruct(w_msg.shape, BF16)],
+        [wide, block, jax.ShapeDtypeStruct(w_msg.shape, BF16), block],
         [VMEM] * 6,
-        [VMEM] * 3,
+        [VMEM] * 4,
         [],
         2 * own_rows * width * (width + size),
         (mask, feats, w_msg, w_self, late_bias[None, :], grad_out),
@@ -357,11 +379,11 @@
     )
     terms = scatter_by_offset(partial, "col")
 
-    grad_w = kernel_call(
+    grad_w, grad_pre, summed = kernel_call(
         functools.partial(act_body, size, len(terms)),
-        block,
+        [block] * 3,
         [VMEM] * (len(terms) + 3),
-        VMEM,
+        [VMEM] * 3,
         [],
         6 * own_rows * width * width,
         (*terms, base, grad_live, w_here),
@@ -384,26 +406,36 @@
     rows = 2 * width + 32
     half = jax.ShapeDtypeStruct((rows // 2, width), F32)
     factor = 1.0 / math.sqrt(own_rows * n_row * n_col)
-    late_live, _ = tie(grad_live, grads[1])
-    hidden, own_part, same, other = kernel_call(
-        functools.partial(weight_body, size, len(terms), factor),
-        [block, wide, half, half],
-        [SMEM] + [VMEM] * (len(terms) + 6),
-        [VMEM] * 4,
-        [
-            pltpu.VMEM((own_rows, width), BF16),
-            pltpu.VMEM((own_rows, width), BF16),
-            pltpu.VMEM((rows, width), F32),
-        ],
-        14 * own_rows * width * width,
-        (place, mask, *terms, base, late_live, w_here, feats, w_self),
-    )
+    same, other = kernel_call(
+        functools.partial(weight_body, factor),
+        [half, half],
+        [SMEM] + [VMEM] * 3,
+        [VMEM] * 2,
+        [pltpu.VMEM((rows, width), F32)],
+        4 * own_rows * width * width,
+        (place, feats_here, grad_pre, summed),
+    )
+    late_live, _ = tie(grad_live, pieces[0])
+    hidden, own_part = kernel_call(
+        functools.partial(rest_body, size, len(terms)),
+        [block, wide],
+        [VMEM] * (len(terms) + 5),
+        [VMEM] * 2,
+        [],
+        8 * own_rows * width * width,
+        (mask, *terms, base, late_live, w_here, w_self),
+    )
+    back = scatter_rows(pieces, "row")
     total = same + exchange(other, "col", 1)
-    steps = [("row", bit) for bit in reversed(bits_of(n_row))]
-    steps = steps[:-1] + [("col", bit) for bit in bits_of(n_col)[1:]] + steps[-1:]
-    for axis, bit in steps:
-        sent = total.astype(BF16)
-        total = sent.astype(F32) + exchange(sent, axis, bit).astype(F32)
+    row_bits, col_bits = bits_of(n_row), bits_of(n_col)[1:]
+    total = add_over(total, (row_bits.pop(min(1, len(row_bits) - 1)), 0))
+    total, _ = tie(total, pieces[0])
+    for bit in reversed(row_bits[1:]):
+        total = add_over(total, (bit, 0))
+    for bit in col_bits[:-1]:
+        total = add_over(total, (0, bit))
+    total = add_over(total, (row_bits[0], 0), (0, col_bits[-1]))
+    total, *_ = tie(total, *back[2:])
     square = jax.ShapeDtypeStruct((width, width), F32)
     msg_grad, self_grad, bias_grad = kernel_call(
         join_body,
@@ -425,11 +457,18 @@
         (cols, count, place, *grads, together),
     )
 
-    back = scatter_rows(pieces, "row")
     column = (hit_mask != 0)[:, None]
     early = jnp.where(column, sum(term.astype(F32) for term in back[:-1]), 0.0) + own_part
     early, last = tie(early, back[-1])
-    grad_feats = (early + jnp.where(column, last.astype(F32), 0.0)).astype(BF16)
+    grad_feats = kernel_call(
+        functools.partial(finish_body, size),
+        block,
+        [VMEM] * 3,
+        VMEM,
+        [],
+        2 * own_rows * size * width,
+        (mask, early, last),
+    )
     return hidden, grad_feats, edge_grad[None, None], msg_grad, self_grad, bias_grad[0]
 
 

time: 103 us -> 99.2 us (0.963)
  waiting for transfers between devices: 53.5 us -> 50.7 us
  starting transfers between devices: 31.6 us -> 29.3 us
  Pallas kernels: 11.8 us -> 13.2 us
    ppermute x26 -> x22, waiting for transfers between devices: 53.5 us -> 41.9 us  [exchange(): return lax.ppermute(value, axis, [(i, i ^ bit) for i in range(size)])]
    ppermute x26 -> x22, starting transfers between devices: 31.6 us -> 22.6 us  [exchange(): return lax.ppermute(value, axis, [(i, i ^ bit) for i in range(size)])]
    ppermute x0 -> x5, waiting for transfers between devices: none -> 8.85 us  [add_over(): got.append(lax.ppermute(sent, ('row', 'col'), pairs).astype(F32))]
    ppermute x0 -> x5, starting transfers between devices: none -> 6.7 us  [add_over(): got.append(lax.ppermute(sent, ('row', 'col'), pairs).astype(F32))]
    pallas_call x9 -> x11, Pallas kernels: 11.8 us -> 13.2 us  [kernel_call(): pl.pallas_call(body, out_shape=outs, in_specs=in_specs, out_specs=out_spe...]
  transfers between devices with their start and end apart: 26 -> 27, of which waited for: 13 -> 13; matrix products, arithmetic and copies ran while one was open for 2% -> 1% of each run, Pallas kernels for 6% -> 6%
where the time goes in v3:
time: 99.2 us; the launch traced here: 98.5 us
  waiting for transfers between devices  50.7 us (51%)
  starting transfers between devices  29.3 us (30%)
  Pallas kernels  13.2 us (13%)
  local copies, waits for them, and re-layouts  3.06 us (3%)
  between operations  1.5 us (2%)
    ppermute x22, waiting for transfers between devices, exchange(): return lax.ppermute(value, axis, [(i, i ^ bit) for i in range(size)])  41.9 us
    ppermute x22, starting transfers between devices, exchange(): return lax.ppermute(value, axis, [(i, i ^ bit) for i in range(size)])  22.6 us
    pallas_call x11, Pallas kernels, kernel_call(): pl.pallas_call(body, out_shape=outs, in_specs=in_specs, out_specs=out_spe...  13.2 us
    ppermute x5, waiting for transfers between devices, add_over(): got.append(lax.ppermute(sent, ('row', 'col'), pairs).astype(F32))  8.85 us
    ppermute x5, starting transfers between devices, add_over(): got.append(lax.ppermute(sent, ('row', 'col'), pairs).astype(F32))  6.7 us
    unnamed x20, local copies, waits for them, and re-layouts  3.06 us
  transfers between devices with their start and end apart: 27, of which 13 were waited for; matrix products, arithmetic and copies ran while one was open for 1% of the time, Pallas kernels for 6%

profile of v3, /device:TPU:0, one launch (start us, length us, event | category | flops | bytes accessed | tf_op | source)
XLA Modules:
  0.0 98.5 jit_solution(13712199849823182071)
XLA Ops:
  0.6 0.0 copy-start.1
  0.6 0.9 copy-done.1
  1.6 0.7 copy-done.6
  2.3 0.3 shard_map.136.refs_0_
  2.5 3.0 %collective-permute-start.1 = (bf16[512,256]{1,0:T(8,128)(2,1)S(1)}, bf16[512,256]{1,0:T(8,128)(2,1)S(1)}, u32[]{:S(2)}, u32[]{:S(2)}) collective-permute-start(bf16[512,256]{1,0:T(8,128)(2,1)S(1)} %shard_map.136.refs_0_), channel_id=1, source_target_pairs={{0,4},{4,0},{8,12},{12,8},{16,20},{20,16},{24,28},{28,24},{1,5},{5... | collective-permute-start | bytes 786440 | tf_op jit(solution)/shard_map/ppermute | solution.py:20
  5.6 2.6 %collective-permute-start = (bf16[512,256]{1,0:T(8,128)(2,1)S(1)}, bf16[512,256]{1,0:T(8,128)(2,1)S(1)}, u32[]{:S(2)}, u32[]{:S(2)}) collective-permute-start(bf16[512,256]{1,0:T(8,128)(2,1)S(1)} %shard_map.136.refs_0_), channel_id=1, source_target_pairs={{0,16},{4,20},{8,24},{12,28},{16,0},{20,4},{24,8},{28,12},{1,17},{... | collective-permute-start | bytes 786440 | tf_op jit(solution)/shard_map/ppermute | solution.py:20
  8.2 1.5 %collective-permute-start.4 = (bf16[512,256]{1,0:T(8,128)(2,1)S(1)}, bf16[512,256]{1,0:T(8,128)(2,1)S(1)}, u32[]{:S(2)}, u32[]{:S(2)}) collective-permute-start(bf16[512,256]{1,0:T(8,128)(2,1)S(1)} %shard_map.136.refs_0_), channel_id=1, source_target_pairs={{0,12},{4,8},{8,4},{12,0},{16,28},{20,24},{24,20},{28,16},{1,13},{... | collective-permute-start | bytes 786440 | tf_op jit(solution)/shard_map/ppermute | solution.py:20
  9.7 6.9 %collective-permute-done.1.refs_1_ = bf16[512,256]{1,0:T(8,128)(2,1)S(1)} collective-permute-done((bf16[512,256]{1,0:T(8,128)(2,1)S(1)}, bf16[512,256]{1,0:T(8,128)(2,1)S(1)}, u32[]{:S(2)}, u32[]{:S(2)}) %collective-permute-start.1) | collective-permute-done | bytes 262176 | tf_op jit(solution)/shard_map/ppermute | solution.py:20
  16.6 3.4 %collective-permute-done.refs_4_ = bf16[512,256]{1,0:T(8,128)(2,1)S(1)} collective-permute-done((bf16[512,256]{1,0:T(8,128)(2,1)S(1)}, bf16[512,256]{1,0:T(8,128)(2,1)S(1)}, u32[]{:S(2)}, u32[]{:S(2)}) %collective-permute-start) | collective-permute-done | bytes 262176 | tf_op jit(solution)/shard_map/ppermute | solution.py:20
  19.9 0.6 collective-permute-start.3
  20.5 1.5 %collective-permute-start.2 = (bf16[512,256]{1,0:T(8,128)(2,1)S(1)}, bf16[512,256]{1,0:T(8,128)(2,1)S(1)}, u32[]{:S(2)}, u32[]{:S(2)}) collective-permute-start(bf16[512,256]{1,0:T(8,128)(2,1)S(1)} %shard_map.136.refs_0_), channel_id=1, source_target_pairs={{0,8},{4,12},{8,0},{12,4},{16,24},{20,28},{24,16},{28,20},{1,9},{5... | collective-permute-start | bytes 786440 | tf_op jit(solution)/shard_map/ppermute | solution.py:20
  22.0 0.5 collective-permute-start.5
  22.4 0.0 collective-permute-done.4.refs_3_
  22.4 6.8 %collective-permute-done.3.refs_6_ = bf16[512,256]{1,0:T(8,128)(2,1)S(1)} collective-permute-done((bf16[512,256]{1,0:T(8,128)(2,1)S(1)}, bf16[512,256]{1,0:T(8,128)(2,1)S(1)}, u32[]{:S(2)}, u32[]{:S(2)}) %collective-permute-start.3) | collective-permute-done | bytes 262176 | tf_op jit(solution)/shard_map/ppermute | solution.py:20
  29.2 0.5 collective-permute-start.6
  30.3 0.0 copy-start
  30.3 1.4 %copy-done = bf16[1,1,48,128,128]{4,3,2,1,0:T(8,128)(2,1)S(1)} copy-done((bf16[1,1,48,128,128]{4,3,2,1,0:T(8,128)(2,1)S(1)}, bf16[1,1,48,128,128]{4,3,2,1,0:T(8,128)(2,1)}, u32[]{:S(2)}) %copy-start) | copy-done | bytes 1572888
  31.7 0.6 shard_map.137.edges
  32.3 0.1 pad_add_fusion.place
  32.4 0.3 collective-permute-done.2.refs_2_
  32.7 2.9 %collective-permute-done.6.refs_7_ = bf16[512,256]{1,0:T(8,128)(2,1)S(1)} collective-permute-done((bf16[512,256]{1,0:T(8,128)(2,1)S(1)}, bf16[512,256]{1,0:T(8,128)(2,1)S(1)}, u32[]{:S(2)}, u32[]{:S(2)}) %collective-permute-start.6) | collective-permute-done | bytes 262176 | tf_op jit(solution)/shard_map/ppermute | solution.py:20
  35.6 0.0 copy-start.5
  35.6 0.0 copy-start.7
  35.6 0.0 copy-start.9
  35.6 1.5 %shard_map.138 = (bf16[512,256]{1,0:T(8,128)(2,1)S(1)}, bf16[512,256]{1,0:T(8,128)(2,1)S(1)}, bf16[512,256]{1,0:T(8,128)(2,1)S(1)}, bf16[512,256]{1,0:T(8,128)(2,1)S(1)}, bf16[4096,256]{1,0:T(8,128)(2,1)S(1)}) custom-call(s32[48]{0:T(128)S(1)} %bitcast.16, s32[2]{0:T(128)S(1)} %pad_add_fusion.place, bf16[48,128,128]{2,1,0:T(8,128)(2,1)S(1)} %shard_map.137.edges, ...), custom_call_target="tpu_custom_call" | custom-call | flops 402653184 | bytes 6815944 | tf_op jit(solution)/shard_map/pallas_call | solution.py:108
  37.1 0.1 collective-permute-start.8
  37.2 0.5 collective-permute-start.7
  37.7 1.0 %collective-permute-done.8 = bf16[512,256]{1,0:T(8,128)(2,1)S(1)} collective-permute-done((bf16[512,256]{1,0:T(8,128)(2,1)S(1)}, bf16[512,256]{1,0:T(8,128)(2,1)S(1)}, u32[]{:S(2)}, u32[]{:S(2)}) %collective-permute-start.8) | collective-permute-done | bytes 262176 | tf_op jit(solution)/shard_map/ppermute | solution.py:20
  38.7 0.1 add_convert_fusion.2
  38.8 1.6 %collective-permute-start.9 = (bf16[512,256]{1,0:T(8,128)(2,1)S(1)}, bf16[512,256]{1,0:T(8,128)(2,1)S(1)}, u32[]{:S(2)}, u32[]{:S(2)}) collective-permute-start(bf16[512,256]{1,0:T(8,128)(2,1)S(1)} %add_convert_fusion.2), channel_id=1, source_target_pairs={{0,2},{1,3},{2,0},{3,1},{4,6},{5,7},{6,4},{7,5},{8,10},{9,11},{10,... | collective-permute-start | bytes 786440 | tf_op jit(solution)/shard_map/ppermute | solution.py:20
  40.4 0.3 shard_map.139
  40.7 6.5 %collective-permute-done.9.refs_2_ = bf16[512,256]{1,0:T(8,128)(2,1)S(1)} collective-permute-done((bf16[512,256]{1,0:T(8,128)(2,1)S(1)}, bf16[512,256]{1,0:T(8,128)(2,1)S(1)}, u32[]{:S(2)}, u32[]{:S(2)}) %collective-permute-start.9) | collective-permute-done | bytes 262176 | tf_op jit(solution)/shard_map/ppermute | solution.py:20
  47.2 0.6 shard_map.140
  47.8 1.0 shard_map.145
  48.8 0.1 collective-permute-start.20
  48.9 1.6 %collective-permute-start.11 = (bf16[512,256]{1,0:T(8,128)(2,1)S(1)}, bf16[512,256]{1,0:T(8,128)(2,1)S(1)}, u32[]{:S(2)}, u32[]{:S(2)}) collective-permute-start(bf16[512,256]{1,0:T(8,128)(2,1)S(1)} %get-tuple-element.58.refs_0_), channel_id=1, source_target_pairs={{0,2},{1,3},{2,0},{3,1},{4,6},{5,7},{6,4},{7,5},{8,10},{9,11},{10,... | collective-permute-start | bytes 786440 | tf_op jit(solution)/shard_map/ppermute | solution.py:20
  50.4 0.0 collective-permute-done.20
  50.5 0.6 collective-permute-start.21
  51.1 6.5 %collective-permute-done.11.refs_2_ = bf16[512,256]{1,0:T(8,128)(2,1)S(1)} collective-permute-done((bf16[512,256]{1,0:T(8,128)(2,1)S(1)}, bf16[512,256]{1,0:T(8,128)(2,1)S(1)}, u32[]{:S(2)}, u32[]{:S(2)}) %collective-permute-start.11) | collective-permute-done | bytes 262176 | tf_op jit(solution)/shard_map/ppermute | solution.py:20
  57.6 1.5 %collective-permute-done.12.refs_3_ = bf16[512,256]{1,0:T(8,128)(2,1)S(1)} collective-permute-done((bf16[512,256]{1,0:T(8,128)(2,1)S(1)}, bf16[512,256]{1,0:T(8,128)(2,1)S(1)}, u32[]{:S(2)}, u32[]{:S(2)}) %collective-permute-start.12) | collective-permute-done | bytes 262176 | tf_op jit(solution)/shard_map/ppermute | solution.py:20
  59.1 2.3 %shard_map.141 = (bf16[512,256]{1,0:T(8,128)(2,1)S(1)}, bf16[512,256]{1,0:T(8,128)(2,1)S(1)}, bf16[512,256]{1,0:T(8,128)(2,1)S(1)}, bf16[512,256]{1,0:T(8,128)(2...) custom-call(s32[48]{0:T(128)S(1)} %bitcast.17, ...), custom_call_target="tpu_custom_call" | custom-call | flops 402653184 | bytes 4718792 | tf_op jit(solution)/shard_map/pallas_call | solution.py:108
  61.5 0.5 collective-permute-start.13
  62.0 0.7 collective-permute-start.14
  62.6 2.4 %collective-permute-start.15 = (bf16[512,256]{1,0:T(8,128)(2,1)S(1)}, bf16[512,256]{1,0:T(8,128)(2,1)S(1)}, u32[]{:S(2)}, u32[]{:S(2)}) collective-permute-start(bf16[512,256]{1,0:T(8,128)(2,1)S(1)} %get-tuple-element.65), channel_id=1, source_target_pairs={{0,12},{4,8},{8,4},{12,0},{16,28},{20,24},{24,20},{28,16},{1,13},{... | collective-permute-start | bytes 786440 | tf_op jit(solution)/shard_map/ppermute | solution.py:20
  65.0 2.5 %collective-permute-start.22 = (bf16[272,256]{1,0:T(8,128)(2,1)S(1)}, bf16[272,256]{1,0:T(8,128)(2,1)S(1)}, u32[]{:S(2)}, u32[]{:S(2)}) collective-permute-start(bf16[272,256]{1,0:T(8,128)(2,1)S(1)} %convert_add_fusion), channel_id=1, source_target_pairs={{0,16},{1,17},{2,18},{3,19},{4,20},{5,21},{6,22},{7,23},{8,24},{9,... | collective-permute-start | bytes 417800 | tf_op jit(solution)/shard_map/ppermute | solution.py:39
  67.5 0.5 collective-permute-start.17
  68.0 8.8 %collective-permute-done.22 = bf16[272,256]{1,0:T(8,128)(2,1)S(1)} collective-permute-done((bf16[272,256]{1,0:T(8,128)(2,1)S(1)}, bf16[272,256]{1,0:T(8,128)(2,1)S(1)}, u32[]{:S(2)}, u32[]{:S(2)}) %collective-permute-start.22) | collective-permute-done | bytes 139296 | tf_op jit(solution)/shard_map/ppermute | solution.py:39
  76.9 2.5 %collective-permute-start.25 = (bf16[272,256]{1,0:T(8,128)(2,1)S(1)}, bf16[272,256]{1,0:T(8,128)(2,1)S(1)}, u32[]{:S(2)}, u32[]{:S(2)}) collective-permute-start(bf16[272,256]{1,0:T(8,128)(2,1)S(1)} %add_convert_fusion.3), channel_id=1, source_target_pairs={{0,6},{1,7},{2,4},{3,5},{4,2},{5,3},{6,0},{7,1},{8,14},{9,15},{10,... | collective-permute-start | bytes 417800 | tf_op jit(solution)/shard_map/ppermute | solution.py:39
  79.4 0.5 collective-permute-start.24
  79.9 0.5 collective-permute-start.23
  80.5 0.1 add_convert_fusion.1
  80.6 3.4 %collective-permute-start.19 = (bf16[512,256]{1,0:T(8,128)(2,1)S(1)}, bf16[512,256]{1,0:T(8,128)(2,1)S(1)}, u32[]{:S(2)}, u32[]{:S(2)}) collective-permute-start(bf16[512,256]{1,0:T(8,128)(2,1)S(1)} %add_convert_fusion.1), channel_id=1, source_target_pairs={{0,16},{4,20},{8,24},{12,28},{16,0},{20,4},{24,8},{28,12},{1,17},{... | collective-permute-start | bytes 786440 | tf_op jit(solution)/shard_map/ppermute | solution.py:20
  84.1 1.3 %collective-permute-done.17 = bf16[512,256]{1,0:T(8,128)(2,1)S(1)} collective-permute-done((bf16[512,256]{1,0:T(8,128)(2,1)S(1)}, bf16[512,256]{1,0:T(8,128)(2,1)S(1)}, u32[]{:S(2)}, u32[]{:S(2)}) %collective-permute-start.17) | collective-permute-done | bytes 262176 | tf_op jit(solution)/shard_map/ppermute | solution.py:20
  85.4 0.1 add_convert_fusion
  85.5 0.1 collective-permute-start.18
  85.5 2.7 %shard_map.144 = bf16[48,128,128]{2,1,0:T(8,128)(2,1)} custom-call(s32[48]{0:T(128)S(1)} %bitcast.18, s32[1]{0:T(128)} %bitcast.10.count, s32[2]{0:T(128)S(1)} %pad_add_fusion.place, bf16[512,256]{1,0:T(8,128)(2,1)S(1)} %get-tuple-element.58.refs_0_, bf16[512,256]{1,0:T(8,128)(2,1)S(1)} %collective-permute-done.10.refs_1_, ...), custom_call_target="tpu_custom_call" | custom-call | flops 402653184 | bytes 4718796 | tf_op jit(solution)/shard_map/pallas_call | solution.py:108
  88.2 1.2 %collective-permute-start.16 = (bf16[512,256]{1,0:T(8,128)(2,1)S(1)}, bf16[512,256]{1,0:T(8,128)(2,1)S(1)}, u32[]{:S(2)}, u32[]{:S(2)}) collective-permute-start(bf16[512,256]{1,0:T(8,128)(2,1)S(1)} %get-tuple-element.67), channel_id=1, source_target_pairs={{0,4},{4,0},{8,12},{12,8},{16,20},{20,16},{24,28},{28,24},{1,5},{5... | collective-permute-start | bytes 786440 | tf_op jit(solution)/shard_map/ppermute | solution.py:20
  89.5 0.1 add_add_fusion.same
  89.5 4.4 %collective-permute-done.19.last = bf16[512,256]{1,0:T(8,128)(2,1)S(1)} collective-permute-done((bf16[512,256]{1,0:T(8,128)(2,1)S(1)}, bf16[512,256]{1,0:T(8,128)(2,1)S(1)}, u32[]{:S(2)}, u32[]{:S(2)}) %collective-permute-start.19) | collective-permute-done | bytes 262176 | tf_op jit(solution)/shard_map/ppermute | solution.py:20
  93.9 0.4 collective-permute-done.18
  94.3 1.7 %shard_map.142 = (bf16[512,256]{1,0:T(8,128)(2,1)}, f32[512,256]{1,0:T(8,128)S(1)}) custom-call(s32[4,128]{1,0:T(4,128)S(1)} %bitcast.14, bf16[512,256]{1,0:T(8,128)(2,1)S(1)} %get-tuple-element.50.refs_0_, bf16[512,256]{1,0:T(8,128)(2,1)S(1)} %collective-permute-done.7.refs_1_, bf16[512,256]{1,0:T(8,128)(2,1)S(1)} %collective-permute-done.9.refs_2_, ...), custom_call_target="tpu_custom_call" | custom-call | flops 268435456 | bytes 2623488 | tf_op jit(solution)/shard_map/pallas_call | solution.py:108
  96.0 0.1 select_add_fusion.early
  96.1 0.9 shard_map.143
  97.1 1.4 %shard_map.146 = (f32[256,256]{1,0:T(8,128)}, f32[256,256]{1,0:T(8,128)}, f32[1,256]{1,0:T(1,128)}) custom-call(s32[2]{0:T(128)S(1)} %pad_add_fusion.place, f32[272,256]{1,0:T(8,128)S(1)} %add_add_fusion.same, f32[272,256]{1,0:T(8,128)S(1)} %collective-permute-done.26.other), custom_call_target="tpu_custom_call" | custom-call | bytes 1082376 | tf_op jit(solution)/shard_map/pallas_call | solution.py:108
  (31 shorter events, 0.2 us)
Async XLA Ops:
  0.6 1.0 copy-start.1
  1.6 0.7 copy-start.6
  2.5 14.0 %collective-permute-start.1 = (bf16[512,256]{1,0:T(8,128)(2,1)S(1)}, bf16[512,256]{1,0:T(8,128)(2,1)S(1)}, u32[]{:S(2)}, u32[]{:S(2)}) collective-permute-start(bf16[512,256]{1,0:T(8,128)(2,1)S(1)} %shard_map.136.refs_0_), channel_id=1, source_target_pairs={{0,4},{4,0},{8,12},{12,8},{16,20},{20,16},{24,28},{28,24},{1,5},{5... | collective-permute-start | bytes 786440 | tf_op jit(solution)/shard_map/ppermute | solution.py:20
  5.6 14.4 %collective-permute-start = (bf16[512,256]{1,0:T(8,128)(2,1)S(1)}, bf16[512,256]{1,0:T(8,128)(2,1)S(1)}, u32[]{:S(2)}, u32[]{:S(2)}) collective-permute-start(bf16[512,256]{1,0:T(8,128)(2,1)S(1)} %shard_map.136.refs_0_), channel_id=1, source_target_pairs={{0,16},{4,20},{8,24},{12,28},{16,0},{20,4},{24,8},{28,12},{1,17},{... | collective-permute-start | bytes 786440 | tf_op jit(solution)/shard_map/ppermute | solution.py:20
  8.2 14.3 %collective-permute-start.4 = (bf16[512,256]{1,0:T(8,128)(2,1)S(1)}, bf16[512,256]{1,0:T(8,128)(2,1)S(1)}, u32[]{:S(2)}, u32[]{:S(2)}) collective-permute-start(bf16[512,256]{1,0:T(8,128)(2,1)S(1)} %shard_map.136.refs_0_), channel_id=1, source_target_pairs={{0,12},{4,8},{8,4},{12,0},{16,28},{20,24},{24,20},{28,16},{1,13},{... | collective-permute-start | bytes 786440 | tf_op jit(solution)/shard_map/ppermute | solution.py:20
  19.9 9.2 %collective-permute-start.3 = (bf16[512,256]{1,0:T(8,128)(2,1)S(1)}, bf16[512,256]{1,0:T(8,128)(2,1)S(1)}, u32[]{:S(2)}, u32[]{:S(2)}) collective-permute-start(bf16[512,256]{1,0:T(8,128)(2,1)S(1)} %collective-permute-done.refs_4_), channel_id=1, source_target_pairs={{0,8},{4,12},{8,0},{12,4},{16,24},{20,28},{24,16},{28,20},{1,9},{5... | collective-permute-start | bytes 786440 | tf_op jit(solution)/shard_map/ppermute | solution.py:20
  20.5 12.1 %collective-permute-start.2 = (bf16[512,256]{1,0:T(8,128)(2,1)S(1)}, bf16[512,256]{1,0:T(8,128)(2,1)S(1)}, u32[]{:S(2)}, u32[]{:S(2)}) collective-permute-start(bf16[512,256]{1,0:T(8,128)(2,1)S(1)} %shard_map.136.refs_0_), channel_id=1, source_target_pairs={{0,8},{4,12},{8,0},{12,4},{16,24},{20,28},{24,16},{28,20},{1,9},{5... | collective-permute-start | bytes 786440 | tf_op jit(solution)/shard_map/ppermute | solution.py:20
  22.0 10.7 %collective-permute-start.5 = (bf16[512,256]{1,0:T(8,128)(2,1)S(1)}, bf16[512,256]{1,0:T(8,128)(2,1)S(1)}, u32[]{:S(2)}, u32[]{:S(2)}) collective-permute-start(bf16[512,256]{1,0:T(8,128)(2,1)S(1)} %collective-permute-done.refs_4_), channel_id=1, source_target_pairs={{0,4},{4,0},{8,12},{12,8},{16,20},{20,16},{24,28},{28,24},{1,5},{5... | collective-permute-start | bytes 786440 | tf_op jit(solution)/shard_map/ppermute | solution.py:20
  29.2 6.4 %collective-permute-start.6 = (bf16[512,256]{1,0:T(8,128)(2,1)S(1)}, bf16[512,256]{1,0:T(8,128)(2,1)S(1)}, u32[]{:S(2)}, u32[]{:S(2)}) collective-permute-start(bf16[512,256]{1,0:T(8,128)(2,1)S(1)} %collective-permute-done.3.refs_6_), channel_id=1, source_target_pairs={{0,4},{4,0},{8,12},{12,8},{16,20},{20,16},{24,28},{28,24},{1,5},{5... | collective-permute-start | bytes 786440 | tf_op jit(solution)/shard_map/ppermute | solution.py:20
  30.3 1.4 %copy-start = (bf16[1,1,48,128,128]{4,3,2,1,0:T(8,128)(2,1)S(1)}, bf16[1,1,48,128,128]{4,3,2,1,0:T(8,128)(2,1)}, u32[]{:S(2)}) copy-start(bf16[1,1,48,128,128]{4,3,2,1,0:T(8,128)(2,1)} %param.16) | copy-start | bytes 4718596
  31.7 3.9 %copy-start.8 = (s32[1,1,48]{2,1,0:T(1,128)S(1)}, s32[1,1,48]{2,1,0:T(1,128)}, u32[]{:S(2)}) copy-start(s32[1,1,48]{2,1,0:T(1,128)} %param.14) | copy-start | bytes 580
  35.6 4.8 %copy-start.2 = (bf16[512,256]{1,0:T(8,128)(2,1)S(1)}, bf16[512,256]{1,0:T(8,128)(2,1)}, u32[]{:S(2)}) copy-start(bf16[512,256]{1,0:T(8,128)(2,1)} %feats.3) | copy-start | bytes 786436
  35.6 4.8 %copy-start.3 = (bf16[256,256]{1,0:T(8,128)(2,1)S(1)}, bf16[256,256]{1,0:T(8,128)(2,1)}, u32[]{:S(2)}) copy-start(bf16[256,256]{1,0:T(8,128)(2,1)} %refs_6_.1) | copy-start | bytes 393220
  35.6 4.8 %copy-start.4 = (bf16[512,256]{1,0:T(8,128)(2,1)S(1)}, bf16[512,256]{1,0:T(8,128)(2,1)}, u32[]{:S(2)}) copy-start(bf16[512,256]{1,0:T(8,128)(2,1)} %grad_out.1) | copy-start | bytes 786436
  35.6 4.8 %copy-start.5 = (bf16[256,256]{1,0:T(8,128)(2,1)S(1)}, bf16[256,256]{1,0:T(8,128)(2,1)}, u32[]{:S(2)}) copy-start(bf16[256,256]{1,0:T(8,128)(2,1)} %w_msg.1) | copy-start | bytes 393220
  35.6 4.8 %copy-start.7 = (s32[512]{0:T(512)S(1)}, s32[512]{0:T(512)}, u32[]{:S(2)}) copy-start(s32[512]{0:T(512)} %param.13) | copy-start | bytes 6148
  35.6 4.8 %copy-start.9 = (f32[256]{0:T(256)S(1)}, f32[256]{0:T(256)}, u32[]{:S(2)}) copy-start(f32[256]{0:T(256)} %param.12) | copy-start | bytes 3076
  37.1 1.6 %collective-permute-start.8 = (bf16[512,256]{1,0:T(8,128)(2,1)S(1)}, bf16[512,256]{1,0:T(8,128)(2,1)S(1)}, u32[]{:S(2)}, u32[]{:S(2)}) collective-permute-start(bf16[512,256]{1,0:T(8,128)(2,1)S(1)} %get-tuple-element.53), channel_id=1, source_target_pairs={{0,1},{1,0},{2,3},{3,2},{4,5},{5,4},{6,7},{7,6},{8,9},{9,8},{10,11... | collective-permute-start | bytes 786440 | tf_op jit(solution)/shard_map/ppermute | solution.py:20
  37.2 3.5 %collective-permute-start.7 = (bf16[512,256]{1,0:T(8,128)(2,1)S(1)}, bf16[512,256]{1,0:T(8,128)(2,1)S(1)}, u32[]{:S(2)}, u32[]{:S(2)}) collective-permute-start(bf16[512,256]{1,0:T(8,128)(2,1)S(1)} %get-tuple-element.51), channel_id=1, source_target_pairs={{0,1},{1,0},{2,3},{3,2},{4,5},{5,4},{6,7},{7,6},{8,9},{9,8},{10,11... | collective-permute-start | bytes 786440 | tf_op jit(solution)/shard_map/ppermute | solution.py:20
  38.8 8.4 %collective-permute-start.9 = (bf16[512,256]{1,0:T(8,128)(2,1)S(1)}, bf16[512,256]{1,0:T(8,128)(2,1)S(1)}, u32[]{:S(2)}, u32[]{:S(2)}) collective-permute-start(bf16[512,256]{1,0:T(8,128)(2,1)S(1)} %add_convert_fusion.2), channel_id=1, source_target_pairs={{0,2},{1,3},{2,0},{3,1},{4,6},{5,7},{6,4},{7,5},{8,10},{9,11},{10,... | collective-permute-start | bytes 786440 | tf_op jit(solution)/shard_map/ppermute | solution.py:20
  48.8 1.7 %collective-permute-start.20 = (f32[272,256]{1,0:T(8,128)S(1)}, f32[272,256]{1,0:T(8,128)S(1)}, u32[]{:S(2)}, u32[]{:S(2)}) collective-permute-start(f32[272,256]{1,0:T(8,128)S(1)} %get-tuple-element.78), channel_id=1, source_target_pairs={{0,1},{1,0},{2,3},{3,2},{4,5},{5,4},{6,7},{7,6},{8,9},{9,8},{10,11... | collective-permute-start | bytes 835592 | tf_op jit(solution)/shard_map/ppermute | solution.py:20
  48.9 8.7 %collective-permute-start.11 = (bf16[512,256]{1,0:T(8,128)(2,1)S(1)}, bf16[512,256]{1,0:T(8,128)(2,1)S(1)}, u32[]{:S(2)}, u32[]{:S(2)}) collective-permute-start(bf16[512,256]{1,0:T(8,128)(2,1)S(1)} %get-tuple-element.58.refs_0_), channel_id=1, source_target_pairs={{0,2},{1,3},{2,0},{3,1},{4,6},{5,7},{6,4},{7,5},{8,10},{9,11},{10,... | collective-permute-start | bytes 786440 | tf_op jit(solution)/shard_map/ppermute | solution.py:20
  50.5 7.1 %collective-permute-start.21 = (bf16[272,256]{1,0:T(8,128)(2,1)S(1)}, bf16[272,256]{1,0:T(8,128)(2,1)S(1)}, u32[]{:S(2)}, u32[]{:S(2)}) collective-permute-start(bf16[272,256]{1,0:T(8,128)(2,1)S(1)} %add_convert_fusion.4), channel_id=1, source_target_pairs={{0,8},{1,9},{2,10},{3,11},{4,12},{5,13},{6,14},{7,15},{8,0},{9,1},... | collective-permute-start | bytes 417800 | tf_op jit(solution)/shard_map/ppermute | solution.py:39
  51.1 6.5 %collective-permute-start.10 = (bf16[512,256]{1,0:T(8,128)(2,1)S(1)}, bf16[512,256]{1,0:T(8,128)(2,1)S(1)}, u32[]{:S(2)}, u32[]{:S(2)}) collective-permute-start(bf16[512,256]{1,0:T(8,128)(2,1)S(1)} %get-tuple-element.58.refs_0_), channel_id=1, source_target_pairs={{0,1},{1,0},{2,3},{3,2},{4,5},{5,4},{6,7},{7,6},{8,9},{9,8},{10,11... | collective-permute-start | bytes 786440 | tf_op jit(solution)/shard_map/ppermute | solution.py:20
  57.6 1.5 %collective-permute-start.12 = (bf16[512,256]{1,0:T(8,128)(2,1)S(1)}, bf16[512,256]{1,0:T(8,128)(2,1)S(1)}, u32[]{:S(2)}, u32[]{:S(2)}) collective-permute-start(bf16[512,256]{1,0:T(8,128)(2,1)S(1)} %collective-permute-done.11.refs_2_), channel_id=1, source_target_pairs={{0,1},{1,0},{2,3},{3,2},{4,5},{5,4},{6,7},{7,6},{8,9},{9,8},{10,11... | collective-permute-start | bytes 786440 | tf_op jit(solution)/shard_map/ppermute | solution.py:20
  61.5 17.9 %collective-permute-start.13 = (bf16[512,256]{1,0:T(8,128)(2,1)S(1)}, bf16[512,256]{1,0:T(8,128)(2,1)S(1)}, u32[]{:S(2)}, u32[]{:S(2)}) collective-permute-start(bf16[512,256]{1,0:T(8,128)(2,1)S(1)} %get-tuple-element.63), channel_id=1, source_target_pairs={{0,4},{4,0},{8,12},{12,8},{16,20},{20,16},{24,28},{28,24},{1,5},{5... | collective-permute-start | bytes 786440 | tf_op jit(solution)/shard_map/ppermute | solution.py:20
  62.0 17.9 %collective-permute-start.14 = (bf16[512,256]{1,0:T(8,128)(2,1)S(1)}, bf16[512,256]{1,0:T(8,128)(2,1)S(1)}, u32[]{:S(2)}, u32[]{:S(2)}) collective-permute-start(bf16[512,256]{1,0:T(8,128)(2,1)S(1)} %get-tuple-element.64), channel_id=1, source_target_pairs={{0,8},{4,12},{8,0},{12,4},{16,24},{20,28},{24,16},{28,20},{1,9},{5... | collective-permute-start | bytes 786440 | tf_op jit(solution)/shard_map/ppermute | solution.py:20
  62.6 17.8 %collective-permute-start.15 = (bf16[512,256]{1,0:T(8,128)(2,1)S(1)}, bf16[512,256]{1,0:T(8,128)(2,1)S(1)}, u32[]{:S(2)}, u32[]{:S(2)}) collective-permute-start(bf16[512,256]{1,0:T(8,128)(2,1)S(1)} %get-tuple-element.65), channel_id=1, source_target_pairs={{0,12},{4,8},{8,4},{12,0},{16,28},{20,24},{24,20},{28,16},{1,13},{... | collective-permute-start | bytes 786440 | tf_op jit(solution)/shard_map/ppermute | solution.py:20
  65.0 11.9 %collective-permute-start.22 = (bf16[272,256]{1,0:T(8,128)(2,1)S(1)}, bf16[272,256]{1,0:T(8,128)(2,1)S(1)}, u32[]{:S(2)}, u32[]{:S(2)}) collective-permute-start(bf16[272,256]{1,0:T(8,128)(2,1)S(1)} %convert_add_fusion), channel_id=1, source_target_pairs={{0,16},{1,17},{2,18},{3,19},{4,20},{5,21},{6,22},{7,23},{8,24},{9,... | collective-permute-start | bytes 417800 | tf_op jit(solution)/shard_map/ppermute | solution.py:39
  67.5 17.8 %collective-permute-start.17 = (bf16[512,256]{1,0:T(8,128)(2,1)S(1)}, bf16[512,256]{1,0:T(8,128)(2,1)S(1)}, u32[]{:S(2)}, u32[]{:S(2)}) collective-permute-start(bf16[512,256]{1,0:T(8,128)(2,1)S(1)} %get-tuple-element.69), channel_id=1, source_target_pairs={{0,4},{4,0},{8,12},{12,8},{16,20},{20,16},{24,28},{28,24},{1,5},{5... | collective-permute-start | bytes 786440 | tf_op jit(solution)/shard_map/ppermute | solution.py:20
  76.9 11.3 %collective-permute-start.25 = (bf16[272,256]{1,0:T(8,128)(2,1)S(1)}, bf16[272,256]{1,0:T(8,128)(2,1)S(1)}, u32[]{:S(2)}, u32[]{:S(2)}) collective-permute-start(bf16[272,256]{1,0:T(8,128)(2,1)S(1)} %add_convert_fusion.3), channel_id=1, source_target_pairs={{0,6},{1,7},{2,4},{3,5},{4,2},{5,3},{6,0},{7,1},{8,14},{9,15},{10,... | collective-permute-start | bytes 417800 | tf_op jit(solution)/shard_map/ppermute | solution.py:39
  79.4 10.1 %collective-permute-start.24 = (bf16[272,256]{1,0:T(8,128)(2,1)S(1)}, bf16[272,256]{1,0:T(8,128)(2,1)S(1)}, u32[]{:S(2)}, u32[]{:S(2)}) collective-permute-start(bf16[272,256]{1,0:T(8,128)(2,1)S(1)} %add_convert_fusion.3), channel_id=1, source_target_pairs={{0,2},{1,3},{2,0},{3,1},{4,6},{5,7},{6,4},{7,5},{8,10},{9,11},{10,... | collective-permute-start | bytes 417800 | tf_op jit(solution)/shard_map/ppermute | solution.py:39
  79.9 9.5 %collective-permute-start.23 = (bf16[272,256]{1,0:T(8,128)(2,1)S(1)}, bf16[272,256]{1,0:T(8,128)(2,1)S(1)}, u32[]{:S(2)}, u32[]{:S(2)}) collective-permute-start(bf16[272,256]{1,0:T(8,128)(2,1)S(1)} %add_convert_fusion.3), channel_id=1, source_target_pairs={{0,4},{1,5},{2,6},{3,7},{4,0},{5,1},{6,2},{7,3},{8,12},{9,13},{10,... | collective-permute-start | bytes 417800 | tf_op jit(solution)/shard_map/ppermute | solution.py:39
  80.6 13.3 %collective-permute-start.19 = (bf16[512,256]{1,0:T(8,128)(2,1)S(1)}, bf16[512,256]{1,0:T(8,128)(2,1)S(1)}, u32[]{:S(2)}, u32[]{:S(2)}) collective-permute-start(bf16[512,256]{1,0:T(8,128)(2,1)S(1)} %add_convert_fusion.1), channel_id=1, source_target_pairs={{0,16},{4,20},{8,24},{12,28},{16,0},{20,4},{24,8},{28,12},{1,17},{... | collective-permute-start | bytes 786440 | tf_op jit(solution)/shard_map/ppermute | solution.py:20
  85.5 8.9 %collective-permute-start.18 = (bf16[512,256]{1,0:T(8,128)(2,1)S(1)}, bf16[512,256]{1,0:T(8,128)(2,1)S(1)}, u32[]{:S(2)}, u32[]{:S(2)}) collective-permute-start(bf16[512,256]{1,0:T(8,128)(2,1)S(1)} %add_convert_fusion), channel_id=1, source_target_pairs={{0,8},{4,12},{8,0},{12,4},{16,24},{20,28},{24,16},{28,20},{1,9},{5... | collective-permute-start | bytes 786440 | tf_op jit(solution)/shard_map/ppermute | solution.py:20
  88.2 7.8 %collective-permute-start.16 = (bf16[512,256]{1,0:T(8,128)(2,1)S(1)}, bf16[512,256]{1,0:T(8,128)(2,1)S(1)}, u32[]{:S(2)}, u32[]{:S(2)}) collective-permute-start(bf16[512,256]{1,0:T(8,128)(2,1)S(1)} %get-tuple-element.67), channel_id=1, source_target_pairs={{0,4},{4,0},{8,12},{12,8},{16,20},{20,16},{24,28},{28,24},{1,5},{5... | collective-permute-start | bytes 786440 | tf_op jit(solution)/shard_map/ppermute | solution.py:20
  94.3 2.8 %collective-permute-start.26 = (f32[272,256]{1,0:T(8,128)S(1)}, f32[272,256]{1,0:T(8,128)S(1)}, u32[]{:S(2)}, u32[]{:S(2)}) collective-permute-start(f32[272,256]{1,0:T(8,128)S(1)} %add_add_fusion.same), channel_id=1, source_target_pairs={{0,1},{1,0},{2,3},{3,2},{4,5},{5,4},{6,7},{7,6},{8,9},{9,8},{10,11... | collective-permute-start | bytes 835592 | tf_op jit(solution)/shard_map/ppermute | solution.py:20

commit v4 on v3

--- a/solution.py
+++ b/solution.py
@@ -86,15 +86,17 @@
 
 def scatter_rows(parts, axis):
     if lax.axis_size(axis) != 8:
-        return scatter_by_offset(parts, axis)
+        terms = scatter_by_offset(parts, axis)
+        return terms + terms[:1]
     got7, got6, got5 = (exchange(parts[4 + bit], axis, bit) for bit in (3, 2, 1))
-    got3 = exchange(parts[3], axis, 1)
+    got7, part3 = tie(got7, parts[3])
+    got3 = exchange(part3, axis, 1)
     far = add_rounded(parts[4], got5, got6, got7)
     got4 = exchange(far, axis, 4)
     _, part1 = tie(far, parts[1])
     got1 = exchange(part1, axis, 1)
     got2 = exchange(add_rounded(parts[2], got3), axis, 2)
-    return [parts[0], got1, got2, got4]
+    return [parts[0], got1, got2, got4, far]
 
 
 def nbytes(shape, dtype):
@@ -284,6 +286,13 @@
         picked = jnp.dot(select_rows(mask, k, size), value, preferred_element_type=F32)
         hidden[rows, :] = picked.astype(BF16)
         own_part[rows, :] = nt(grad, w_self[...])
+
+
+def side_body(dims, n_edge, size, n_terms, n_rest, cols, count, place, *refs):
+    edge_refs, rest_refs = refs[:n_edge], refs[n_edge : n_edge + n_rest]
+    edge_grad, hidden, own_part = refs[n_edge + n_rest :]
+    rest_body(size, n_terms, *rest_refs, hidden, own_part)
+    edge_body(*dims, cols, count, place, *edge_refs, edge_grad)
 
 
 def weight_body(factor, place, feats, grad_pre, summed, same, other, stack):
@@ -403,6 +412,17 @@
         (cols, place, live, *grads),
     )
 
+    rest = (mask, *terms, base, grad_live, w_here, w_self)
+    edge_grad, hidden, own_part = kernel_call(
+        functools.partial(side_body, dims, n_col + 1, size, len(terms), len(rest)),
+        [jax.ShapeDtypeStruct((slots, size, size), BF16), block, wide],
+        [SMEM] * 3 + [VMEM] * (n_col + 1 + len(rest)),
+        [VMEM] * 3,
+        [],
+        edge_flops + 8 * own_rows * width * width,
+        (cols, count, place, *grads, together, *rest),
+    )
+
     rows = 2 * width + 32
     half = jax.ShapeDtypeStruct((rows // 2, width), F32)
     factor = 1.0 / math.sqrt(own_rows * n_row * n_col)
@@ -415,17 +435,7 @@
         4 * own_rows * width * width,
         (place, feats_here, grad_pre, summed),
     )
-    late_live, _ = tie(grad_live, pieces[0])
-    hidden, own_part = kernel_call(
-        functools.partial(rest_body, size, len(terms)),
-        [block, wide],
-        [VMEM] * (len(terms) + 5),
-        [VMEM] * 2,
-        [],
-        8 * own_rows * width * width,
-        (mask, *terms, base, late_live, w_here, w_self),
-    )
-    back = scatter_rows(pieces, "row")
+    *back, far = scatter_rows(pieces, "row")
     total = same + exchange(other, "col", 1)
     row_bits, col_bits = bits_of(n_row), bits_of(n_col)[1:]
     total = add_over(total, (row_bits.pop(min(1, len(row_bits) - 1)), 0))
@@ -434,8 +444,9 @@
         total = add_over(total, (bit, 0))
     for bit in col_bits[:-1]:
         total = add_over(total, (0, bit))
+    total, *_ = tie(total, far, own_part)
     total = add_over(total, (row_bits[0], 0), (0, col_bits[-1]))
-    total, *_ = tie(total, *back[2:])
+    total, *_ = tie(total, own_part, *back[2:])
     square = jax.ShapeDtypeStruct((width, width), F32)
     msg_grad, self_grad, bias_grad = kernel_call(
         join_body,
@@ -445,16 +456,6 @@
         [pltpu.VMEM((rows, width), F32)],
         0,
         (place, total, exchange(total, "col", 1)),
-    )
-
-    edge_grad = kernel_call(
-        functools.partial(edge_body, *dims),
-        jax.ShapeDtypeStruct((slots, size, size), BF16),
-        [SMEM] * 3 + [VMEM] * (n_col + 1),
-        VMEM,
-        [],
-        edge_flops,
-        (cols, count, place, *grads, together),
     )
 
     column = (hit_mask != 0)[:, None]

time: 99.2 us -> 99.5 us (level)
  starting transfers between devices: 29.3 us -> 34.5 us
  waiting for transfers between devices: 50.7 us -> 47.3 us
  Pallas kernels: 13.2 us -> 12.2 us
    ppermute x5, waiting for transfers between devices: 8.85 us -> 1.34 us  [add_over(): got.append(lax.ppermute(sent, ('row', 'col'), pairs).astype(F32))]
    ppermute x22, starting transfers between devices: 22.6 us -> 27.7 us  [exchange(): return lax.ppermute(value, axis, [(i, i ^ bit) for i in range(size)])]
    ppermute x22, waiting for transfers between devices: 41.9 us -> 46 us  [exchange(): return lax.ppermute(value, axis, [(i, i ^ bit) for i in range(size)])]
    pallas_call x11 -> x10, Pallas kernels: 13.2 us -> 12.2 us  [kernel_call(): pl.pallas_call(body, out_shape=outs, in_specs=in_specs, out_specs=out_spe...]
  transfers between devices with their start and end apart: 27 -> 27, of which waited for: 13 -> 12; matrix products, arithmetic and copies ran while one was open for 1% -> 1% of each run, Pallas kernels for 6% -> 8%
where the time goes in v4:
time: 99.5 us; the launch traced here: 99.3 us
  waiting for transfers between devices  47.3 us (48%)
  starting transfers between devices  34.5 us (35%)
  Pallas kernels  12.2 us (12%)
  local copies, waits for them, and re-layouts  3.06 us (3%)
  between operations  1.49 us (1%)
    ppermute x22, waiting for transfers between devices, exchange(): return lax.ppermute(value, axis, [(i, i ^ bit) for i in range(size)])  46 us
    ppermute x22, starting transfers between devices, exchange(): return lax.ppermute(value, axis, [(i, i ^ bit) for i in range(size)])  27.7 us
    pallas_call x10, Pallas kernels, kernel_call(): pl.pallas_call(body, out_shape=outs, in_specs=in_specs, out_specs=out_spe...  12.2 us
    ppermute x5, starting transfers between devices, add_over(): got.append(lax.ppermute(sent, ('row', 'col'), pairs).astype(F32))  6.81 us
    unnamed x20, local copies, waits for them, and re-layouts  3.06 us
  transfers between devices with their start and end apart: 27, of which 12 were waited for; matrix products, arithmetic and copies ran while one was open for 1% of the time, Pallas kernels for 8%

profile of v4, /device:TPU:0, one launch (start us, length us, event | category | flops | bytes accessed | tf_op | source)
XLA Modules:
  0.0 99.3 jit_solution(588096364094719714)
XLA Ops:
  0.6 0.0 copy-start.1
  0.6 0.9 copy-done.1
  1.6 0.7 copy-done.6
  2.3 0.3 shard_map.136.refs_0_
  2.5 4.1 %collective-permute-start = (bf16[512,256]{1,0:T(8,128)(2,1)S(1)}, bf16[512,256]{1,0:T(8,128)(2,1)S(1)}, u32[]{:S(2)}, u32[]{:S(2)}) collective-permute-start(bf16[512,256]{1,0:T(8,128)(2,1)S(1)} %shard_map.136.refs_0_), channel_id=1, source_target_pairs={{0,16},{4,20},{8,24},{12,28},{16,0},{20,4},{24,8},{28,12},{1,17},{... | collective-permute-start | bytes 786440 | tf_op jit(solution)/shard_map/ppermute | solution.py:20
  6.6 1.5 %collective-permute-start.1 = (bf16[512,256]{1,0:T(8,128)(2,1)S(1)}, bf16[512,256]{1,0:T(8,128)(2,1)S(1)}, u32[]{:S(2)}, u32[]{:S(2)}) collective-permute-start(bf16[512,256]{1,0:T(8,128)(2,1)S(1)} %shard_map.136.refs_0_), channel_id=1, source_target_pairs={{0,4},{4,0},{8,12},{12,8},{16,20},{20,16},{24,28},{28,24},{1,5},{5... | collective-permute-start | bytes 786440 | tf_op jit(solution)/shard_map/ppermute | solution.py:20
  8.2 1.5 %collective-permute-start.4 = (bf16[512,256]{1,0:T(8,128)(2,1)S(1)}, bf16[512,256]{1,0:T(8,128)(2,1)S(1)}, u32[]{:S(2)}, u32[]{:S(2)}) collective-permute-start(bf16[512,256]{1,0:T(8,128)(2,1)S(1)} %shard_map.136.refs_0_), channel_id=1, source_target_pairs={{0,12},{4,8},{8,4},{12,0},{16,28},{20,24},{24,20},{28,16},{1,13},{... | collective-permute-start | bytes 786440 | tf_op jit(solution)/shard_map/ppermute | solution.py:20
  9.7 9.0 %collective-permute-done.refs_4_ = bf16[512,256]{1,0:T(8,128)(2,1)S(1)} collective-permute-done((bf16[512,256]{1,0:T(8,128)(2,1)S(1)}, bf16[512,256]{1,0:T(8,128)(2,1)S(1)}, u32[]{:S(2)}, u32[]{:S(2)}) %collective-permute-start) | collective-permute-done | bytes 262176 | tf_op jit(solution)/shard_map/ppermute | solution.py:20
  18.7 0.0 collective-permute-done.1.refs_1_
  18.7 2.9 %collective-permute-start.3 = (bf16[512,256]{1,0:T(8,128)(2,1)S(1)}, bf16[512,256]{1,0:T(8,128)(2,1)S(1)}, u32[]{:S(2)}, u32[]{:S(2)}) collective-permute-start(bf16[512,256]{1,0:T(8,128)(2,1)S(1)} %collective-permute-done.refs_4_), channel_id=1, source_target_pairs={{0,8},{4,12},{8,0},{12,4},{16,24},{20,28},{24,16},{28,20},{1,9},{5... | collective-permute-start | bytes 786440 | tf_op jit(solution)/shard_map/ppermute | solution.py:20
  21.6 0.0 collective-permute-start.2
  21.6 1.5 %collective-permute-start.5 = (bf16[512,256]{1,0:T(8,128)(2,1)S(1)}, bf16[512,256]{1,0:T(8,128)(2,1)S(1)}, u32[]{:S(2)}, u32[]{:S(2)}) collective-permute-start(bf16[512,256]{1,0:T(8,128)(2,1)S(1)} %collective-permute-done.refs_4_), channel_id=1, source_target_pairs={{0,4},{4,0},{8,12},{12,8},{16,20},{20,16},{24,28},{28,24},{1,5},{5... | collective-permute-start | bytes 786440 | tf_op jit(solution)/shard_map/ppermute | solution.py:20
  23.1 0.0 collective-permute-done.4.refs_3_
  23.2 5.7 %collective-permute-done.3.refs_6_ = bf16[512,256]{1,0:T(8,128)(2,1)S(1)} collective-permute-done((bf16[512,256]{1,0:T(8,128)(2,1)S(1)}, bf16[512,256]{1,0:T(8,128)(2,1)S(1)}, u32[]{:S(2)}, u32[]{:S(2)}) %collective-permute-start.3) | collective-permute-done | bytes 262176 | tf_op jit(solution)/shard_map/ppermute | solution.py:20
  28.8 1.4 %collective-permute-start.6 = (bf16[512,256]{1,0:T(8,128)(2,1)S(1)}, bf16[512,256]{1,0:T(8,128)(2,1)S(1)}, u32[]{:S(2)}, u32[]{:S(2)}) collective-permute-start(bf16[512,256]{1,0:T(8,128)(2,1)S(1)} %collective-permute-done.3.refs_6_), channel_id=1, source_target_pairs={{0,4},{4,0},{8,12},{12,8},{16,20},{20,16},{24,28},{28,24},{1,5},{5... | collective-permute-start | bytes 786440 | tf_op jit(solution)/shard_map/ppermute | solution.py:20
  30.8 0.0 copy-start
  30.8 1.4 %copy-done = bf16[1,1,48,128,128]{4,3,2,1,0:T(8,128)(2,1)S(1)} copy-done((bf16[1,1,48,128,128]{4,3,2,1,0:T(8,128)(2,1)S(1)}, bf16[1,1,48,128,128]{4,3,2,1,0:T(8,128)(2,1)}, u32[]{:S(2)}) %copy-start) | copy-done | bytes 1572888
  32.2 0.6 shard_map.137.edges
  32.8 0.1 pad_add_fusion.place
  32.9 2.3 %collective-permute-done.6.refs_7_ = bf16[512,256]{1,0:T(8,128)(2,1)S(1)} collective-permute-done((bf16[512,256]{1,0:T(8,128)(2,1)S(1)}, bf16[512,256]{1,0:T(8,128)(2,1)S(1)}, u32[]{:S(2)}, u32[]{:S(2)}) %collective-permute-start.6) | collective-permute-done | bytes 262176 | tf_op jit(solution)/shard_map/ppermute | solution.py:20
  35.2 0.0 copy-start.5
  35.2 0.0 copy-start.7
  35.2 0.0 copy-start.9
  35.2 1.5 %shard_map.138 = (bf16[512,256]{1,0:T(8,128)(2,1)S(1)}, bf16[512,256]{1,0:T(8,128)(2,1)S(1)}, bf16[512,256]{1,0:T(8,128)(2,1)S(1)}, bf16[512,256]{1,0:T(8,128)(2,1)S(1)}, bf16[4096,256]{1,0:T(8,128)(2,1)S(1)}) custom-call(s32[48]{0:T(128)S(1)} %bitcast.16, s32[2]{0:T(128)S(1)} %pad_add_fusion.place, bf16[48,128,128]{2,1,0:T(8,128)(2,1)S(1)} %shard_map.137.edges, ...), custom_call_target="tpu_custom_call" | custom-call | flops 402653184 | bytes 6815944 | tf_op jit(solution)/shard_map/pallas_call | solution.py:110
  36.8 0.1 collective-permute-start.8
  36.8 0.5 collective-permute-start.7
  37.3 1.0 %collective-permute-done.8 = bf16[512,256]{1,0:T(8,128)(2,1)S(1)} collective-permute-done((bf16[512,256]{1,0:T(8,128)(2,1)S(1)}, bf16[512,256]{1,0:T(8,128)(2,1)S(1)}, u32[]{:S(2)}, u32[]{:S(2)}) %collective-permute-start.8) | collective-permute-done | bytes 262176 | tf_op jit(solution)/shard_map/ppermute | solution.py:20
  38.4 0.1 add_convert_fusion.2
  38.4 1.4 %collective-permute-start.9 = (bf16[512,256]{1,0:T(8,128)(2,1)S(1)}, bf16[512,256]{1,0:T(8,128)(2,1)S(1)}, u32[]{:S(2)}, u32[]{:S(2)}) collective-permute-start(bf16[512,256]{1,0:T(8,128)(2,1)S(1)} %add_convert_fusion.2), channel_id=1, source_target_pairs={{0,2},{1,3},{2,0},{3,1},{4,6},{5,7},{6,4},{7,5},{8,10},{9,11},{10,... | collective-permute-start | bytes 786440 | tf_op jit(solution)/shard_map/ppermute | solution.py:20
  39.9 0.3 shard_map.139
  40.2 0.0 collective-permute-done.7.refs_1_.refs_7_
  40.2 6.7 %collective-permute-done.9.refs_2_.refs_8_ = bf16[512,256]{1,0:T(8,128)(2,1)S(1)} collective-permute-done((bf16[512,256]{1,0:T(8,128)(2,1)S(1)}, bf16[512,256]{1,0:T(8,128)(2,1)S(1)}, u32[]{:S(2)}, u32[]{:S(2)}) %collective-permute-start.9) | collective-permute-done | bytes 262176 | tf_op jit(solution)/shard_map/ppermute | solution.py:20
  46.9 0.6 shard_map.140
  47.4 1.0 shard_map.144
  48.4 0.1 collective-permute-start.20
  48.5 1.4 %collective-permute-start.11 = (bf16[512,256]{1,0:T(8,128)(2,1)S(1)}, bf16[512,256]{1,0:T(8,128)(2,1)S(1)}, u32[]{:S(2)}, u32[]{:S(2)}) collective-permute-start(bf16[512,256]{1,0:T(8,128)(2,1)S(1)} %get-tuple-element.61.refs_0_), channel_id=1, source_target_pairs={{0,2},{1,3},{2,0},{3,1},{4,6},{5,7},{6,4},{7,5},{8,10},{9,11},{10,... | collective-permute-start | bytes 786440 | tf_op jit(solution)/shard_map/ppermute | solution.py:20
  49.9 0.2 collective-permute-start.10
  50.1 7.2 %collective-permute-done.11.refs_2_ = bf16[512,256]{1,0:T(8,128)(2,1)S(1)} collective-permute-done((bf16[512,256]{1,0:T(8,128)(2,1)S(1)}, bf16[512,256]{1,0:T(8,128)(2,1)S(1)}, u32[]{:S(2)}, u32[]{:S(2)}) %collective-permute-start.11) | collective-permute-done | bytes 262176 | tf_op jit(solution)/shard_map/ppermute | solution.py:20
  57.3 1.6 %collective-permute-start.21 = (bf16[272,256]{1,0:T(8,128)(2,1)S(1)}, bf16[272,256]{1,0:T(8,128)(2,1)S(1)}, u32[]{:S(2)}, u32[]{:S(2)}) collective-permute-start(bf16[272,256]{1,0:T(8,128)(2,1)S(1)} %add_convert_fusion.3), channel_id=1, source_target_pairs={{0,8},{1,9},{2,10},{3,11},{4,12},{5,13},{6,14},{7,15},{8,0},{9,1},... | collective-permute-start | bytes 417800 | tf_op jit(solution)/shard_map/ppermute | solution.py:39
  58.9 2.3 %shard_map.142 = (bf16[512,256]{1,0:T(8,128)(2,1)S(1)}, bf16[512,256]{1,0:T(8,128)(2,1)S(1)}, bf16[512,256]{1,0:T(8,128)(2,1)S(1)}, bf16[512,256]{1,0:T(8,128)(2...) custom-call(s32[48]{0:T(128)S(1)} %bitcast.17, ...), custom_call_target="tpu_custom_call" | custom-call | flops 402653184 | bytes 4718792 | tf_op jit(solution)/shard_map/pallas_call | solution.py:110
  61.2 2.4 %collective-permute-start.15 = (bf16[512,256]{1,0:T(8,128)(2,1)S(1)}, bf16[512,256]{1,0:T(8,128)(2,1)S(1)}, u32[]{:S(2)}, u32[]{:S(2)}) collective-permute-start(bf16[512,256]{1,0:T(8,128)(2,1)S(1)} %get-tuple-element.68), channel_id=1, source_target_pairs={{0,12},{4,8},{8,4},{12,0},{16,28},{20,24},{24,20},{28,16},{1,13},{... | collective-permute-start | bytes 786440 | tf_op jit(solution)/shard_map/ppermute | solution.py:20
  63.7 1.6 %collective-permute-start.22 = (bf16[272,256]{1,0:T(8,128)(2,1)S(1)}, bf16[272,256]{1,0:T(8,128)(2,1)S(1)}, u32[]{:S(2)}, u32[]{:S(2)}) collective-permute-start(bf16[272,256]{1,0:T(8,128)(2,1)S(1)} %convert_add_fusion.1), channel_id=1, source_target_pairs={{0,16},{1,17},{2,18},{3,19},{4,20},{5,21},{6,22},{7,23},{8,24},{9,... | collective-permute-start | bytes 417800 | tf_op jit(solution)/shard_map/ppermute | solution.py:39
  65.3 1.3 %collective-permute-start.13 = (bf16[512,256]{1,0:T(8,128)(2,1)S(1)}, bf16[512,256]{1,0:T(8,128)(2,1)S(1)}, u32[]{:S(2)}, u32[]{:S(2)}) collective-permute-start(bf16[512,256]{1,0:T(8,128)(2,1)S(1)} %get-tuple-element.66), channel_id=1, source_target_pairs={{0,4},{4,0},{8,12},{12,8},{16,20},{20,16},{24,28},{28,24},{1,5},{5... | collective-permute-start | bytes 786440 | tf_op jit(solution)/shard_map/ppermute | solution.py:20
  66.7 1.5 %collective-permute-start.14 = (bf16[512,256]{1,0:T(8,128)(2,1)S(1)}, bf16[512,256]{1,0:T(8,128)(2,1)S(1)}, u32[]{:S(2)}, u32[]{:S(2)}) collective-permute-start(bf16[512,256]{1,0:T(8,128)(2,1)S(1)} %get-tuple-element.67), channel_id=1, source_target_pairs={{0,8},{4,12},{8,0},{12,4},{16,24},{20,28},{24,16},{28,20},{1,9},{5... | collective-permute-start | bytes 786440 | tf_op jit(solution)/shard_map/ppermute | solution.py:20
  68.2 3.4 %shard_map.141 = (bf16[48,128,128]{2,1,0:T(8,128)(2,1)}, bf16[512,256]{1,0:T(8,128)(2,1)}, f32[512,256]{1,0:T(8,128)S(1)}) custom-call(s32[48]{0:T(128)S(1)} %bitcast.18, s32[1]{0:T(128)} %bitcast.10.count, s32[2]{0:T(128)S(1)} %pad_add_fusion.place, bf16[512,256]{1,0:T(8,128)(2,1)S(1)} %get-tuple-element.61.refs_0_, ...), custom_call_target="tpu_custom_call" | custom-call | flops 671088640 | bytes 7342284 | tf_op jit(solution)/shard_map/pallas_call | solution.py:110
  71.6 2.8 %collective-permute-done.15 = bf16[512,256]{1,0:T(8,128)(2,1)S(1)} collective-permute-done((bf16[512,256]{1,0:T(8,128)(2,1)S(1)}, bf16[512,256]{1,0:T(8,128)(2,1)S(1)}, u32[]{:S(2)}, u32[]{:S(2)}) %collective-permute-start.15) | collective-permute-done | bytes 262176 | tf_op jit(solution)/shard_map/ppermute | solution.py:20
  74.3 1.5 %collective-permute-start.17 = (bf16[512,256]{1,0:T(8,128)(2,1)S(1)}, bf16[512,256]{1,0:T(8,128)(2,1)S(1)}, u32[]{:S(2)}, u32[]{:S(2)}) collective-permute-start(bf16[512,256]{1,0:T(8,128)(2,1)S(1)} %get-tuple-element.74), channel_id=1, source_target_pairs={{0,4},{4,0},{8,12},{12,8},{16,20},{20,16},{24,28},{28,24},{1,5},{5... | collective-permute-start | bytes 786440 | tf_op jit(solution)/shard_map/ppermute | solution.py:20
  75.9 0.8 collective-permute-done.13
  76.8 2.6 %collective-permute-done.14 = bf16[512,256]{1,0:T(8,128)(2,1)S(1)} collective-permute-done((bf16[512,256]{1,0:T(8,128)(2,1)S(1)}, bf16[512,256]{1,0:T(8,128)(2,1)S(1)}, u32[]{:S(2)}, u32[]{:S(2)}) %collective-permute-start.14) | collective-permute-done | bytes 262176 | tf_op jit(solution)/shard_map/ppermute | solution.py:20
  79.3 0.1 add_convert_fusion.1
  79.4 0.6 collective-permute-start.23
  80.0 1.5 %collective-permute-start.24 = (bf16[272,256]{1,0:T(8,128)(2,1)S(1)}, bf16[272,256]{1,0:T(8,128)(2,1)S(1)}, u32[]{:S(2)}, u32[]{:S(2)}) collective-permute-start(bf16[272,256]{1,0:T(8,128)(2,1)S(1)} %convert_add_fusion), channel_id=1, source_target_pairs={{0,2},{1,3},{2,0},{3,1},{4,6},{5,7},{6,4},{7,5},{8,10},{9,11},{10,... | collective-permute-start | bytes 417800 | tf_op jit(solution)/shard_map/ppermute | solution.py:39
  81.5 1.5 %collective-permute-start.25 = (bf16[272,256]{1,0:T(8,128)(2,1)S(1)}, bf16[272,256]{1,0:T(8,128)(2,1)S(1)}, u32[]{:S(2)}, u32[]{:S(2)}) collective-permute-start(bf16[272,256]{1,0:T(8,128)(2,1)S(1)} %convert_add_fusion), channel_id=1, source_target_pairs={{0,6},{1,7},{2,4},{3,5},{4,2},{5,3},{6,0},{7,1},{8,14},{9,15},{10,... | collective-permute-start | bytes 417800 | tf_op jit(solution)/shard_map/ppermute | solution.py:39
  83.0 1.6 %collective-permute-start.19 = (bf16[512,256]{1,0:T(8,128)(2,1)S(1)}, bf16[512,256]{1,0:T(8,128)(2,1)S(1)}, u32[]{:S(2)}, u32[]{:S(2)}) collective-permute-start(bf16[512,256]{1,0:T(8,128)(2,1)S(1)} %add_convert_fusion.1), channel_id=1, source_target_pairs={{0,16},{4,20},{8,24},{12,28},{16,0},{20,4},{24,8},{28,12},{1,17},{... | collective-permute-start | bytes 786440 | tf_op jit(solution)/shard_map/ppermute | solution.py:20
  84.6 0.1 add_convert_fusion
  84.7 1.4 %collective-permute-start.18 = (bf16[512,256]{1,0:T(8,128)(2,1)S(1)}, bf16[512,256]{1,0:T(8,128)(2,1)S(1)}, u32[]{:S(2)}, u32[]{:S(2)}) collective-permute-start(bf16[512,256]{1,0:T(8,128)(2,1)S(1)} %add_convert_fusion), channel_id=1, source_target_pairs={{0,8},{4,12},{8,0},{12,4},{16,24},{20,28},{24,16},{28,20},{1,9},{5... | collective-permute-start | bytes 786440 | tf_op jit(solution)/shard_map/ppermute | solution.py:20
  86.0 1.3 %collective-permute-start.16 = (bf16[512,256]{1,0:T(8,128)(2,1)S(1)}, bf16[512,256]{1,0:T(8,128)(2,1)S(1)}, u32[]{:S(2)}, u32[]{:S(2)}) collective-permute-start(bf16[512,256]{1,0:T(8,128)(2,1)S(1)} %get-tuple-element.72), channel_id=1, source_target_pairs={{0,4},{4,0},{8,12},{12,8},{16,20},{20,16},{24,28},{28,24},{1,5},{5... | collective-permute-start | bytes 786440 | tf_op jit(solution)/shard_map/ppermute | solution.py:20
  87.4 1.3 %collective-permute-done.25 = bf16[272,256]{1,0:T(8,128)(2,1)S(1)} collective-permute-done((bf16[272,256]{1,0:T(8,128)(2,1)S(1)}, bf16[272,256]{1,0:T(8,128)(2,1)S(1)}, u32[]{:S(2)}, u32[]{:S(2)}) %collective-permute-start.25) | collective-permute-done | bytes 139296 | tf_op jit(solution)/shard_map/ppermute | solution.py:39
  88.7 0.1 add_add_fusion.same
  88.8 7.5 %collective-permute-done.19.last = bf16[512,256]{1,0:T(8,128)(2,1)S(1)} collective-permute-done((bf16[512,256]{1,0:T(8,128)(2,1)S(1)}, bf16[512,256]{1,0:T(8,128)(2,1)S(1)}, u32[]{:S(2)}, u32[]{:S(2)}) %collective-permute-start.19) | collective-permute-done | bytes 262176 | tf_op jit(solution)/shard_map/ppermute | solution.py:20
  96.3 0.1 select_add_fusion.early
  96.5 0.9 shard_map.143
  97.4 0.5 collective-permute-done.26.other
  97.9 1.4 %shard_map.145 = (f32[256,256]{1,0:T(8,128)}, f32[256,256]{1,0:T(8,128)}, f32[1,256]{1,0:T(1,128)}) custom-call(s32[2]{0:T(128)S(1)} %pad_add_fusion.place, f32[272,256]{1,0:T(8,128)S(1)} %add_add_fusion.same, f32[272,256]{1,0:T(8,128)S(1)} %collective-permute-done.26.other), custom_call_target="tpu_custom_call" | custom-call | bytes 1082376 | tf_op jit(solution)/shard_map/pallas_call | solution.py:110
  (30 shorter events, 0.2 us)
Async XLA Ops:
  0.6 1.0 copy-start.1
  1.6 0.7 copy-start.6
  2.5 16.1 %collective-permute-start = (bf16[512,256]{1,0:T(8,128)(2,1)S(1)}, bf16[512,256]{1,0:T(8,128)(2,1)S(1)}, u32[]{:S(2)}, u32[]{:S(2)}) collective-permute-start(bf16[512,256]{1,0:T(8,128)(2,1)S(1)} %shard_map.136.refs_0_), channel_id=1, source_target_pairs={{0,16},{4,20},{8,24},{12,28},{16,0},{20,4},{24,8},{28,12},{1,17},{... | collective-permute-start | bytes 786440 | tf_op jit(solution)/shard_map/ppermute | solution.py:20
  6.6 12.0 %collective-permute-start.1 = (bf16[512,256]{1,0:T(8,128)(2,1)S(1)}, bf16[512,256]{1,0:T(8,128)(2,1)S(1)}, u32[]{:S(2)}, u32[]{:S(2)}) collective-permute-start(bf16[512,256]{1,0:T(8,128)(2,1)S(1)} %shard_map.136.refs_0_), channel_id=1, source_target_pairs={{0,4},{4,0},{8,12},{12,8},{16,20},{20,16},{24,28},{28,24},{1,5},{5... | collective-permute-start | bytes 786440 | tf_op jit(solution)/shard_map/ppermute | solution.py:20
  8.2 15.0 %collective-permute-start.4 = (bf16[512,256]{1,0:T(8,128)(2,1)S(1)}, bf16[512,256]{1,0:T(8,128)(2,1)S(1)}, u32[]{:S(2)}, u32[]{:S(2)}) collective-permute-start(bf16[512,256]{1,0:T(8,128)(2,1)S(1)} %shard_map.136.refs_0_), channel_id=1, source_target_pairs={{0,12},{4,8},{8,4},{12,0},{16,28},{20,24},{24,20},{28,16},{1,13},{... | collective-permute-start | bytes 786440 | tf_op jit(solution)/shard_map/ppermute | solution.py:20
  18.7 10.2 %collective-permute-start.3 = (bf16[512,256]{1,0:T(8,128)(2,1)S(1)}, bf16[512,256]{1,0:T(8,128)(2,1)S(1)}, u32[]{:S(2)}, u32[]{:S(2)}) collective-permute-start(bf16[512,256]{1,0:T(8,128)(2,1)S(1)} %collective-permute-done.refs_4_), channel_id=1, source_target_pairs={{0,8},{4,12},{8,0},{12,4},{16,24},{20,28},{24,16},{28,20},{1,9},{5... | collective-permute-start | bytes 786440 | tf_op jit(solution)/shard_map/ppermute | solution.py:20
  21.6 11.3 %collective-permute-start.2 = (bf16[512,256]{1,0:T(8,128)(2,1)S(1)}, bf16[512,256]{1,0:T(8,128)(2,1)S(1)}, u32[]{:S(2)}, u32[]{:S(2)}) collective-permute-start(bf16[512,256]{1,0:T(8,128)(2,1)S(1)} %shard_map.136.refs_0_), channel_id=1, source_target_pairs={{0,8},{4,12},{8,0},{12,4},{16,24},{20,28},{24,16},{28,20},{1,9},{5... | collective-permute-start | bytes 786440 | tf_op jit(solution)/shard_map/ppermute | solution.py:20
  21.6 11.3 %collective-permute-start.5 = (bf16[512,256]{1,0:T(8,128)(2,1)S(1)}, bf16[512,256]{1,0:T(8,128)(2,1)S(1)}, u32[]{:S(2)}, u32[]{:S(2)}) collective-permute-start(bf16[512,256]{1,0:T(8,128)(2,1)S(1)} %collective-permute-done.refs_4_), channel_id=1, source_target_pairs={{0,4},{4,0},{8,12},{12,8},{16,20},{20,16},{24,28},{28,24},{1,5},{5... | collective-permute-start | bytes 786440 | tf_op jit(solution)/shard_map/ppermute | solution.py:20
  28.8 6.4 %collective-permute-start.6 = (bf16[512,256]{1,0:T(8,128)(2,1)S(1)}, bf16[512,256]{1,0:T(8,128)(2,1)S(1)}, u32[]{:S(2)}, u32[]{:S(2)}) collective-permute-start(bf16[512,256]{1,0:T(8,128)(2,1)S(1)} %collective-permute-done.3.refs_6_), channel_id=1, source_target_pairs={{0,4},{4,0},{8,12},{12,8},{16,20},{20,16},{24,28},{28,24},{1,5},{5... | collective-permute-start | bytes 786440 | tf_op jit(solution)/shard_map/ppermute | solution.py:20
  30.8 1.4 %copy-start = (bf16[1,1,48,128,128]{4,3,2,1,0:T(8,128)(2,1)S(1)}, bf16[1,1,48,128,128]{4,3,2,1,0:T(8,128)(2,1)}, u32[]{:S(2)}) copy-start(bf16[1,1,48,128,128]{4,3,2,1,0:T(8,128)(2,1)} %param.16) | copy-start | bytes 4718596
  32.2 2.9 %copy-start.8 = (s32[1,1,48]{2,1,0:T(1,128)S(1)}, s32[1,1,48]{2,1,0:T(1,128)}, u32[]{:S(2)}) copy-start(s32[1,1,48]{2,1,0:T(1,128)} %param.14) | copy-start | bytes 580
  35.2 4.7 %copy-start.2 = (bf16[512,256]{1,0:T(8,128)(2,1)S(1)}, bf16[512,256]{1,0:T(8,128)(2,1)}, u32[]{:S(2)}) copy-start(bf16[512,256]{1,0:T(8,128)(2,1)} %feats.3) | copy-start | bytes 786436
  35.2 4.7 %copy-start.3 = (bf16[256,256]{1,0:T(8,128)(2,1)S(1)}, bf16[256,256]{1,0:T(8,128)(2,1)}, u32[]{:S(2)}) copy-start(bf16[256,256]{1,0:T(8,128)(2,1)} %refs_12_.1) | copy-start | bytes 393220
  35.2 4.7 %copy-start.4 = (bf16[512,256]{1,0:T(8,128)(2,1)S(1)}, bf16[512,256]{1,0:T(8,128)(2,1)}, u32[]{:S(2)}) copy-start(bf16[512,256]{1,0:T(8,128)(2,1)} %grad_out.1) | copy-start | bytes 786436
  35.2 4.6 %copy-start.5 = (bf16[256,256]{1,0:T(8,128)(2,1)S(1)}, bf16[256,256]{1,0:T(8,128)(2,1)}, u32[]{:S(2)}) copy-start(bf16[256,256]{1,0:T(8,128)(2,1)} %w_msg.1) | copy-start | bytes 393220
  35.2 4.6 %copy-start.7 = (s32[512]{0:T(512)S(1)}, s32[512]{0:T(512)}, u32[]{:S(2)}) copy-start(s32[512]{0:T(512)} %param.13) | copy-start | bytes 6148
  35.2 4.6 %copy-start.9 = (f32[256]{0:T(256)S(1)}, f32[256]{0:T(256)}, u32[]{:S(2)}) copy-start(f32[256]{0:T(256)} %param.12) | copy-start | bytes 3076
  36.8 1.6 %collective-permute-start.8 = (bf16[512,256]{1,0:T(8,128)(2,1)S(1)}, bf16[512,256]{1,0:T(8,128)(2,1)S(1)}, u32[]{:S(2)}, u32[]{:S(2)}) collective-permute-start(bf16[512,256]{1,0:T(8,128)(2,1)S(1)} %get-tuple-element.56), channel_id=1, source_target_pairs={{0,1},{1,0},{2,3},{3,2},{4,5},{5,4},{6,7},{7,6},{8,9},{9,8},{10,11... | collective-permute-start | bytes 786440 | tf_op jit(solution)/shard_map/ppermute | solution.py:20
  36.8 3.3 %collective-permute-start.7 = (bf16[512,256]{1,0:T(8,128)(2,1)S(1)}, bf16[512,256]{1,0:T(8,128)(2,1)S(1)}, u32[]{:S(2)}, u32[]{:S(2)}) collective-permute-start(bf16[512,256]{1,0:T(8,128)(2,1)S(1)} %get-tuple-element.54), channel_id=1, source_target_pairs={{0,1},{1,0},{2,3},{3,2},{4,5},{5,4},{6,7},{7,6},{8,9},{9,8},{10,11... | collective-permute-start | bytes 786440 | tf_op jit(solution)/shard_map/ppermute | solution.py:20
  38.4 8.4 %collective-permute-start.9 = (bf16[512,256]{1,0:T(8,128)(2,1)S(1)}, bf16[512,256]{1,0:T(8,128)(2,1)S(1)}, u32[]{:S(2)}, u32[]{:S(2)}) collective-permute-start(bf16[512,256]{1,0:T(8,128)(2,1)S(1)} %add_convert_fusion.2), channel_id=1, source_target_pairs={{0,2},{1,3},{2,0},{3,1},{4,6},{5,7},{6,4},{7,5},{8,10},{9,11},{10,... | collective-permute-start | bytes 786440 | tf_op jit(solution)/shard_map/ppermute | solution.py:20
  48.4 8.8 %collective-permute-start.20 = (f32[272,256]{1,0:T(8,128)S(1)}, f32[272,256]{1,0:T(8,128)S(1)}, u32[]{:S(2)}, u32[]{:S(2)}) collective-permute-start(f32[272,256]{1,0:T(8,128)S(1)} %get-tuple-element.83), channel_id=1, source_target_pairs={{0,1},{1,0},{2,3},{3,2},{4,5},{5,4},{6,7},{7,6},{8,9},{9,8},{10,11... | collective-permute-start | bytes 835592 | tf_op jit(solution)/shard_map/ppermute | solution.py:20
  48.5 8.7 %collective-permute-start.11 = (bf16[512,256]{1,0:T(8,128)(2,1)S(1)}, bf16[512,256]{1,0:T(8,128)(2,1)S(1)}, u32[]{:S(2)}, u32[]{:S(2)}) collective-permute-start(bf16[512,256]{1,0:T(8,128)(2,1)S(1)} %get-tuple-element.61.refs_0_), channel_id=1, source_target_pairs={{0,2},{1,3},{2,0},{3,1},{4,6},{5,7},{6,4},{7,5},{8,10},{9,11},{10,... | collective-permute-start | bytes 786440 | tf_op jit(solution)/shard_map/ppermute | solution.py:20
  49.9 9.0 %collective-permute-start.10 = (bf16[512,256]{1,0:T(8,128)(2,1)S(1)}, bf16[512,256]{1,0:T(8,128)(2,1)S(1)}, u32[]{:S(2)}, u32[]{:S(2)}) collective-permute-start(bf16[512,256]{1,0:T(8,128)(2,1)S(1)} %get-tuple-element.61.refs_0_), channel_id=1, source_target_pairs={{0,1},{1,0},{2,3},{3,2},{4,5},{5,4},{6,7},{7,6},{8,9},{9,8},{10,11... | collective-permute-start | bytes 786440 | tf_op jit(solution)/shard_map/ppermute | solution.py:20
  57.2 1.7 %collective-permute-start.12 = (bf16[512,256]{1,0:T(8,128)(2,1)S(1)}, bf16[512,256]{1,0:T(8,128)(2,1)S(1)}, u32[]{:S(2)}, u32[]{:S(2)}) collective-permute-start(bf16[512,256]{1,0:T(8,128)(2,1)S(1)} %collective-permute-done.11.refs_2_), channel_id=1, source_target_pairs={{0,1},{1,0},{2,3},{3,2},{4,5},{5,4},{6,7},{7,6},{8,9},{9,8},{10,11... | collective-permute-start | bytes 786440 | tf_op jit(solution)/shard_map/ppermute | solution.py:20
  57.3 6.4 %collective-permute-start.21 = (bf16[272,256]{1,0:T(8,128)(2,1)S(1)}, bf16[272,256]{1,0:T(8,128)(2,1)S(1)}, u32[]{:S(2)}, u32[]{:S(2)}) collective-permute-start(bf16[272,256]{1,0:T(8,128)(2,1)S(1)} %add_convert_fusion.3), channel_id=1, source_target_pairs={{0,8},{1,9},{2,10},{3,11},{4,12},{5,13},{6,14},{7,15},{8,0},{9,1},... | collective-permute-start | bytes 417800 | tf_op jit(solution)/shard_map/ppermute | solution.py:39
  61.2 13.1 %collective-permute-start.15 = (bf16[512,256]{1,0:T(8,128)(2,1)S(1)}, bf16[512,256]{1,0:T(8,128)(2,1)S(1)}, u32[]{:S(2)}, u32[]{:S(2)}) collective-permute-start(bf16[512,256]{1,0:T(8,128)(2,1)S(1)} %get-tuple-element.68), channel_id=1, source_target_pairs={{0,12},{4,8},{8,4},{12,0},{16,28},{20,24},{24,20},{28,16},{1,13},{... | collective-permute-start | bytes 786440 | tf_op jit(solution)/shard_map/ppermute | solution.py:20
  63.7 12.2 %collective-permute-start.22 = (bf16[272,256]{1,0:T(8,128)(2,1)S(1)}, bf16[272,256]{1,0:T(8,128)(2,1)S(1)}, u32[]{:S(2)}, u32[]{:S(2)}) collective-permute-start(bf16[272,256]{1,0:T(8,128)(2,1)S(1)} %convert_add_fusion.1), channel_id=1, source_target_pairs={{0,16},{1,17},{2,18},{3,19},{4,20},{5,21},{6,22},{7,23},{8,24},{9,... | collective-permute-start | bytes 417800 | tf_op jit(solution)/shard_map/ppermute | solution.py:39
  65.3 11.4 %collective-permute-start.13 = (bf16[512,256]{1,0:T(8,128)(2,1)S(1)}, bf16[512,256]{1,0:T(8,128)(2,1)S(1)}, u32[]{:S(2)}, u32[]{:S(2)}) collective-permute-start(bf16[512,256]{1,0:T(8,128)(2,1)S(1)} %get-tuple-element.66), channel_id=1, source_target_pairs={{0,4},{4,0},{8,12},{12,8},{16,20},{20,16},{24,28},{28,24},{1,5},{5... | collective-permute-start | bytes 786440 | tf_op jit(solution)/shard_map/ppermute | solution.py:20
  66.7 12.6 %collective-permute-start.14 = (bf16[512,256]{1,0:T(8,128)(2,1)S(1)}, bf16[512,256]{1,0:T(8,128)(2,1)S(1)}, u32[]{:S(2)}, u32[]{:S(2)}) collective-permute-start(bf16[512,256]{1,0:T(8,128)(2,1)S(1)} %get-tuple-element.67), channel_id=1, source_target_pairs={{0,8},{4,12},{8,0},{12,4},{16,24},{20,28},{24,16},{28,20},{1,9},{5... | collective-permute-start | bytes 786440 | tf_op jit(solution)/shard_map/ppermute | solution.py:20
  74.3 10.2 %collective-permute-start.17 = (bf16[512,256]{1,0:T(8,128)(2,1)S(1)}, bf16[512,256]{1,0:T(8,128)(2,1)S(1)}, u32[]{:S(2)}, u32[]{:S(2)}) collective-permute-start(bf16[512,256]{1,0:T(8,128)(2,1)S(1)} %get-tuple-element.74), channel_id=1, source_target_pairs={{0,4},{4,0},{8,12},{12,8},{16,20},{20,16},{24,28},{28,24},{1,5},{5... | collective-permute-start | bytes 786440 | tf_op jit(solution)/shard_map/ppermute | solution.py:20
  79.4 6.6 %collective-permute-start.23 = (bf16[272,256]{1,0:T(8,128)(2,1)S(1)}, bf16[272,256]{1,0:T(8,128)(2,1)S(1)}, u32[]{:S(2)}, u32[]{:S(2)}) collective-permute-start(bf16[272,256]{1,0:T(8,128)(2,1)S(1)} %convert_add_fusion), channel_id=1, source_target_pairs={{0,4},{1,5},{2,6},{3,7},{4,0},{5,1},{6,2},{7,3},{8,12},{9,13},{10,... | collective-permute-start | bytes 417800 | tf_op jit(solution)/shard_map/ppermute | solution.py:39
  80.0 7.4 %collective-permute-start.24 = (bf16[272,256]{1,0:T(8,128)(2,1)S(1)}, bf16[272,256]{1,0:T(8,128)(2,1)S(1)}, u32[]{:S(2)}, u32[]{:S(2)}) collective-permute-start(bf16[272,256]{1,0:T(8,128)(2,1)S(1)} %convert_add_fusion), channel_id=1, source_target_pairs={{0,2},{1,3},{2,0},{3,1},{4,6},{5,7},{6,4},{7,5},{8,10},{9,11},{10,... | collective-permute-start | bytes 417800 | tf_op jit(solution)/shard_map/ppermute | solution.py:39
  81.5 7.2 %collective-permute-start.25 = (bf16[272,256]{1,0:T(8,128)(2,1)S(1)}, bf16[272,256]{1,0:T(8,128)(2,1)S(1)}, u32[]{:S(2)}, u32[]{:S(2)}) collective-permute-start(bf16[272,256]{1,0:T(8,128)(2,1)S(1)} %convert_add_fusion), channel_id=1, source_target_pairs={{0,6},{1,7},{2,4},{3,5},{4,2},{5,3},{6,0},{7,1},{8,14},{9,15},{10,... | collective-permute-start | bytes 417800 | tf_op jit(solution)/shard_map/ppermute | solution.py:39
  83.0 13.3 %collective-permute-start.19 = (bf16[512,256]{1,0:T(8,128)(2,1)S(1)}, bf16[512,256]{1,0:T(8,128)(2,1)S(1)}, u32[]{:S(2)}, u32[]{:S(2)}) collective-permute-start(bf16[512,256]{1,0:T(8,128)(2,1)S(1)} %add_convert_fusion.1), channel_id=1, source_target_pairs={{0,16},{4,20},{8,24},{12,28},{16,0},{20,4},{24,8},{28,12},{1,17},{... | collective-permute-start | bytes 786440 | tf_op jit(solution)/shard_map/ppermute | solution.py:20
  84.7 11.6 %collective-permute-start.18 = (bf16[512,256]{1,0:T(8,128)(2,1)S(1)}, bf16[512,256]{1,0:T(8,128)(2,1)S(1)}, u32[]{:S(2)}, u32[]{:S(2)}) collective-permute-start(bf16[512,256]{1,0:T(8,128)(2,1)S(1)} %add_convert_fusion), channel_id=1, source_target_pairs={{0,8},{4,12},{8,0},{12,4},{16,24},{20,28},{24,16},{28,20},{1,9},{5... | collective-permute-start | bytes 786440 | tf_op jit(solution)/shard_map/ppermute | solution.py:20
  86.0 10.3 %collective-permute-start.16 = (bf16[512,256]{1,0:T(8,128)(2,1)S(1)}, bf16[512,256]{1,0:T(8,128)(2,1)S(1)}, u32[]{:S(2)}, u32[]{:S(2)}) collective-permute-start(bf16[512,256]{1,0:T(8,128)(2,1)S(1)} %get-tuple-element.72), channel_id=1, source_target_pairs={{0,4},{4,0},{8,12},{12,8},{16,20},{20,16},{24,28},{28,24},{1,5},{5... | collective-permute-start | bytes 786440 | tf_op jit(solution)/shard_map/ppermute | solution.py:20
  96.3 1.6 %collective-permute-start.26 = (f32[272,256]{1,0:T(8,128)S(1)}, f32[272,256]{1,0:T(8,128)S(1)}, u32[]{:S(2)}, u32[]{:S(2)}) collective-permute-start(f32[272,256]{1,0:T(8,128)S(1)} %add_add_fusion.same), channel_id=1, source_target_pairs={{0,1},{1,0},{2,3},{3,2},{4,5},{5,4},{6,7},{7,6},{8,9},{9,8},{10,11... | collective-permute-start | bytes 835592 | tf_op jit(solution)/shard_map/ppermute | solution.py:20
